TPU v7x, 512 devices: a whole 4x8x8 slice. The times are simulated.
512 devices in a mesh: ctx: 64 (over y, z_lo, core), head: 8 (over x, z_hi).
Axes of the slice: x: 4, y: 8, z: 8 (z_hi: 2, z_lo: 4; z = z_hi * 4 + z_lo), core: 2. Of those that a mesh axis runs over, the one named last changes fastest.
Arguments:
- queries: bfloat16 [32768, 8192], P(('ctx', 'head')), may hold values from -72 to 72
- keys: bfloat16 [32768, 1024], P(('ctx', 'head')), may hold values from -4 to 4
- values: bfloat16 [32768, 1024], P(('ctx', 'head')), may hold values from -6 to 6
- assignment: int32 [64], replicated, may hold values from 0 to 63, each once
- anchor: int32 [1], replicated, may hold values from 0 to 63
- lengths: int32 [64], replicated, may hold values from 257 to 512
Outputs:
- attended: bfloat16 [32768, 8192], P(('ctx', 'head'))
Inputs may be any that keep to these rules, and one draw needn't show every extreme that they name: `assignment`: every block number appears once.
All inputs are finite; a program needn't handle non-finite values.
Results may differ from a plain program's by a relative error of at most 0.0027.
Values may be sent and summed in bfloat16 or wider, within the bound.
No kernel may reach another device: no remote copies, remote signals or barrier semaphores. Data moves between devices by JAX's collectives and lax.ppermute only.
A program may use at most 64 MiB of HBM per device.

v0:
```python
import math

import jax
import jax.numpy as jnp
from jax import lax
from jax.sharding import PartitionSpec as P

HEAD_DIM = 128


def broadcast(block, axis, source):
    block = jnp.where(lax.axis_index(axis) == source, block, jnp.zeros_like(block))
    return lax.psum(block, axis)


def attend_tile(
    query_tile, query_pos, own_keys, own_vals, anc_keys, anc_vals, my_len, anc_len, is_anchor
):
    factor = 1.0 / math.sqrt(query_tile.shape[-1])
    key_pos = jnp.arange(own_keys.shape[0], dtype=jnp.int32)

    def attend_part(key_set, val_set, keep):
        scores = jnp.dot(query_tile, key_set.T, preferred_element_type=jnp.float32) * factor
        scores = jnp.where(keep, scores, -jnp.inf)
        row_max = jnp.max(scores, axis=1, keepdims=True)
        weights = jnp.exp(scores - row_max)
        row_sum = jnp.sum(weights, axis=1, keepdims=True)
        result = (
            jnp.dot(weights.astype(jnp.bfloat16), val_set, preferred_element_type=jnp.float32)
            / row_sum
        )
        return (result, row_max + jnp.log(row_sum))

    own_mask = (key_pos[None, :] <= query_pos[:, None]) & (key_pos[None, :] < my_len)
    anc_mask = jnp.broadcast_to(key_pos[None, :] < anc_len, own_mask.shape)
    own_out, own_lse = attend_part(own_keys, own_vals, own_mask)
    anc_out, anc_lse = attend_part(anc_keys, anc_vals, anc_mask)
    anc_lse = jnp.where(is_anchor, -jnp.inf, anc_lse)
    biggest = jnp.maximum(own_lse, anc_lse)
    own_weight = jnp.exp(own_lse - biggest)
    anc_weight = jnp.where(is_anchor, jnp.zeros_like(own_weight), jnp.exp(anc_lse - biggest))
    merged = (own_weight * own_out + anc_weight * anc_out) / (own_weight + anc_weight)
    return merged.astype(jnp.bfloat16)


def shards(queries, keys, values, assignment, anchor, lengths):
    groups_n = lax.axis_size("head")
    row_count = queries.shape[0]
    block_len = row_count * groups_n
    kv_heads = keys.shape[1] // HEAD_DIM
    head_count = queries.shape[1] // HEAD_DIM
    per_group = head_count // kv_heads
    shard_ids = jnp.arange(assignment.shape[0], dtype=jnp.int32)
    my_index = lax.axis_index("ctx")
    block_id = jnp.sum(jnp.where(shard_ids == my_index, assignment, 0))
    anchor_shard = jnp.sum(jnp.where(assignment == anchor[0], shard_ids, 0))
    my_len = jnp.sum(jnp.where(shard_ids == block_id, lengths, 0))
    anc_len = jnp.sum(jnp.where(shard_ids == anchor[0], lengths, 0))
    is_anchor = block_id == anchor[0]
    q_local = queries.reshape(row_count, groups_n, -1)
    kv_local = jnp.concatenate(
        [keys.reshape(row_count, groups_n, -1), values.reshape(row_count, groups_n, -1)], axis=2
    )
    q_mine, kv_mine = (
        lax.all_to_all(q_local, "head", split_axis=1, concat_axis=0, tiled=True),
        lax.all_to_all(kv_local, "head", split_axis=1, concat_axis=0, tiled=True),
    )
    kv_anchor = broadcast(kv_mine, "ctx", anchor_shard)
    kv_local_heads = kv_heads // groups_n
    local_heads = kv_local_heads * per_group
    half_width = kv_local_heads * HEAD_DIM
    q_heads = q_mine.reshape(block_len, local_heads, HEAD_DIM)
    k_mine = kv_mine[:, 0, :half_width].reshape(block_len, kv_local_heads, HEAD_DIM)
    v_mine = kv_mine[:, 0, half_width:].reshape(block_len, kv_local_heads, HEAD_DIM)
    k_anchor = kv_anchor[:, 0, :half_width].reshape(block_len, kv_local_heads, HEAD_DIM)
    v_anchor = kv_anchor[:, 0, half_width:].reshape(block_len, kv_local_heads, HEAD_DIM)
    query_pos = jnp.arange(block_len, dtype=jnp.int32)

    def one_head(head_index):
        kv_index = head_index // per_group
        return attend_tile(
            q_heads[:, head_index],
            query_pos,
            k_mine[:, kv_index],
            v_mine[:, kv_index],
            k_anchor[:, kv_index],
            v_anchor[:, kv_index],
            my_len,
            anc_len,
            is_anchor,
        )

    per_head = lax.map(one_head, jnp.arange(local_heads, dtype=jnp.int32))
    returned = jnp.transpose(per_head, (1, 0, 2)).reshape(block_len, 1, local_heads * HEAD_DIM)
    arrived = lax.all_to_all(returned, "head", split_axis=0, concat_axis=1, tiled=True)
    return arrived.reshape(row_count, head_count * HEAD_DIM)


def solution(mesh):
    in_specs = (
        P(("ctx", "head"), None),
        P(("ctx", "head"), None),
        P(("ctx", "head"), None),
        P(),
        P(),
        P(),
    )
    out_specs = P(("ctx", "head"), None)
    return jax.shard_map(shards, mesh=mesh, in_specs=in_specs, out_specs=out_specs, check_vma=False)
```

profile of v0, /device:TPU:1, one launch (start us, length us, event | category | flops | bytes accessed | tf_op | source)
XLA Modules:
  0.0 635.6 jit_solution(4460527220219805976)
XLA Ops:
  6.5 1.0 copy.29
  7.6 0.9 copy.30
  8.5 0.7 copy.19
  9.3 13.3 %all-to-all-start.1 = ((bf16[64,8,256]{2,0,1:T(8,128)(2,1)}), bf16[64,8,256]{2,0,1:T(8,128)(2,1)S(1)}, u32[]{:S(2)}, u32[]{:S(2)}) async-start(bf16[64,8,256]{2,0,1:T(8,128)(2,1)} %copy.19), calls=%async_computation.1 | async-start | bytes 524288 | tf_op jit(solution)/shard_map/all_to_all | solution.py:66
  22.6 1.1 copy.34
  23.6 9.1 %all-to-all-done.1 = bf16[64,8,256]{2,0,1:T(8,128)(2,1)S(1)} async-done(((bf16[64,8,256]{2,0,1:T(8,128)(2,1)}), bf16[64,8,256]{2,0,1:T(8,128)(2,1)S(1)}, u32[]{:S(2)}, u32[]{:S(2)}) %all-to-all-start.1) | async-done | bytes 262176 | tf_op jit(solution)/shard_map/all_to_all | solution.py:66
  32.7 3.6 all-to-all-start
  37.0 0.7 fusion.35
  38.4 0.7 broadcast_select_fusion
  39.2 1.3 fusion.34
  41.0 499.2 %all-reduce.2.cloned.1.call-done = bf16[512,1,256]{2,0,1:T(8,128)(2,1)} async-done(((bf16[512,1,256]{2,0,1:T(8,128)(2,1)}), bf16[512,1,256]{2,0,1:T(8,128)(2,1)}) %all-reduce.2.cloned.1.call-update) | async-done | bytes 262160 | tf_op jit(solution)/shard_map/psum | solution.py:13
  540.3 1.0 fusion.41
  541.7 46.8 %while.11 = (s32[]{:T(128)}, bf16[8,512,128]{1,2,0:T(8,128)(2,1)S(1)}, s32[]{:T(128)}, s32[8]{0:T(128)S(1)}, bf16[512,8,128]{2,0,1:T(8,128)(2,1)S(1)}, /*index=5...) while((s32[]{:T(128)}, ...), condition=%wide.region_10.11_spmd.clone, body=%wide.region_5.10_spmd.clone.sunk | while | flops 273091584 | bytes 8300744 | solution.py:93
  541.7 0.6 dynamic_slice.30
  544.2 1.3 iota_compare_fusion.4
  545.5 0.3 fusion.60
  546.0 0.3 fusion.58
  546.6 0.4 fusion.63
  546.9 0.4 fusion.64
  547.6 0.6 dynamic_slice.30
  550.1 1.3 iota_compare_fusion.4
  551.4 0.3 fusion.60
  551.9 0.3 fusion.58
  552.4 0.4 fusion.63
  552.8 0.4 fusion.64
  553.4 0.6 dynamic_slice.30
  555.9 1.3 iota_compare_fusion.4
  557.2 0.3 fusion.60
  557.7 0.3 fusion.58
  558.3 0.4 fusion.63
  558.7 0.4 fusion.64
  559.3 0.6 dynamic_slice.30
  561.8 1.3 iota_compare_fusion.4
  563.6 0.3 fusion.58
  564.1 0.4 fusion.63
  564.5 0.4 fusion.64
  565.1 0.6 dynamic_slice.30
  567.6 1.3 iota_compare_fusion.4
  569.4 0.3 fusion.58
  570.0 0.4 fusion.63
  570.4 0.4 fusion.64
  571.0 0.6 dynamic_slice.30
  573.5 1.3 iota_compare_fusion.4
  575.3 0.3 fusion.58
  575.8 0.4 fusion.63
  576.2 0.4 fusion.64
  576.8 0.6 dynamic_slice.30
  579.3 1.3 iota_compare_fusion.4
  581.1 0.3 fusion.58
  581.7 0.4 fusion.63
  582.1 0.4 fusion.64
  582.7 0.6 dynamic_slice.30
  585.2 1.3 iota_compare_fusion.4
  587.0 0.3 fusion.58
  587.5 0.4 fusion.63
  587.9 0.4 fusion.64
  588.5 0.5 broadcast.82
  589.0 1.5 reduce
  590.5 0.5 copy.35
  591.0 0.8 reshape.101
  591.8 34.4 %all_to_all.48 = bf16[8,2,32768]{2,1,0:T(2,128)(2,1)S(1)} all-to-all(bf16[8,2,32768]{2,1,0:T(2,128)(2,1)S(1)} %reshape.101), channel_id=1, replica_groups=mesh['ctx'=64,'head'=8] {'head'}, dimensions={0} | all-to-all | bytes 2097152 | tf_op jit(solution)/shard_map/all_to_all | solution.py:95
  626.2 1.0 reshape.102
  627.3 0.4 copy.26
  627.7 1.1 copy.31
  (60 shorter events, 6.5 us)
Async XLA Ops:
  6.5 16.0 %copy-start = (bf16[64,8192]{1,0:T(8,128)(2,1)S(1)}, bf16[64,8192]{1,0:T(8,128)(2,1)}, u32[]{:S(2)}) copy-start(bf16[64,8192]{1,0:T(8,128)(2,1)} %param.8) | copy-start | bytes 3145732
  9.3 23.5 %all-to-all-start.1 = ((bf16[64,8,256]{2,0,1:T(8,128)(2,1)}), bf16[64,8,256]{2,0,1:T(8,128)(2,1)S(1)}, u32[]{:S(2)}, u32[]{:S(2)}) async-start(bf16[64,8,256]{2,0,1:T(8,128)(2,1)} %copy.19), calls=%async_computation.1 | async-start | bytes 524288 | tf_op jit(solution)/shard_map/all_to_all | solution.py:66
  22.6 14.4 %copy-start.1 = (s32[64]{0:T(128)S(1)}, s32[64]{0:T(128)}, u32[]{:S(2)}) copy-start(s32[64]{0:T(128)} %param.11) | copy-start | bytes 772
  22.6 16.6 %copy-start.2 = (s32[64]{0:T(128)S(1)}, s32[64]{0:T(128)}, u32[]{:S(2)}) copy-start(s32[64]{0:T(128)} %param.13) | copy-start | bytes 772
  32.7 508.5 %all-to-all-start = ((bf16[64,8,1024]{2,0,1:T(8,128)(2,1)}), bf16[64,8,1024]{2,0,1:T(8,128)(2,1)S(1)}, u32[]{:S(2)}, u32[]{:S(2)}) async-start(bf16[64,8,1024]{2,0,1:T(8,128)(2,1)} %bitcast.62), calls=%async_computation | async-start | bytes 2097152 | tf_op jit(solution)/shard_map/all_to_all | solution.py:65
  36.3 504.0 %all-reduce.2.cloned.1.call-start = ((), (), s32[]{:S(2)}) async-start(), calls=%async_computation.3 | async-start | bytes 524288 | tf_op jit(solution)/shard_map/psum | solution.py:13
Sparse Core Ops, SparseCore 0:
  40.0 500.1 all-reduce.1
where the time goes:
time: 636 us
  waiting for transfers between devices  508 us (80%)
  blocking collectives  34.4 us (5%)
  other arithmetic  17.6 us (3%)
  starting transfers between devices  16.9 us (3%)
  loops' own time  16 us (3%)
  between operations  15.5 us (2%)
  local copies, waits for them, and re-layouts  15.2 us (2%)
  matrix products  11.7 us (2%)
    psum x1, waiting for transfers between devices, broadcast(): return lax.psum(block, axis)  499 us
    all_to_all x1, blocking collectives, shards(): lax.all_to_all(returned, 'head', split_axis=0, concat_axis=1, tiled=True)  34.4 us
    another operation x1, loops' own time, shards(): per_head = lax.map(one_head, jnp.arange(local_heads, dtype=jnp.int32))  16 us
    all_to_all x1, starting transfers between devices, shards(): lax.all_to_all(kv_local, 'head', split_axis=1, concat_axis=0, tiled=True)  13.3 us
  transfers between devices with their start and end apart: 3, of which 2 were waited for; matrix products, arithmetic and copies ran while one was open for 1% of the time, Pallas kernels for 0%

commit v1 on v0

v1 whole, which is shorter than its diff:
```python
import math

import jax
import jax.numpy as jnp
from jax import lax
from jax.experimental import pallas as pl
from jax.experimental.pallas import tpu as pltpu
from jax.sharding import Mesh, PartitionSpec as P

HEAD_DIM = 128
GROUP = 8
AXES = ("y", "zl", "core", "x", "zh")
SIZES = (8, 4, 2, 4, 2)
CHUNK = 4
SCALE = math.log2(math.e) / math.sqrt(HEAD_DIM)
NEG = -math.inf


def head_columns(g, c):
    first = g * GROUP + c * CHUNK
    return [
        pl.ds(pl.multiple_of((first + i) * HEAD_DIM, HEAD_DIM), HEAD_DIM) for i in range(CHUNK)
    ]


def attend_set(q_ref, cols, k, v, bias):
    rows = q_ref.shape[0]
    q = jnp.concatenate([q_ref[:, at] for at in cols], axis=0)
    s = lax.dot_general(q, k, (((1,), (1,)), ((), ())), preferred_element_type=jnp.float32)
    s = (s.reshape(CHUNK, rows, -1) + bias[None]).reshape(CHUNK * rows, -1)
    m = jnp.max(s, axis=1, keepdims=True)
    e = jnp.exp2((s - m) * SCALE)
    l = jnp.sum(e, axis=1, keepdims=True)
    return m, l, jnp.dot(e.astype(jnp.bfloat16), v, preferred_element_type=jnp.float32)


def own_kernel(meta, q_ref, kv_ref, o_ref, stat_ref, bias_ref):
    rows = q_ref.shape[0]
    head_me, my_len = meta[0], meta[1]
    col = lax.broadcasted_iota(jnp.int32, bias_ref.shape, 1)
    row = lax.broadcasted_iota(jnp.int32, bias_ref.shape, 0) + head_me * rows
    bias_ref[...] = jnp.where((col <= row) & (col < my_len), 0.0, NEG)
    first = lax.broadcasted_iota(jnp.int32, (CHUNK * rows, HEAD_DIM), 1) == 0

    def one_group(g, carry):
        k = kv_ref[:, pl.ds(pl.multiple_of(g * HEAD_DIM, HEAD_DIM), HEAD_DIM)]
        v = kv_ref[:, pl.ds(pl.multiple_of((8 + g) * HEAD_DIM, HEAD_DIM), HEAD_DIM)]
        for c in range(GROUP // CHUNK):
            m, l, o = attend_set(q_ref, head_columns(g, c), k, v, bias_ref[...])
            at = pl.ds(c * CHUNK * rows, CHUNK * rows)
            o_ref[g, at] = o
            stat_ref[g, at] = jnp.where(first, m, l)
        return carry

    lax.fori_loop(0, 8, one_group, 0)


def anchor_kernel(meta, q_ref, mine_ref, other_ref, o_ref, stat_ref, out_ref, bias_ref):
    rows = q_ref.shape[0]
    anc_len, is_anchor, core = meta[2], meta[3], meta[4]
    col = lax.broadcasted_iota(jnp.int32, bias_ref.shape, 1)
    bias_ref[...] = jnp.where(col < anc_len, 0.0, NEG)

    def one_group(g, carry):
        mine = mine_ref[:, g].reshape(512, HEAD_DIM)
        other = other_ref[:, g].reshape(512, HEAD_DIM)
        k = jnp.where(core == 0, mine, other)
        v = jnp.where(core == 0, other, mine)
        for c in range(GROUP // CHUNK):
            cols = head_columns(g, c)
            m1, l1, o1 = attend_set(q_ref, cols, k, v, bias_ref[0:1, :])
            m1 = jnp.where(is_anchor > 0, NEG, m1)
            at = pl.ds(c * CHUNK * rows, CHUNK * rows)
            m0, l0 = stat_ref[g, at, 0:1], stat_ref[g, at, 1:2]
            big = jnp.maximum(m0, m1)
            w0 = jnp.exp2((m0 - big) * SCALE)
            w1 = jnp.exp2((m1 - big) * SCALE)
            inv = 1.0 / (w0 * l0 + w1 * l1)
            o = ((w0 * inv) * o_ref[g, at] + (w1 * inv) * o1).astype(out_ref.dtype)
            for i, to in enumerate(cols):
                out_ref[:, to] = o[i * rows : (i + 1) * rows]
        return carry

    lax.fori_loop(0, 8, one_group, 0)


VMEM = pl.BlockSpec(memory_space=pltpu.VMEM)
SMEM = pl.BlockSpec(memory_space=pltpu.SMEM)
COST = pl.CostEstimate(flops=2**30, bytes_accessed=6 * 2**20, transcendentals=2**21)
PARAMS = pltpu.CompilerParams(vmem_limit_bytes=40 * 1024 * 1024)


def attend_own(meta, queries, own, interpret=False):
    rows = queries.shape[0]
    part = jax.ShapeDtypeStruct((8, GROUP * rows, HEAD_DIM), jnp.float32)
    return pl.pallas_call(
        own_kernel,
        out_shape=(part, part),
        in_specs=[SMEM, VMEM, VMEM],
        out_specs=(VMEM, VMEM),
        scratch_shapes=[pltpu.VMEM((rows, 512), jnp.float32)],
        compiler_params=PARAMS,
        cost_estimate=COST,
        interpret=interpret,
    )(meta, queries, own)


def attend_anchor(meta, queries, mine, other, o, stat, interpret=False):
    return pl.pallas_call(
        anchor_kernel,
        out_shape=jax.ShapeDtypeStruct(queries.shape, jnp.bfloat16),
        in_specs=[SMEM] + [VMEM] * 5,
        out_specs=VMEM,
        scratch_shapes=[pltpu.VMEM((8, 512), jnp.float32)],
        compiler_params=PARAMS,
        cost_estimate=COST,
        interpret=interpret,
    )(meta, queries, mine, other, o, stat)


def attend(meta, queries, own, anc, interpret=False):
    o, stat = attend_own(meta, queries, own, interpret)
    return attend_anchor(meta, queries, *anc, o, stat, interpret)


def swap(a, axis):
    return lax.ppermute(a, axis, [(0, 1), (1, 0)])


def exchange(a, axes):
    return lax.all_to_all(a, axes, split_axis=0, concat_axis=0, tiled=True)


def to_all(a, axes, n):
    return exchange(jnp.broadcast_to(a[None], (n,) + a.shape), axes)


def communicate(keys, values, anchor_shard):
    rows = keys.shape[0]
    zh = lax.axis_index("zh")
    kv = jnp.concatenate([keys, values], axis=1)
    other = swap(kv, "zh")
    pair = jnp.where(zh == 0, jnp.stack([kv, other]), jnp.stack([other, kv]))
    own = to_all(pair, "x", 4).reshape(8 * rows, -1)
    cut = [a.reshape(rows, 8, HEAD_DIM).transpose(1, 0, 2) for a in (keys, values)]
    got = exchange(jnp.stack(cut, axis=1).reshape(16, rows, HEAD_DIM), ("y", "core"))
    source = (anchor_shard >> 3) * 2 + (anchor_shard & 1)
    part = lax.dynamic_index_in_dim(got, source, 0, keepdims=False)
    part = to_all(part, ("zl", "zh"), 8).reshape(4, 2, rows, HEAD_DIM)
    part = lax.dynamic_index_in_dim(part, (anchor_shard >> 1) & 3, 0, keepdims=False)
    part = to_all(part, "y", 8)
    mine = to_all(part, "x", 4)
    return own, (mine, swap(mine, "core"))


def shards(queries, keys, values, assignment, anchor, lengths):
    ids = jnp.arange(assignment.shape[0], dtype=jnp.int32)
    y, zl, core, x, zh = (lax.axis_index(a) for a in AXES)
    my_index = (y * 4 + zl) * 2 + core
    block_id = jnp.sum(jnp.where(ids == my_index, assignment, 0))
    anchor_shard = jnp.sum(jnp.where(assignment == anchor[0], ids, 0))
    my_len = jnp.sum(jnp.where(ids == block_id, lengths, 0))
    anc_len = jnp.sum(jnp.where(ids == anchor[0], lengths, 0))
    is_anchor = (block_id == anchor[0]).astype(jnp.int32)
    meta = jnp.stack([x * 2 + zh, my_len, anc_len, is_anchor, core]).astype(jnp.int32)
    own, anc = communicate(keys, values, anchor_shard)
    return attend(meta, queries, own, anc)


def solution(mesh):
    fine = Mesh(mesh.devices.reshape(SIZES), AXES)
    spec = P(AXES, None)
    return jax.shard_map(
        shards,
        mesh=fine,
        in_specs=(spec, spec, spec, P(), P(), P()),
        out_specs=spec,
        check_vma=False,
    )
```

time: 636 us -> 129 us (0.20)
  the two profiles are of different devices: /device:TPU:1 before, /device:TPU:64 now
where the time goes in v1:
time: 129 us; the launch traced here: 128 us
  waiting for transfers between devices  51.1 us (40%)
  starting transfers between devices  31.6 us (24%)
  Pallas kernels  16.4 us (13%)
  blocking collectives  14.8 us (11%)
  local copies, waits for them, and re-layouts  8.73 us (7%)
  between operations  3.52 us (3%)
  other arithmetic  2.14 us (2%)
    all_to_all x4, waiting for transfers between devices, exchange(): return lax.all_to_all(a, axes, split_axis=0, concat_axis=0, tiled=True)  37.4 us
    all_to_all x4, starting transfers between devices, exchange(): return lax.all_to_all(a, axes, split_axis=0, concat_axis=0, tiled=True)  26.1 us
    all_to_all x1, blocking collectives, exchange(): return lax.all_to_all(a, axes, split_axis=0, concat_axis=0, tiled=True)  14.8 us
    ppermute x2, waiting for transfers between devices, swap(): return lax.ppermute(a, axis, [(0, 1), (1, 0)])  13.8 us
    pallas_call x1, Pallas kernels, attend_anchor(): pl.pallas_call(anchor_kernel, out_shape=jax.ShapeDtypeStruct(queries.shap...  9.73 us
    pallas_call x1, Pallas kernels, attend_own(): pl.pallas_call(own_kernel, out_shape=(part, part), in_specs=[SMEM, VMEM,...  6.68 us
    ppermute x2, starting transfers between devices, swap(): return lax.ppermute(a, axis, [(0, 1), (1, 0)])  5.53 us
    broadcast_in_dim x6, local copies, waits for them, and re-layouts, to_all(): return exchange(jnp.broadcast_to(a[None], (n,) + a.shape), axes)  3.58 us
  transfers between devices with their start and end apart: 6, of which 4 were waited for; matrix products, arithmetic and copies ran while one was open for 3% of the time, Pallas kernels for 5%

profile of v1, /device:TPU:64, one launch (start us, length us, event | category | flops | bytes accessed | tf_op | source)
XLA Modules:
  0.0 128.4 jit_solution(17161313184458897280)
XLA Ops:
  0.0 0.0 copy-start.3
  0.0 0.9 copy.9
  0.9 0.9 copy.8
  1.9 0.8 copy.7
  2.7 7.2 %all-to-all-start = ((bf16[16,64,128]{2,1,0:T(8,128)(2,1)}), bf16[16,64,128]{2,1,0:T(8,128)(2,1)S(1)}, u32[]{:S(2)}, u32[]{:S(2)}) async-start(bf16[16,64,128]{2,1,0:T(8,128)(2,1)} %bitcast.10), calls=%async_computation | async-start | bytes 524288 | tf_op jit(solution)/shard_map/all_to_all | solution.py:131
  10.5 0.0 copy-done.3
  10.5 0.7 fusion.3
  12.7 8.4 %all-to-all-done = bf16[16,64,128]{2,1,0:T(8,128)(2,1)S(1)} async-done(((bf16[16,64,128]{2,1,0:T(8,128)(2,1)}), bf16[16,64,128]{2,1,0:T(8,128)(2,1)S(1)}, u32[]{:S(2)}, u32[]{:S(2)}) %all-to-all-start) | async-done | bytes 262176 | tf_op jit(solution)/shard_map/all_to_all | solution.py:131
  21.1 0.7 broadcast_in_dim.37
  21.7 10.0 %all-to-all-start.1 = ((bf16[8,64,128]{2,1,0:T(8,128)(2,1)}), bf16[8,64,128]{2,1,0:T(8,128)(2,1)S(1)}, u32[]{:S(2)}, u32[]{:S(2)}) async-start(bf16[8,64,128]{2,1,0:T(8,128)(2,1)} %broadcast_in_dim.37), calls=%async_computation.1 | async-start | bytes 262144 | tf_op jit(solution)/shard_map/all_to_all | solution.py:131
  32.4 7.8 %all-to-all-done.1 = bf16[8,64,128]{2,1,0:T(8,128)(2,1)S(1)} async-done(((bf16[8,64,128]{2,1,0:T(8,128)(2,1)}), bf16[8,64,128]{2,1,0:T(8,128)(2,1)S(1)}, u32[]{:S(2)}, u32[]{:S(2)}) %all-to-all-start.1) | async-done | bytes 131104 | tf_op jit(solution)/shard_map/all_to_all | solution.py:131
  40.2 0.0 copy-start.1
  40.3 0.0 copy-start.2
  40.3 14.8 %all_to_all.25 = bf16[8,2,64,128]{3,2,1,0:T(8,128)(2,1)S(1)} all-to-all(bf16[8,2,64,128]{3,2,1,0:T(8,128)(2,1)S(1)} %broadcast_in_dim.39), channel_id=1, replica_groups=mesh['y'=8,'zl'=4,'core'=2,'x'=4,'zh'=2] {'y'}, dimensions={0} | all-to-all | bytes 524288 | tf_op jit(solution)/shard_map/all_to_all | solution.py:131
  55.1 1.2 broadcast_in_dim.40
  56.3 4.3 %all-to-all-start.3 = ((bf16[4,8,2,64,128]{4,3,2,1,0:T(8,128)(2,1)}), bf16[4,8,2,64,128]{4,3,2,1,0:T(8,128)(2,1)S(1)}, u32[]{:S(2)}, u32[]{:S(2)}) async-start(bf16[4,8,2,64,128]{4,3,2,1,0:T(8,128)(2,1)} %broadcast_in_dim.40), calls=%async_computation.3 | async-start | bytes 2097152 | tf_op jit(solution)/shard_map/all_to_all | solution.py:131
  60.6 0.0 copy-done.1
  60.6 0.0 copy-done.2
  60.6 3.6 %collective-permute-start.1 = (bf16[64,2048]{1,0:T(8,128)(2,1)S(1)}, bf16[64,2048]{1,0:T(8,128)(2,1)S(1)}, u32[]{:S(2)}, u32[]{:S(2)}) collective-permute-start(bf16[64,2048]{1,0:T(8,128)(2,1)S(1)} %constant_dynamic-update-slice_fusion), channel_id=1, source_target_pairs={{0,1},{1,0},{2,3},{3,2},{4,5},{5,4},{6,7},{7,6},{8,9},{9,8},{10,11... | collective-permute-start | bytes 786440 | tf_op jit(solution)/shard_map/ppermute | solution.py:127
  64.3 13.8 %collective-permute-done.1 = bf16[64,2048]{1,0:T(8,128)(2,1)S(1)} collective-permute-done((bf16[64,2048]{1,0:T(8,128)(2,1)S(1)}, bf16[64,2048]{1,0:T(8,128)(2,1)S(1)}, u32[]{:S(2)}, u32[]{:S(2)}) %collective-permute-start.1) | collective-permute-done | bytes 262176 | tf_op jit(solution)/shard_map/ppermute | solution.py:127
  78.0 0.1 maximum_select_fusion
  78.1 0.0 all-to-all-done.3.mine_ref
  78.1 1.6 %broadcast_in_dim.41 = bf16[4,2,64,2048]{3,2,1,0:T(8,128)(2,1)} broadcast(bf16[2,64,2048]{2,1,0:T(8,128)(2,1)S(1)} %maximum_select_fusion), dimensions={1,2,3} | broadcast | bytes 2621440 | tf_op jit(solution)/shard_map/broadcast_in_dim | solution.py:135
  79.8 0.0 copy-start.4
  79.8 4.6 %all-to-all-start.4 = ((bf16[4,2,64,2048]{3,2,1,0:T(8,128)(2,1)}), bf16[4,2,64,2048]{3,2,1,0:T(8,128)(2,1)S(1)}, u32[]{:S(2)}, u32[]{:S(2)}) async-start(bf16[4,2,64,2048]{3,2,1,0:T(8,128)(2,1)} %broadcast_in_dim.41), calls=%async_computation.4 | async-start | bytes 4194304 | tf_op jit(solution)/shard_map/all_to_all | solution.py:131
  84.4 1.9 %collective-permute-start = (bf16[4,8,2,64,128]{4,3,2,1,0:T(8,128)(2,1)S(1)}, bf16[4,8,2,64,128]{4,3,2,1,0:T(8,128)(2,1)}, u32[]{:S(2)}, u32[]{:S(2)}) collective-permute-start(bf16[4,8,2,64,128]{4,3,2,1,0:T(8,128)(2,1)S(1)} %all-to-all-done.3.mine_ref), channel_id=1, source_target_pairs={{0,8},{8,0},{1,9},{9,1},{2,10},{10,2},{3,11},{11,3},{4,12},{12,4},... | collective-permute-start | bytes 3145736 | tf_op jit(solution)/shard_map/ppermute | solution.py:127
  87.0 0.0 copy-done.4
  87.0 1.3 %fusion.2 = (s32[]{:T(128)}, s32[]{:T(128)}) fusion(s32[64]{0:T(128)S(1)} %copy-done.4, s32[]{:T(128)} %bitcast.27, s32[]{:T(128)} %get-tuple-element.10), kind=kLoop, calls=%fused_computation.12 | loop fusion | flops 382 | bytes 272 | tf_op jit(solution)/shard_map/reduce_sum | solution.py:163
  88.3 1.3 stack.50.meta
  89.6 21.2 %all-to-all-done.4 = bf16[4,2,64,2048]{3,2,1,0:T(8,128)(2,1)S(1)} async-done(((bf16[4,2,64,2048]{3,2,1,0:T(8,128)(2,1)}), bf16[4,2,64,2048]{3,2,1,0:T(8,128)(2,1)S(1)}, u32[]{:S(2)}, u32[]{:S(2)}) %all-to-all-start.4) | async-done | bytes 2097184 | tf_op jit(solution)/shard_map/all_to_all | solution.py:131
  110.7 0.0 copy-start
  110.7 1.2 copy-done
  112.0 6.7 %shard_map.64 = (f32[8,512,128]{2,1,0:T(8,128)S(1)}, f32[8,512,128]{2,1,0:T(8,128)S(1)}) custom-call(s32[5]{0:T(128)S(1)} %stack.50.meta, bf16[64,8192]{1,0:T(8,128)(2,1)S(1)} %copy-done, bf16[512,2048]{1,0:T(8,128)(2,1)S(1)} %bitcast.30), custom_call_target="tpu_custom_call" | custom-call | flops 1073741824 | bytes 6291456 | tf_op jit(solution)/shard_map/pallas_call | solution.py:96
  118.6 0.0 collective-permute-done.other_ref
  118.7 9.7 %shard_map.65 = bf16[64,8192]{1,0:T(8,128)(2,1)} custom-call(s32[5]{0:T(128)S(1)} %stack.50.meta, bf16[64,8192]{1,0:T(8,128)(2,1)S(1)} %copy-done, bf16[4,8,2,64,128]{4,3,2,1,0:T(8,128)(2,1)S(1)} %all-to-all-done.3.mine_ref, bf16[4,8,2,64,128]{4,3,2,1,0:T(8,128)(2,1)} %collective-permute-done.other_ref, f32[8,512,128]{2,1,0:T(8,128)S(1)} %get-tuple-element.7.o_ref, ...), custom_call_target="tpu_custom_call" | custom-call | flops 1073741824 | bytes 6291456 | tf_op jit(solution)/shard_map/pallas_call | solution.py:109
  (6 shorter events, 0.1 us)
Async XLA Ops:
  0.0 10.5 %copy-start.3 = (s32[64]{0:T(128)S(1)}, s32[64]{0:T(128)}, u32[]{:S(2)}) copy-start(s32[64]{0:T(128)} %param.9) | copy-start | bytes 772
  2.7 18.4 %all-to-all-start = ((bf16[16,64,128]{2,1,0:T(8,128)(2,1)}), bf16[16,64,128]{2,1,0:T(8,128)(2,1)S(1)}, u32[]{:S(2)}, u32[]{:S(2)}) async-start(bf16[16,64,128]{2,1,0:T(8,128)(2,1)} %bitcast.10), calls=%async_computation | async-start | bytes 524288 | tf_op jit(solution)/shard_map/all_to_all | solution.py:131
  21.7 18.5 %all-to-all-start.1 = ((bf16[8,64,128]{2,1,0:T(8,128)(2,1)}), bf16[8,64,128]{2,1,0:T(8,128)(2,1)S(1)}, u32[]{:S(2)}, u32[]{:S(2)}) async-start(bf16[8,64,128]{2,1,0:T(8,128)(2,1)} %broadcast_in_dim.37), calls=%async_computation.1 | async-start | bytes 262144 | tf_op jit(solution)/shard_map/all_to_all | solution.py:131
  40.2 20.4 %copy-start.1 = (bf16[64,1024]{1,0:T(8,128)(2,1)S(1)}, bf16[64,1024]{1,0:T(8,128)(2,1)}, u32[]{:S(2)}) copy-start(bf16[64,1024]{1,0:T(8,128)(2,1)} %param.7) | copy-start | bytes 393220
  40.3 20.3 %copy-start.2 = (bf16[64,1024]{1,0:T(8,128)(2,1)S(1)}, bf16[64,1024]{1,0:T(8,128)(2,1)}, u32[]{:S(2)}) copy-start(bf16[64,1024]{1,0:T(8,128)(2,1)} %param.8) | copy-start | bytes 393220
  56.3 21.8 %all-to-all-start.3 = ((bf16[4,8,2,64,128]{4,3,2,1,0:T(8,128)(2,1)}), bf16[4,8,2,64,128]{4,3,2,1,0:T(8,128)(2,1)S(1)}, u32[]{:S(2)}, u32[]{:S(2)}) async-start(bf16[4,8,2,64,128]{4,3,2,1,0:T(8,128)(2,1)} %broadcast_in_dim.40), calls=%async_computation.3 | async-start | bytes 2097152 | tf_op jit(solution)/shard_map/all_to_all | solution.py:131
  60.6 17.4 %collective-permute-start.1 = (bf16[64,2048]{1,0:T(8,128)(2,1)S(1)}, bf16[64,2048]{1,0:T(8,128)(2,1)S(1)}, u32[]{:S(2)}, u32[]{:S(2)}) collective-permute-start(bf16[64,2048]{1,0:T(8,128)(2,1)S(1)} %constant_dynamic-update-slice_fusion), channel_id=1, source_target_pairs={{0,1},{1,0},{2,3},{3,2},{4,5},{5,4},{6,7},{7,6},{8,9},{9,8},{10,11... | collective-permute-start | bytes 786440 | tf_op jit(solution)/shard_map/ppermute | solution.py:127
  79.8 7.2 %copy-start.4 = (s32[64]{0:T(128)S(1)}, s32[64]{0:T(128)}, u32[]{:S(2)}) copy-start(s32[64]{0:T(128)} %param.11) | copy-start | bytes 772
  79.8 31.0 %all-to-all-start.4 = ((bf16[4,2,64,2048]{3,2,1,0:T(8,128)(2,1)}), bf16[4,2,64,2048]{3,2,1,0:T(8,128)(2,1)S(1)}, u32[]{:S(2)}, u32[]{:S(2)}) async-start(bf16[4,2,64,2048]{3,2,1,0:T(8,128)(2,1)} %broadcast_in_dim.41), calls=%async_computation.4 | async-start | bytes 4194304 | tf_op jit(solution)/shard_map/all_to_all | solution.py:131
  84.4 34.2 %collective-permute-start = (bf16[4,8,2,64,128]{4,3,2,1,0:T(8,128)(2,1)S(1)}, bf16[4,8,2,64,128]{4,3,2,1,0:T(8,128)(2,1)}, u32[]{:S(2)}, u32[]{:S(2)}) collective-permute-start(bf16[4,8,2,64,128]{4,3,2,1,0:T(8,128)(2,1)S(1)} %all-to-all-done.3.mine_ref), channel_id=1, source_target_pairs={{0,8},{8,0},{1,9},{9,1},{2,10},{10,2},{3,11},{11,3},{4,12},{12,4},... | collective-permute-start | bytes 3145736 | tf_op jit(solution)/shard_map/ppermute | solution.py:127
  110.7 1.2 copy-start

commit v2 on v1

v2 whole, which is shorter than its diff:
```python
import math

import jax
import jax.numpy as jnp
from jax import lax
from jax.experimental import pallas as pl
from jax.experimental.pallas import tpu as pltpu
from jax.sharding import Mesh, PartitionSpec as P

HEAD_DIM = 128
GROUP = 8
KV_HEADS = 8
WIDTH = GROUP * HEAD_DIM
AXES = ("y", "zl", "core", "x", "zh")
SIZES = (8, 4, 2, 4, 2)
CHUNK = 4
SCALE = math.log2(math.e) / math.sqrt(HEAD_DIM)
NEG = -math.inf


def group_columns(g):
    return pl.ds(pl.multiple_of(g * WIDTH, WIDTH), WIDTH)


def attend_set(q_ref, c, k, v, bias):
    rows = q_ref.shape[0]
    first = c * CHUNK * HEAD_DIM
    q = jnp.concatenate(
        [q_ref[:, first + i * HEAD_DIM : first + (i + 1) * HEAD_DIM] for i in range(CHUNK)], axis=0
    )
    s = lax.dot_general(q, k, (((1,), (1,)), ((), ())), preferred_element_type=jnp.float32)
    s = (s.reshape(CHUNK, rows, -1) + bias[None]).reshape(CHUNK * rows, -1)
    m = jnp.max(s, axis=1, keepdims=True)
    e = jnp.exp2((s - m) * SCALE)
    l = jnp.sum(e, axis=1, keepdims=True)
    o = jnp.dot(e.astype(jnp.bfloat16), v, preferred_element_type=jnp.float32)
    return m, l, o


def query_copy(q_hbm, q_buf, sem, g):
    return pltpu.make_async_copy(q_hbm.at[:, group_columns(g)], q_buf.at[g], sem.at[g])


def own_kernel(me, assignment, lengths, q_hbm, *refs):
    pair_refs, (o_ref, lse_ref, bias_ref, q_buf, sem) = refs[:4], refs[4:]
    rows = q_buf.shape[1]
    for g in range(KV_HEADS):
        query_copy(q_hbm, q_buf, sem, g).start()
    head_me = me[0] & 7
    my_len = lengths[assignment[me[0] >> 3]]
    col = lax.broadcasted_iota(jnp.int32, bias_ref.shape, 1)
    row = lax.broadcasted_iota(jnp.int32, bias_ref.shape, 0) + head_me * rows
    pos = (((head_me >> 1) - (col >> 7)) & 3) * 2 * rows + (col & 127)
    bias_ref[...] = jnp.where((pos <= row) & (pos < my_len), 0.0, NEG)

    def column(at):
        cols = pl.ds(pl.multiple_of(at * HEAD_DIM, HEAD_DIM), HEAD_DIM)
        return jnp.concatenate([r[:, :, cols].reshape(2 * rows, HEAD_DIM) for r in pair_refs], axis=0)

    def one_group(g, carry):
        k = column(g)
        v = column(KV_HEADS + g)
        query_copy(q_hbm, q_buf, sem, g).wait()
        for c in range(GROUP // CHUNK):
            m, l, o = attend_set(q_buf.at[g], c, k, v, bias_ref[...])
            at = pl.ds(c * CHUNK * rows, CHUNK * rows)
            o_ref[g, at] = o * (1.0 / l)
            lse_ref[g, at] = jnp.broadcast_to(m * SCALE + jnp.log2(l), o.shape)
        return carry

    lax.fori_loop(0, KV_HEADS, one_group, 0)


def out_copy(out_buf, out_hbm, sem, g):
    return pltpu.make_async_copy(out_buf.at[g], out_hbm.at[:, group_columns(g)], sem.at[g])


def anchor_kernel(
    me, assignment, anchor, lengths, q_hbm, mine_ref, other_ref, o_ref, lse_ref, out_hbm,
    bias_ref, q_buf, out_buf, q_sem, out_sem
):
    rows = q_buf.shape[1]
    for g in range(KV_HEADS):
        query_copy(q_hbm, q_buf, q_sem, g).start()
    anc_len = lengths[anchor[0]]
    is_anchor = assignment[me[0] >> 3] == anchor[0]
    core = (me[0] >> 3) & 1
    col = lax.broadcasted_iota(jnp.int32, bias_ref.shape, 1)
    bias_ref[...] = jnp.where(col < anc_len, 0.0, NEG)

    def one_group(g, carry):
        mine = mine_ref[:, g].reshape(512, HEAD_DIM)
        other = other_ref[:, g].reshape(512, HEAD_DIM)
        k = jnp.where(core == 0, mine, other)
        v = jnp.where(core == 0, other, mine)
        query_copy(q_hbm, q_buf, q_sem, g).wait()
        for c in range(GROUP // CHUNK):
            m1, l1, o1 = attend_set(q_buf.at[g], c, k, v, bias_ref[0:1, :])
            at = pl.ds(c * CHUNK * rows, CHUNK * rows)
            lse1 = jnp.where(is_anchor, NEG, m1 * SCALE + jnp.log2(l1))
            share = 1.0 / (1.0 + jnp.exp2(lse_ref[g, at] - lse1))
            o = (1.0 - share) * o_ref[g, at] + (share * (1.0 / l1)) * o1
            o = o.astype(out_buf.dtype)
            for i in range(CHUNK):
                to = (c * CHUNK + i) * HEAD_DIM
                out_buf[g, :, to : to + HEAD_DIM] = o[i * rows : (i + 1) * rows]
        out_copy(out_buf, out_hbm, out_sem, g).start()
        return carry

    lax.fori_loop(0, KV_HEADS, one_group, 0)
    for g in range(KV_HEADS):
        out_copy(out_buf, out_hbm, out_sem, g).wait()


VMEM = pl.BlockSpec(memory_space=pltpu.VMEM)
SMEM = pl.BlockSpec(memory_space=pltpu.SMEM)
HBM = pl.BlockSpec(memory_space=pltpu.HBM)
COST = pl.CostEstimate(flops=2**30, bytes_accessed=6 * 2**20, transcendentals=2**21)
PARAMS = pltpu.CompilerParams(vmem_limit_bytes=20 * 1024 * 1024)


def attend_own(me, assignment, lengths, queries, own, interpret=False):
    rows = queries.shape[0]
    part = jax.ShapeDtypeStruct((KV_HEADS, GROUP * rows, HEAD_DIM), jnp.float32)
    return pl.pallas_call(
        own_kernel,
        out_shape=(part, part),
        in_specs=[SMEM, SMEM, SMEM, HBM] + [VMEM] * 4,
        out_specs=(VMEM, VMEM),
        scratch_shapes=[
            pltpu.VMEM((rows, 512), jnp.float32),
            pltpu.VMEM((KV_HEADS, rows, WIDTH), jnp.bfloat16),
            pltpu.SemaphoreType.DMA((KV_HEADS,)),
        ],
        compiler_params=PARAMS,
        cost_estimate=COST,
        interpret=interpret,
    )(me, assignment, lengths, queries, *own)


def attend_anchor(me, assignment, anchor, lengths, queries, mine, other, o, lse, interpret=False):
    rows = queries.shape[0]
    return pl.pallas_call(
        anchor_kernel,
        out_shape=jax.ShapeDtypeStruct(queries.shape, jnp.bfloat16),
        in_specs=[SMEM] * 4 + [HBM] + [VMEM] * 4,
        out_specs=HBM,
        scratch_shapes=[
            pltpu.VMEM((8, 512), jnp.float32),
            pltpu.VMEM((KV_HEADS, rows, WIDTH), jnp.bfloat16),
            pltpu.VMEM((KV_HEADS, rows, WIDTH), jnp.bfloat16),
            pltpu.SemaphoreType.DMA((KV_HEADS,)),
            pltpu.SemaphoreType.DMA((KV_HEADS,)),
        ],
        compiler_params=PARAMS,
        cost_estimate=COST,
        interpret=interpret,
    )(me, assignment, anchor, lengths, queries, mine, other, o, lse)


def cut_kernel(k_ref, v_ref, kv_ref, piece_ref):
    half = k_ref.shape[1]
    kv_ref[:, :half] = k_ref[...]
    kv_ref[:, half:] = v_ref[...]
    for core, ref in enumerate((k_ref, v_ref)):
        for g in range(KV_HEADS):
            block = ref[:, g * HEAD_DIM : (g + 1) * HEAD_DIM]
            piece_ref[g, core] = block


def cut(keys, values, interpret=False):
    rows, width = keys.shape
    return pl.pallas_call(
        cut_kernel,
        out_shape=(
            jax.ShapeDtypeStruct((rows, 2 * width), keys.dtype),
            jax.ShapeDtypeStruct((KV_HEADS, 2, rows, HEAD_DIM), keys.dtype),
        ),
        in_specs=[VMEM, VMEM],
        out_specs=(VMEM, VMEM),
        interpret=interpret,
    )(keys, values)


def to_all(a, axes, n):
    return exchange(jnp.broadcast_to(a[None], (n,) + a.shape), axes)


def swap(a, axis):
    return lax.ppermute(a, axis, [(0, 1), (1, 0)])


def exchange(a, axes):
    return lax.all_to_all(a, axes, split_axis=0, concat_axis=0, tiled=True)


def shift(a, axis, by):
    n = lax.axis_size(axis)
    return lax.ppermute(a, axis, [(i, (i + by) % n) for i in range(n)])


def run(me, zh, queries, keys, values, assignment, anchor, lengths, interpret=False):
    ids = jnp.arange(assignment.shape[0], dtype=jnp.int32)
    anchor_shard = jnp.sum(jnp.where(assignment == anchor[0], ids, 0))
    kv, pieces = cut(keys, values, interpret)
    got = exchange(pieces.reshape((16,) + pieces.shape[2:]), ("y", "core"))
    other = swap(kv, "zh")
    source = (anchor_shard >> 3) * 2 + (anchor_shard & 1)
    part = lax.dynamic_index_in_dim(got, source, 0, keepdims=False)
    part = to_all(part, ("zl", "zh"), 8)
    part = part.reshape((4, 2) + part.shape[1:])
    part = lax.dynamic_index_in_dim(part, (anchor_shard >> 1) & 3, 0, keepdims=False)
    part, other = lax.optimization_barrier((part, other))
    pair = jnp.where(zh == 0, jnp.stack([kv, other]), jnp.stack([other, kv]))
    own = [pair] + [shift(pair, "x", s) for s in range(1, 4)]
    part = to_all(part, "y", 8)
    mine = to_all(part, "x", 4)
    o, lse = attend_own(me, assignment, lengths, queries, own, interpret)
    mine, o, lse = lax.optimization_barrier((mine, o, lse))
    theirs = swap(mine, "core")
    return attend_anchor(
        me, assignment, anchor, lengths, queries, mine, theirs, o, lse, interpret
    )


def shards(queries, keys, values, assignment, anchor, lengths):
    me = lax.axis_index(AXES).astype(jnp.int32).reshape(1)
    zh = lax.axis_index("zh")
    return run(me, zh, queries, keys, values, assignment, anchor, lengths)


def solution(mesh):
    fine = Mesh(mesh.devices.reshape(SIZES), AXES)
    spec = P(AXES, None)
    return jax.shard_map(
        shards,
        mesh=fine,
        in_specs=(spec, spec, spec, P(), P(), P()),
        out_specs=spec,
        check_vma=False,
    )
```

time: 129 us -> 145 us (1.12)
  the two profiles are of different devices: /device:TPU:64 before, /device:TPU:1 now
where the time goes in v2:
time: 145 us; the launch traced here: 144 us
  waiting for transfers between devices  58.6 us (40%)
  starting transfers between devices  48.2 us (33%)
  Pallas kernels  17.8 us (12%)
  local copies, waits for them, and re-layouts  15.4 us (11%)
  between operations  2.69 us (2%)
    all_to_all x4, starting transfers between devices, exchange(): return lax.all_to_all(a, axes, split_axis=0, concat_axis=0, tiled=True)  25.9 us
    ppermute x3, waiting for transfers between devices, shift(): return lax.ppermute(a, axis, [(i, (i + by) % n) for i in range(n)])  23.7 us
    all_to_all x4, waiting for transfers between devices, exchange(): return lax.all_to_all(a, axes, split_axis=0, concat_axis=0, tiled=True)  20.2 us
    ppermute x2, waiting for transfers between devices, swap(): return lax.ppermute(a, axis, [(0, 1), (1, 0)])  14.6 us
    unnamed x30, local copies, waits for them, and re-layouts  12.7 us
    ppermute x2, starting transfers between devices, swap(): return lax.ppermute(a, axis, [(0, 1), (1, 0)])  11.5 us
    ppermute x3, starting transfers between devices, shift(): return lax.ppermute(a, axis, [(i, (i + by) % n) for i in range(n)])  10.8 us
    pallas_call x1, Pallas kernels, attend_anchor(): pl.pallas_call(anchor_kernel, out_shape=jax.ShapeDtypeStruct(queries.shap...  8.44 us
  transfers between devices with their start and end apart: 9, of which 6 were waited for; matrix products, arithmetic and copies ran while one was open for 1% of the time, Pallas kernels for 5%

profile of v2, /device:TPU:1, one launch (start us, length us, event | category | flops | bytes accessed | tf_op | source)
XLA Modules:
  0.0 144.1 jit_solution(3873380621305859433)
XLA Ops:
  0.0 1.8 %shard_map.64 = (bf16[64,2048]{1,0:T(8,128)(2,1)}, bf16[8,2,64,128]{3,2,1,0:T(8,128)(2,1)}) custom-call(bf16[64,1024]{1,0:T(8,128)(2,1)} %k_ref.1, bf16[64,1024]{1,0:T(8,128)(2,1)} %v_ref.1), custom_call_target="tpu_custom_call" | custom-call | tf_op jit(solution)/shard_map/pallas_call | solution.py:173
  1.8 10.2 %all-to-all-start = ((bf16[16,64,128]{2,1,0:T(8,128)(2,1)}), bf16[16,64,128]{2,1,0:T(8,128)(2,1)S(1)}, u32[]{:S(2)}, u32[]{:S(2)}) async-start(bf16[16,64,128]{2,1,0:T(8,128)(2,1)} %bitcast.11), calls=%async_computation | async-start | bytes 524288 | tf_op jit(solution)/shard_map/all_to_all | solution.py:194
  12.7 1.3 fusion
  15.3 8.6 %all-to-all-done = bf16[16,64,128]{2,1,0:T(8,128)(2,1)S(1)} async-done(((bf16[16,64,128]{2,1,0:T(8,128)(2,1)}), bf16[16,64,128]{2,1,0:T(8,128)(2,1)S(1)}, u32[]{:S(2)}, u32[]{:S(2)}) %all-to-all-start) | async-done | bytes 262176 | tf_op jit(solution)/shard_map/all_to_all | solution.py:194
  23.9 0.7 broadcast_in_dim.26
  24.6 8.3 %all-to-all-start.1 = ((bf16[8,64,128]{2,1,0:T(8,128)(2,1)}), bf16[8,64,128]{2,1,0:T(8,128)(2,1)S(1)}, u32[]{:S(2)}, u32[]{:S(2)}) async-start(bf16[8,64,128]{2,1,0:T(8,128)(2,1)} %broadcast_in_dim.26), calls=%async_computation.1 | async-start | bytes 262144 | tf_op jit(solution)/shard_map/all_to_all | solution.py:194
  32.9 7.3 %collective-permute-start = (bf16[64,2048]{1,0:T(8,128)(2,1)}, bf16[64,2048]{1,0:T(8,128)(2,1)S(1)}, u32[]{:S(2)}, u32[]{:S(2)}) collective-permute-start(bf16[64,2048]{1,0:T(8,128)(2,1)} %get-tuple-element.15), channel_id=1, source_target_pairs={{0,1},{1,0},{2,3},{3,2},{4,5},{5,4},{6,7},{7,6},{8,9},{9,8},{10,11... | collective-permute-start | bytes 786440 | tf_op jit(solution)/shard_map/ppermute | solution.py:190
  40.8 0.0 all-to-all-done.1
  40.8 0.0 copy-start.14
  40.8 12.4 %collective-permute-done = bf16[64,2048]{1,0:T(8,128)(2,1)S(1)} collective-permute-done((bf16[64,2048]{1,0:T(8,128)(2,1)}, bf16[64,2048]{1,0:T(8,128)(2,1)S(1)}, u32[]{:S(2)}, u32[]{:S(2)}) %collective-permute-start) | collective-permute-done | bytes 262176 | tf_op jit(solution)/shard_map/ppermute | solution.py:190
  53.2 0.8 broadcast_in_dim.27
  53.9 3.4 %all-to-all-start.2 = ((bf16[8,2,64,128]{3,2,1,0:T(8,128)(2,1)}), bf16[8,2,64,128]{3,2,1,0:T(8,128)(2,1)S(1)}, u32[]{:S(2)}, u32[]{:S(2)}) async-start(bf16[8,2,64,128]{3,2,1,0:T(8,128)(2,1)} %broadcast_in_dim.27), calls=%async_computation.2 | async-start | bytes 524288 | tf_op jit(solution)/shard_map/all_to_all | solution.py:194
  57.3 0.0 copy-start.6
  57.3 0.0 copy-start.7
  57.4 11.6 %all-to-all-done.2 = bf16[8,2,64,128]{3,2,1,0:T(8,128)(2,1)S(1)} async-done(((bf16[8,2,64,128]{3,2,1,0:T(8,128)(2,1)}), bf16[8,2,64,128]{3,2,1,0:T(8,128)(2,1)S(1)}, u32[]{:S(2)}, u32[]{:S(2)}) %all-to-all-start.2) | async-done | bytes 262176 | tf_op jit(solution)/shard_map/all_to_all | solution.py:194
  68.9 1.2 broadcast_in_dim.28
  70.2 4.0 %all-to-all-start.3 = ((bf16[4,8,2,64,128]{4,3,2,1,0:T(8,128)(2,1)}), bf16[4,8,2,64,128]{4,3,2,1,0:T(8,128)(2,1)S(1)}, u32[]{:S(2)}, u32[]{:S(2)}) async-start(bf16[4,8,2,64,128]{4,3,2,1,0:T(8,128)(2,1)} %broadcast_in_dim.28), calls=%async_computation.3 | async-start | bytes 2097152 | tf_op jit(solution)/shard_map/all_to_all | solution.py:194
  74.2 0.0 copy-done.14
  74.2 0.1 maximum_select_fusion.refs_0_
  74.3 3.4 %collective-permute-start.1 = (bf16[2,64,2048]{2,1,0:T(8,128)(2,1)S(1)}, bf16[2,64,2048]{2,1,0:T(8,128)(2,1)S(1)}, u32[]{:S(2)}, u32[]{:S(2)}) collective-permute-start(bf16[2,64,2048]{2,1,0:T(8,128)(2,1)S(1)} %maximum_select_fusion.refs_0_), channel_id=1, source_target_pairs={{0,2},{2,4},{4,6},{6,0},{1,3},{3,5},{5,7},{7,1},{8,10},{10,12},{12... | collective-permute-start | bytes 1572872 | tf_op jit(solution)/shard_map/ppermute | solution.py:199
  77.6 4.3 %collective-permute-start.2 = (bf16[2,64,2048]{2,1,0:T(8,128)(2,1)S(1)}, bf16[2,64,2048]{2,1,0:T(8,128)(2,1)S(1)}, u32[]{:S(2)}, u32[]{:S(2)}) collective-permute-start(bf16[2,64,2048]{2,1,0:T(8,128)(2,1)S(1)} %maximum_select_fusion.refs_0_), channel_id=1, source_target_pairs={{0,4},{2,6},{4,0},{6,2},{1,5},{3,7},{5,1},{7,3},{8,12},{10,14},{12... | collective-permute-start | bytes 1572872 | tf_op jit(solution)/shard_map/ppermute | solution.py:199
  82.0 3.1 %collective-permute-start.3 = (bf16[2,64,2048]{2,1,0:T(8,128)(2,1)S(1)}, bf16[2,64,2048]{2,1,0:T(8,128)(2,1)S(1)}, u32[]{:S(2)}, u32[]{:S(2)}) collective-permute-start(bf16[2,64,2048]{2,1,0:T(8,128)(2,1)S(1)} %maximum_select_fusion.refs_0_), channel_id=1, source_target_pairs={{0,6},{2,0},{4,2},{6,4},{1,7},{3,1},{5,3},{7,5},{8,14},{10,8},{12,... | collective-permute-start | bytes 1572872 | tf_op jit(solution)/shard_map/ppermute | solution.py:199
  85.1 0.0 copy-start.4
  85.1 0.8 copy-done.4
  85.9 13.0 %collective-permute-done.1.refs_1_ = bf16[2,64,2048]{2,1,0:T(8,128)(2,1)S(1)} collective-permute-done((bf16[2,64,2048]{2,1,0:T(8,128)(2,1)S(1)}, bf16[2,64,2048]{2,1,0:T(8,128)(2,1)S(1)}, u32[]{:S(2)}, u32[]{:S(2)}) %collective-permute-start.1) | collective-permute-done | bytes 524320 | tf_op jit(solution)/shard_map/ppermute | solution.py:199
  98.8 0.0 copy-start.8
  98.8 0.8 copy-done.8
  99.7 10.8 %collective-permute-done.2.refs_2_ = bf16[2,64,2048]{2,1,0:T(8,128)(2,1)S(1)} collective-permute-done((bf16[2,64,2048]{2,1,0:T(8,128)(2,1)S(1)}, bf16[2,64,2048]{2,1,0:T(8,128)(2,1)S(1)}, u32[]{:S(2)}, u32[]{:S(2)}) %collective-permute-start.2) | collective-permute-done | bytes 524320 | tf_op jit(solution)/shard_map/ppermute | solution.py:199
  110.4 0.0 copy-start.10
  110.4 0.8 copy-done.10
  111.2 0.0 collective-permute-done.3.refs_3_
  111.2 0.0 copy-start.12
  111.2 0.8 copy-done.12
  112.0 0.0 copy-done.6
  112.0 0.0 copy-done.7
  112.0 0.0 copy-start.2
  112.0 1.2 copy-done.2
  113.2 0.0 copy-start.5
  113.2 1.0 copy-done.5
  114.3 0.0 copy-start.9
  114.3 1.0 copy-done.9
  115.3 0.0 copy-start.11
  115.3 1.0 copy-done.11
  116.4 0.0 copy-start.13
  116.4 1.0 copy-done.13
  117.4 7.5 %shard_map.65 = (f32[8,512,128]{2,1,0:T(8,128)S(1)}, f32[8,512,128]{2,1,0:T(8,128)S(1)}) custom-call(s32[1]{0:T(128)} %bitcast.me, s32[64]{0:T(128)S(1)} %copy-done.6, s32[64]{0:T(128)S(1)} %copy-done.7, bf16[64,8192]{1,0:T(8,128)(2,1)S(1)} %copy-done.2, bf16[2,64,2048]{2,1,0:T(8,128)(2,1)S(1)} %copy-done.5, bf16[2,64,2048]{2,1,0:T(8,128)(2,1)S(1)} %copy-done.9, ...), custom_call_target="tpu_custom_call" | custom-call | flops 1073741824 | bytes 6291456 | tf_op jit(solution)/shard_map/pallas_call | solution.py:125
  125.0 0.0 copy-start
  125.0 1.3 copy-done
  126.3 0.0 all-to-all-done.3.mine_ref
  126.3 4.2 %collective-permute-start.4 = (bf16[4,8,2,64,128]{4,3,2,1,0:T(8,128)(2,1)S(1)}, bf16[4,8,2,64,128]{4,3,2,1,0:T(8,128)(2,1)S(1)}, u32[]{:S(2)}, u32[]{:S(2)}) collective-permute-start(bf16[4,8,2,64,128]{4,3,2,1,0:T(8,128)(2,1)S(1)} %all-to-all-done.3.mine_ref), channel_id=1, source_target_pairs={{0,8},{8,0},{1,9},{9,1},{2,10},{10,2},{3,11},{11,3},{4,12},{12,4},... | collective-permute-start | bytes 3145736 | tf_op jit(solution)/shard_map/ppermute | solution.py:190
  130.5 2.3 %collective-permute-done.4.other_ref = bf16[4,8,2,64,128]{4,3,2,1,0:T(8,128)(2,1)S(1)} collective-permute-done((bf16[4,8,2,64,128]{4,3,2,1,0:T(8,128)(2,1)S(1)}, bf16[4,8,2,64,128]{4,3,2,1,0:T(8,128)(2,1)S(1)}, u32[]{:S(2)}, u32[]{:S(2)}) %collective-permute-start.4) | collective-permute-done | bytes 1048608 | tf_op jit(solution)/shard_map/ppermute | solution.py:190
  132.8 0.0 copy-start.1
  132.8 1.6 %copy-done.1 = f32[8,512,128]{2,1,0:T(8,128)S(1)} copy-done((f32[8,512,128]{2,1,0:T(8,128)S(1)}, f32[8,512,128]{2,1,0:T(8,128)}, u32[]{:S(2)}) %copy-start.1) | copy-done | bytes 2097176
  134.4 0.0 copy-start.3
  134.4 1.2 copy-done.3
  135.6 8.4 %shard_map.66 = bf16[64,8192]{1,0:T(8,128)(2,1)} custom-call(s32[1]{0:T(128)} %bitcast.me, s32[64]{0:T(128)S(1)} %copy-done.6, s32[1]{0:T(128)} %copy.7.anchor, s32[64]{0:T(128)S(1)} %copy-done.7, bf16[64,8192]{1,0:T(8,128)(2,1)S(1)} %copy-done.3, bf16[4,8,2,64,128]{4,3,2,1,0:T(8,128)(2,1)S(1)} %all-to-all-done.3.mine_ref, ...), custom_call_target="tpu_custom_call" | custom-call | flops 1073741824 | bytes 6291456 | tf_op jit(solution)/shard_map/pallas_call | solution.py:143
  (2 shorter events, 0.0 us)
Async XLA Ops:
  1.8 22.1 %all-to-all-start = ((bf16[16,64,128]{2,1,0:T(8,128)(2,1)}), bf16[16,64,128]{2,1,0:T(8,128)(2,1)S(1)}, u32[]{:S(2)}, u32[]{:S(2)}) async-start(bf16[16,64,128]{2,1,0:T(8,128)(2,1)} %bitcast.11), calls=%async_computation | async-start | bytes 524288 | tf_op jit(solution)/shard_map/all_to_all | solution.py:194
  24.6 16.2 %all-to-all-start.1 = ((bf16[8,64,128]{2,1,0:T(8,128)(2,1)}), bf16[8,64,128]{2,1,0:T(8,128)(2,1)S(1)}, u32[]{:S(2)}, u32[]{:S(2)}) async-start(bf16[8,64,128]{2,1,0:T(8,128)(2,1)} %broadcast_in_dim.26), calls=%async_computation.1 | async-start | bytes 262144 | tf_op jit(solution)/shard_map/all_to_all | solution.py:194
  32.9 20.3 %collective-permute-start = (bf16[64,2048]{1,0:T(8,128)(2,1)}, bf16[64,2048]{1,0:T(8,128)(2,1)S(1)}, u32[]{:S(2)}, u32[]{:S(2)}) collective-permute-start(bf16[64,2048]{1,0:T(8,128)(2,1)} %get-tuple-element.15), channel_id=1, source_target_pairs={{0,1},{1,0},{2,3},{3,2},{4,5},{5,4},{6,7},{7,6},{8,9},{9,8},{10,11... | collective-permute-start | bytes 786440 | tf_op jit(solution)/shard_map/ppermute | solution.py:190
  40.8 33.4 %copy-start.14 = (bf16[64,2048]{1,0:T(8,128)(2,1)S(1)}, bf16[64,2048]{1,0:T(8,128)(2,1)}, u32[]{:S(2)}) copy-start(bf16[64,2048]{1,0:T(8,128)(2,1)} %get-tuple-element.15) | copy-start | bytes 786436
  53.9 15.0 %all-to-all-start.2 = ((bf16[8,2,64,128]{3,2,1,0:T(8,128)(2,1)}), bf16[8,2,64,128]{3,2,1,0:T(8,128)(2,1)S(1)}, u32[]{:S(2)}, u32[]{:S(2)}) async-start(bf16[8,2,64,128]{3,2,1,0:T(8,128)(2,1)} %broadcast_in_dim.27), calls=%async_computation.2 | async-start | bytes 524288 | tf_op jit(solution)/shard_map/all_to_all | solution.py:194
  57.3 54.7 %copy-start.6 = (s32[64]{0:T(128)S(1)}, s32[64]{0:T(128)}, u32[]{:S(2)}) copy-start(s32[64]{0:T(128)} %assignment.3) | copy-start | bytes 772
  57.3 54.7 %copy-start.7 = (s32[64]{0:T(128)S(1)}, s32[64]{0:T(128)}, u32[]{:S(2)}) copy-start(s32[64]{0:T(128)} %lengths.3) | copy-start | bytes 772
  70.2 56.1 %all-to-all-start.3 = ((bf16[4,8,2,64,128]{4,3,2,1,0:T(8,128)(2,1)}), bf16[4,8,2,64,128]{4,3,2,1,0:T(8,128)(2,1)S(1)}, u32[]{:S(2)}, u32[]{:S(2)}) async-start(bf16[4,8,2,64,128]{4,3,2,1,0:T(8,128)(2,1)} %broadcast_in_dim.28), calls=%async_computation.3 | async-start | bytes 2097152 | tf_op jit(solution)/shard_map/all_to_all | solution.py:194
  74.3 24.6 %collective-permute-start.1 = (bf16[2,64,2048]{2,1,0:T(8,128)(2,1)S(1)}, bf16[2,64,2048]{2,1,0:T(8,128)(2,1)S(1)}, u32[]{:S(2)}, u32[]{:S(2)}) collective-permute-start(bf16[2,64,2048]{2,1,0:T(8,128)(2,1)S(1)} %maximum_select_fusion.refs_0_), channel_id=1, source_target_pairs={{0,2},{2,4},{4,6},{6,0},{1,3},{3,5},{5,7},{7,1},{8,10},{10,12},{12... | collective-permute-start | bytes 1572872 | tf_op jit(solution)/shard_map/ppermute | solution.py:199
  77.6 32.8 %collective-permute-start.2 = (bf16[2,64,2048]{2,1,0:T(8,128)(2,1)S(1)}, bf16[2,64,2048]{2,1,0:T(8,128)(2,1)S(1)}, u32[]{:S(2)}, u32[]{:S(2)}) collective-permute-start(bf16[2,64,2048]{2,1,0:T(8,128)(2,1)S(1)} %maximum_select_fusion.refs_0_), channel_id=1, source_target_pairs={{0,4},{2,6},{4,0},{6,2},{1,5},{3,7},{5,1},{7,3},{8,12},{10,14},{12... | collective-permute-start | bytes 1572872 | tf_op jit(solution)/shard_map/ppermute | solution.py:199
  82.0 29.3 %collective-permute-start.3 = (bf16[2,64,2048]{2,1,0:T(8,128)(2,1)S(1)}, bf16[2,64,2048]{2,1,0:T(8,128)(2,1)S(1)}, u32[]{:S(2)}, u32[]{:S(2)}) collective-permute-start(bf16[2,64,2048]{2,1,0:T(8,128)(2,1)S(1)} %maximum_select_fusion.refs_0_), channel_id=1, source_target_pairs={{0,6},{2,0},{4,2},{6,4},{1,7},{3,1},{5,3},{7,5},{8,14},{10,8},{12,... | collective-permute-start | bytes 1572872 | tf_op jit(solution)/shard_map/ppermute | solution.py:199
  85.1 0.8 copy-start.4
  98.8 0.8 copy-start.8
  110.4 0.8 copy-start.10
  111.2 0.8 copy-start.12
  112.0 1.2 copy-start.2
  113.2 1.0 copy-start.5
  114.3 1.0 copy-start.9
  115.3 1.0 copy-start.11
  116.4 1.0 copy-start.13
  125.0 1.3 copy-start
  126.3 6.5 %collective-permute-start.4 = (bf16[4,8,2,64,128]{4,3,2,1,0:T(8,128)(2,1)S(1)}, bf16[4,8,2,64,128]{4,3,2,1,0:T(8,128)(2,1)S(1)}, u32[]{:S(2)}, u32[]{:S(2)}) collective-permute-start(bf16[4,8,2,64,128]{4,3,2,1,0:T(8,128)(2,1)S(1)} %all-to-all-done.3.mine_ref), channel_id=1, source_target_pairs={{0,8},{8,0},{1,9},{9,1},{2,10},{10,2},{3,11},{11,3},{4,12},{12,4},... | collective-permute-start | bytes 3145736 | tf_op jit(solution)/shard_map/ppermute | solution.py:190
  132.8 1.6 %copy-start.1 = (f32[8,512,128]{2,1,0:T(8,128)S(1)}, f32[8,512,128]{2,1,0:T(8,128)}, u32[]{:S(2)}) copy-start(f32[8,512,128]{2,1,0:T(8,128)} %copy-done) | copy-start | bytes 6291460
  134.4 1.2 copy-start.3

commit v3 on v2

--- a/solution.py
+++ b/solution.py
@@ -42,46 +42,75 @@
 
 
 def own_kernel(me, assignment, lengths, q_hbm, *refs):
-    pair_refs, (o_ref, lse_ref, bias_ref, q_buf, sem) = refs[:4], refs[4:]
+    pairs_hbm, (o_hbm, lse_hbm) = refs[:4], refs[4:6]
+    bias_ref, q_buf, kv_buf, o_buf, lse_buf, q_sem, kv_sem, o_sem, lse_sem = refs[6:]
     rows = q_buf.shape[1]
+    pair_copies = [
+        pltpu.make_async_copy(ref, kv_buf.at[i], kv_sem.at[i]) for i, ref in enumerate(pairs_hbm)
+    ]
+    for copy in pair_copies:
+        copy.start()
     for g in range(KV_HEADS):
-        query_copy(q_hbm, q_buf, sem, g).start()
+        query_copy(q_hbm, q_buf, q_sem, g).start()
     head_me = me[0] & 7
     my_len = lengths[assignment[me[0] >> 3]]
     col = lax.broadcasted_iota(jnp.int32, bias_ref.shape, 1)
     row = lax.broadcasted_iota(jnp.int32, bias_ref.shape, 0) + head_me * rows
     pos = (((head_me >> 1) - (col >> 7)) & 3) * 2 * rows + (col & 127)
     bias_ref[...] = jnp.where((pos <= row) & (pos < my_len), 0.0, NEG)
+    for copy in pair_copies:
+        copy.wait()
 
     def column(at):
         cols = pl.ds(pl.multiple_of(at * HEAD_DIM, HEAD_DIM), HEAD_DIM)
-        return jnp.concatenate([r[:, :, cols].reshape(2 * rows, HEAD_DIM) for r in pair_refs], axis=0)
+        return kv_buf[:, :, :, cols].reshape(8 * rows, HEAD_DIM)
+
+    def result_copies(g):
+        return (
+            pltpu.make_async_copy(o_buf.at[g], o_hbm.at[g], o_sem.at[g]),
+            pltpu.make_async_copy(lse_buf.at[g], lse_hbm.at[g], lse_sem.at[g]),
+        )
 
     def one_group(g, carry):
         k = column(g)
         v = column(KV_HEADS + g)
-        query_copy(q_hbm, q_buf, sem, g).wait()
+        query_copy(q_hbm, q_buf, q_sem, g).wait()
         for c in range(GROUP // CHUNK):
             m, l, o = attend_set(q_buf.at[g], c, k, v, bias_ref[...])
             at = pl.ds(c * CHUNK * rows, CHUNK * rows)
-            o_ref[g, at] = o * (1.0 / l)
-            lse_ref[g, at] = jnp.broadcast_to(m * SCALE + jnp.log2(l), o.shape)
+            o_buf[g, at] = o * (1.0 / l)
+            lse_buf[g, at] = jnp.broadcast_to(m * SCALE + jnp.log2(l), o.shape)
+        for copy in result_copies(g):
+            copy.start()
         return carry
 
     lax.fori_loop(0, KV_HEADS, one_group, 0)
-
-
-def out_copy(out_buf, out_hbm, sem, g):
-    return pltpu.make_async_copy(out_buf.at[g], out_hbm.at[:, group_columns(g)], sem.at[g])
+    for g in range(KV_HEADS):
+        for copy in result_copies(g):
+            copy.wait()
 
 
 def anchor_kernel(
-    me, assignment, anchor, lengths, q_hbm, mine_ref, other_ref, o_ref, lse_ref, out_hbm,
-    bias_ref, q_buf, out_buf, q_sem, out_sem
+    me, assignment, anchor, lengths, q_hbm, mine_hbm, theirs_hbm, o_hbm, lse_hbm, out_hbm,
+    bias_ref, q_buf, mine_buf, theirs_buf, o_buf, lse_buf, out_buf, q_sem, in_sem, out_sem
 ):
     rows = q_buf.shape[1]
+
+    def group_copies(g):
+        return (
+            query_copy(q_hbm, q_buf, q_sem, g),
+            pltpu.make_async_copy(mine_hbm.at[:, g], mine_buf.at[g], in_sem.at[0, g]),
+            pltpu.make_async_copy(theirs_hbm.at[:, g], theirs_buf.at[g], in_sem.at[1, g]),
+            pltpu.make_async_copy(o_hbm.at[g], o_buf.at[g], in_sem.at[2, g]),
+            pltpu.make_async_copy(lse_hbm.at[g], lse_buf.at[g], in_sem.at[3, g]),
+        )
+
+    def out_copy(g):
+        return pltpu.make_async_copy(out_buf.at[g], out_hbm.at[:, group_columns(g)], out_sem.at[g])
+
     for g in range(KV_HEADS):
-        query_copy(q_hbm, q_buf, q_sem, g).start()
+        for copy in group_copies(g):
+            copy.start()
     anc_len = lengths[anchor[0]]
     is_anchor = assignment[me[0] >> 3] == anchor[0]
     core = (me[0] >> 3) & 1
@@ -89,34 +118,36 @@
     bias_ref[...] = jnp.where(col < anc_len, 0.0, NEG)
 
     def one_group(g, carry):
-        mine = mine_ref[:, g].reshape(512, HEAD_DIM)
-        other = other_ref[:, g].reshape(512, HEAD_DIM)
-        k = jnp.where(core == 0, mine, other)
-        v = jnp.where(core == 0, other, mine)
-        query_copy(q_hbm, q_buf, q_sem, g).wait()
+        for copy in group_copies(g):
+            copy.wait()
+        mine = mine_buf[g].reshape(8 * rows, HEAD_DIM)
+        theirs = theirs_buf[g].reshape(8 * rows, HEAD_DIM)
+        k = jnp.where(core == 0, mine, theirs)
+        v = jnp.where(core == 0, theirs, mine)
         for c in range(GROUP // CHUNK):
             m1, l1, o1 = attend_set(q_buf.at[g], c, k, v, bias_ref[0:1, :])
             at = pl.ds(c * CHUNK * rows, CHUNK * rows)
             lse1 = jnp.where(is_anchor, NEG, m1 * SCALE + jnp.log2(l1))
-            share = 1.0 / (1.0 + jnp.exp2(lse_ref[g, at] - lse1))
-            o = (1.0 - share) * o_ref[g, at] + (share * (1.0 / l1)) * o1
+            share = 1.0 / (1.0 + jnp.exp2(lse_buf[g, at] - lse1))
+            o = (1.0 - share) * o_buf[g, at] + (share * (1.0 / l1)) * o1
             o = o.astype(out_buf.dtype)
             for i in range(CHUNK):
                 to = (c * CHUNK + i) * HEAD_DIM
                 out_buf[g, :, to : to + HEAD_DIM] = o[i * rows : (i + 1) * rows]
-        out_copy(out_buf, out_hbm, out_sem, g).start()
+        out_copy(g).start()
         return carry
 
     lax.fori_loop(0, KV_HEADS, one_group, 0)
     for g in range(KV_HEADS):
-        out_copy(out_buf, out_hbm, out_sem, g).wait()
+        out_copy(g).wait()
 
 
 VMEM = pl.BlockSpec(memory_space=pltpu.VMEM)
 SMEM = pl.BlockSpec(memory_space=pltpu.SMEM)
-HBM = pl.BlockSpec(memory_space=pltpu.HBM)
-COST = pl.CostEstimate(flops=2**30, bytes_accessed=6 * 2**20, transcendentals=2**21)
-PARAMS = pltpu.CompilerParams(vmem_limit_bytes=20 * 1024 * 1024)
+ANY = pl.BlockSpec(memory_space=pl.ANY)
+COST = pl.CostEstimate(flops=2**31, bytes_accessed=6 * 2**20, transcendentals=2**21)
+LONG = pl.CostEstimate(flops=2**36, bytes_accessed=6 * 2**20, transcendentals=2**21)
+PARAMS = pltpu.CompilerParams(vmem_limit_bytes=60 * 1024 * 1024)
 
 
 def attend_own(me, assignment, lengths, queries, own, interpret=False):
@@ -125,37 +156,73 @@
     return pl.pallas_call(
         own_kernel,
         out_shape=(part, part),
-        in_specs=[SMEM, SMEM, SMEM, HBM] + [VMEM] * 4,
-        out_specs=(VMEM, VMEM),
+        in_specs=[SMEM, SMEM, SMEM] + [ANY] * 5,
+        out_specs=(ANY, ANY),
         scratch_shapes=[
-            pltpu.VMEM((rows, 512), jnp.float32),
+            pltpu.VMEM((rows, 8 * rows), jnp.float32),
             pltpu.VMEM((KV_HEADS, rows, WIDTH), jnp.bfloat16),
+            pltpu.VMEM((4,) + own[0].shape, jnp.bfloat16),
+            pltpu.VMEM(part.shape, jnp.float32),
+            pltpu.VMEM(part.shape, jnp.float32),
+            pltpu.SemaphoreType.DMA((KV_HEADS,)),
+            pltpu.SemaphoreType.DMA((4,)),
+            pltpu.SemaphoreType.DMA((KV_HEADS,)),
+            pltpu.SemaphoreType.DMA((KV_HEADS,)),
+        ],
+        compiler_params=PARAMS,
+        cost_estimate=LONG,
+        interpret=interpret,
+    )(me, assignment, lengths, queries, *own)
+
+
+def attend_anchor(me, assignment, anchor, lengths, queries, mine, theirs, o, lse, interpret=False):
+    rows = queries.shape[0]
+    group = (KV_HEADS, 4, 2, rows, HEAD_DIM)
+    return pl.pallas_call(
+        anchor_kernel,
+        out_shape=jax.ShapeDtypeStruct(queries.shape, jnp.bfloat16),
+        in_specs=[SMEM] * 4 + [ANY] * 5,
+        out_specs=ANY,
+        scratch_shapes=[
+            pltpu.VMEM((8, 8 * rows), jnp.float32),
+            pltpu.VMEM((KV_HEADS, rows, WIDTH), jnp.bfloat16),
+            pltpu.VMEM(group, jnp.bfloat16),
+            pltpu.VMEM(group, jnp.bfloat16),
+            pltpu.VMEM(o.shape, jnp.float32),
+            pltpu.VMEM(o.shape, jnp.float32),
+            pltpu.VMEM((KV_HEADS, rows, WIDTH), jnp.bfloat16),
+            pltpu.SemaphoreType.DMA((KV_HEADS,)),
+            pltpu.SemaphoreType.DMA((4, KV_HEADS)),
             pltpu.SemaphoreType.DMA((KV_HEADS,)),
         ],
         compiler_params=PARAMS,
         cost_estimate=COST,
         interpret=interpret,
-    )(me, assignment, lengths, queries, *own)
-
-
-def attend_anchor(me, assignment, anchor, lengths, queries, mine, other, o, lse, interpret=False):
-    rows = queries.shape[0]
+    )(me, assignment, anchor, lengths, queries, mine, theirs, o, lse)
+
+
+def pair_kernel(me, kv_hbm, other_hbm, pair_hbm, sem):
+    zh = me[0] & 1
+    copies = (
+        pltpu.make_async_copy(kv_hbm, pair_hbm.at[zh], sem.at[0]),
+        pltpu.make_async_copy(other_hbm, pair_hbm.at[1 - zh], sem.at[1]),
+    )
+    for copy in copies:
+        copy.start()
+    for copy in copies:
+        copy.wait()
+
+
+def make_pair(me, kv, other, interpret=False):
     return pl.pallas_call(
-        anchor_kernel,
-        out_shape=jax.ShapeDtypeStruct(queries.shape, jnp.bfloat16),
-        in_specs=[SMEM] * 4 + [HBM] + [VMEM] * 4,
-        out_specs=HBM,
-        scratch_shapes=[
-            pltpu.VMEM((8, 512), jnp.float32),
-            pltpu.VMEM((KV_HEADS, rows, WIDTH), jnp.bfloat16),
-            pltpu.VMEM((KV_HEADS, rows, WIDTH), jnp.bfloat16),
-            pltpu.SemaphoreType.DMA((KV_HEADS,)),
-            pltpu.SemaphoreType.DMA((KV_HEADS,)),
-        ],
-        compiler_params=PARAMS,
-        cost_estimate=COST,
+        pair_kernel,
+        out_shape=jax.ShapeDtypeStruct((2,) + kv.shape, kv.dtype),
+        in_specs=[SMEM, ANY, ANY],
+        out_specs=ANY,
+        scratch_shapes=[pltpu.SemaphoreType.DMA((2,))],
+        cost_estimate=LONG,
         interpret=interpret,
-    )(me, assignment, anchor, lengths, queries, mine, other, o, lse)
+    )(me, kv, other)
 
 
 def cut_kernel(k_ref, v_ref, kv_ref, piece_ref):
@@ -199,7 +266,7 @@
     return lax.ppermute(a, axis, [(i, (i + by) % n) for i in range(n)])
 
 
-def run(me, zh, queries, keys, values, assignment, anchor, lengths, interpret=False):
+def run(me, queries, keys, values, assignment, anchor, lengths, interpret=False):
     ids = jnp.arange(assignment.shape[0], dtype=jnp.int32)
     anchor_shard = jnp.sum(jnp.where(assignment == anchor[0], ids, 0))
     kv, pieces = cut(keys, values, interpret)
@@ -210,8 +277,8 @@
     part = to_all(part, ("zl", "zh"), 8)
     part = part.reshape((4, 2) + part.shape[1:])
     part = lax.dynamic_index_in_dim(part, (anchor_shard >> 1) & 3, 0, keepdims=False)
-    part, other = lax.optimization_barrier((part, other))
-    pair = jnp.where(zh == 0, jnp.stack([kv, other]), jnp.stack([other, kv]))
+    pair = make_pair(me, kv, other, interpret)
+    part, pair = lax.optimization_barrier((part, pair))
     own = [pair] + [shift(pair, "x", s) for s in range(1, 4)]
     part = to_all(part, "y", 8)
     mine = to_all(part, "x", 4)
@@ -225,8 +292,7 @@
 
 def shards(queries, keys, values, assignment, anchor, lengths):
     me = lax.axis_index(AXES).astype(jnp.int32).reshape(1)
-    zh = lax.axis_index("zh")
-    return run(me, zh, queries, keys, values, assignment, anchor, lengths)
+    return run(me, queries, keys, values, assignment, anchor, lengths)
 
 
 def solution(mesh):

time: 145 us -> 114 us (0.79)
  waiting for transfers between devices: 58.6 us -> 5.36 us
  Pallas kernels: 17.8 us -> 39.8 us
  blocking collectives: 0 us -> 12.3 us
  local copies, waits for them, and re-layouts: 15.4 us -> 4.49 us
    ppermute x3, waiting for transfers between devices: 23.7 us -> 3.08 us  [shift(): return lax.ppermute(a, axis, [(i, (i + by) % n) for i in range(n)])]
    all_to_all x4 -> x3, waiting for transfers between devices: 20.2 us -> 0.01 us  [exchange(): return lax.all_to_all(a, axes, split_axis=0, concat_axis=0, tiled=True)]
    pallas_call x0 -> x1, Pallas kernels: none -> 17 us  [make_pair(): pl.pallas_call(pair_kernel, out_shape=jax.ShapeDtypeStruct((2,) + kv.shap...]
    ppermute x2, waiting for transfers between devices: 14.6 us -> 2.27 us  [swap(): return lax.ppermute(a, axis, [(0, 1), (1, 0)])]
    all_to_all x0 -> x1, blocking collectives: none -> 12.3 us  [exchange(): return lax.all_to_all(a, axes, split_axis=0, concat_axis=0, tiled=True)]
    unnamed x30 -> x12, local copies, waits for them, and re-layouts: 12.7 us -> 2.53 us
    all_to_all x4 -> x3, starting transfers between devices: 25.9 us -> 21.4 us  [exchange(): return lax.all_to_all(a, axes, split_axis=0, concat_axis=0, tiled=True)]
    ppermute x2, starting transfers between devices: 11.5 us -> 15.3 us  [swap(): return lax.ppermute(a, axis, [(0, 1), (1, 0)])]
  transfers between devices with their start and end apart: 9 -> 8, of which waited for: 6 -> 3; matrix products, arithmetic and copies ran while one was open for 1% -> 3% of each run, Pallas kernels for 5% -> 24%
where the time goes in v3:
time: 114 us; the launch traced here: 113 us
  starting transfers between devices  47.3 us (41%)
  Pallas kernels  39.8 us (35%)
  blocking collectives  12.3 us (11%)
  waiting for transfers between devices  5.36 us (5%)
  local copies, waits for them, and re-layouts  4.49 us (4%)
  between operations  2.53 us (2%)
  other arithmetic  1.29 us (1%)
    all_to_all x3, starting transfers between devices, exchange(): return lax.all_to_all(a, axes, split_axis=0, concat_axis=0, tiled=True)  21.4 us
    pallas_call x1, Pallas kernels, make_pair(): pl.pallas_call(pair_kernel, out_shape=jax.ShapeDtypeStruct((2,) + kv.shap...  17 us
    ppermute x2, starting transfers between devices, swap(): return lax.ppermute(a, axis, [(0, 1), (1, 0)])  15.3 us
    all_to_all x1, blocking collectives, exchange(): return lax.all_to_all(a, axes, split_axis=0, concat_axis=0, tiled=True)  12.3 us
    pallas_call x1, Pallas kernels, attend_anchor(): pl.pallas_call(anchor_kernel, out_shape=jax.ShapeDtypeStruct(queries.shap...  10.7 us
    ppermute x3, starting transfers between devices, shift(): return lax.ppermute(a, axis, [(i, (i + by) % n) for i in range(n)])  10.5 us
    pallas_call x1, Pallas kernels, attend_own(): pl.pallas_call(own_kernel, out_shape=(part, part), in_specs=[SMEM, SMEM,...  10.3 us
    ppermute x3, waiting for transfers between devices, shift(): return lax.ppermute(a, axis, [(i, (i + by) % n) for i in range(n)])  3.08 us
  transfers between devices with their start and end apart: 8, of which 3 were waited for; matrix products, arithmetic and copies ran while one was open for 3% of the time, Pallas kernels for 24%

profile of v3, /device:TPU:1, one launch (start us, length us, event | category | flops | bytes accessed | tf_op | source)
XLA Modules:
  0.0 113.0 jit_solution(9174855213307731346)
XLA Ops:
  0.0 1.8 %shard_map.64 = (bf16[64,2048]{1,0:T(8,128)(2,1)}, bf16[8,2,64,128]{3,2,1,0:T(8,128)(2,1)}) custom-call(bf16[64,1024]{1,0:T(8,128)(2,1)} %k_ref.1, bf16[64,1024]{1,0:T(8,128)(2,1)} %v_ref.1), custom_call_target="tpu_custom_call" | custom-call | tf_op jit(solution)/shard_map/pallas_call | solution.py:240
  1.8 10.2 %all-to-all-start = ((bf16[16,64,128]{2,1,0:T(8,128)(2,1)}), bf16[16,64,128]{2,1,0:T(8,128)(2,1)S(1)}, u32[]{:S(2)}, u32[]{:S(2)}) async-start(bf16[16,64,128]{2,1,0:T(8,128)(2,1)} %bitcast.9), calls=%async_computation | async-start | bytes 524288 | tf_op jit(solution)/shard_map/all_to_all | solution.py:261
  12.0 9.1 %collective-permute-start = (bf16[64,2048]{1,0:T(8,128)(2,1)}, bf16[64,2048]{1,0:T(8,128)(2,1)S(1)}, u32[]{:S(2)}, u32[]{:S(2)}) collective-permute-start(bf16[64,2048]{1,0:T(8,128)(2,1)} %get-tuple-element.15.kv_hbm), channel_id=1, source_target_pairs={{0,1},{1,0},{2,3},{3,2},{4,5},{5,4},{6,7},{7,6},{8,9},{9,8},{10,11... | collective-permute-start | bytes 786440 | tf_op jit(solution)/shard_map/ppermute | solution.py:257
  21.7 1.3 %fusion = s32[]{:T(128)} fusion(s32[64]{0:T(128)} %assignment.3, s32[]{:T(128)} %bitcast.8), kind=kLoop, calls=%fused_computation.3 | loop fusion | flops 191 | bytes 264 | tf_op jit(solution)/shard_map/reduce_sum | solution.py:271
  24.7 0.0 all-to-all-done
  24.8 0.7 broadcast_in_dim.26
  25.4 7.7 %all-to-all-start.1 = ((bf16[8,64,128]{2,1,0:T(8,128)(2,1)}), bf16[8,64,128]{2,1,0:T(8,128)(2,1)S(1)}, u32[]{:S(2)}, u32[]{:S(2)}) async-start(bf16[8,64,128]{2,1,0:T(8,128)(2,1)} %broadcast_in_dim.26), calls=%async_computation.1 | async-start | bytes 262144 | tf_op jit(solution)/shard_map/all_to_all | solution.py:261
  33.1 0.0 collective-permute-done.other_hbm
  33.1 0.0 copy-start.5
  33.2 0.7 copy-done.5
  33.8 17.0 %shard_map.65.refs_0_ = bf16[2,64,2048]{2,1,0:T(8,128)(2,1)} custom-call(s32[1]{0:T(128)} %bitcast.me, bf16[64,2048]{1,0:T(8,128)(2,1)} %get-tuple-element.15.kv_hbm, bf16[64,2048]{1,0:T(8,128)(2,1)} %copy-done.5), custom_call_target="tpu_custom_call" | custom-call | flops 68719476736 | bytes 6291456 | tf_op jit(solution)/shard_map/pallas_call | solution.py:217
  50.9 0.0 all-to-all-done.1
  50.9 3.1 %collective-permute-start.1 = (bf16[2,64,2048]{2,1,0:T(8,128)(2,1)}, bf16[2,64,2048]{2,1,0:T(8,128)(2,1)S(1)}, u32[]{:S(2)}, u32[]{:S(2)}) collective-permute-start(bf16[2,64,2048]{2,1,0:T(8,128)(2,1)} %shard_map.65.refs_0_), channel_id=1, source_target_pairs={{0,2},{2,4},{4,6},{6,0},{1,3},{3,5},{5,7},{7,1},{8,10},{10,12},{12... | collective-permute-start | bytes 1572872 | tf_op jit(solution)/shard_map/ppermute | solution.py:266
  54.0 4.4 %collective-permute-start.2 = (bf16[2,64,2048]{2,1,0:T(8,128)(2,1)}, bf16[2,64,2048]{2,1,0:T(8,128)(2,1)S(1)}, u32[]{:S(2)}, u32[]{:S(2)}) collective-permute-start(bf16[2,64,2048]{2,1,0:T(8,128)(2,1)} %shard_map.65.refs_0_), channel_id=1, source_target_pairs={{0,4},{2,6},{4,0},{6,2},{1,5},{3,7},{5,1},{7,3},{8,12},{10,14},{12... | collective-permute-start | bytes 1572872 | tf_op jit(solution)/shard_map/ppermute | solution.py:266
  58.4 3.1 %collective-permute-start.3 = (bf16[2,64,2048]{2,1,0:T(8,128)(2,1)}, bf16[2,64,2048]{2,1,0:T(8,128)(2,1)S(1)}, u32[]{:S(2)}, u32[]{:S(2)}) collective-permute-start(bf16[2,64,2048]{2,1,0:T(8,128)(2,1)} %shard_map.65.refs_0_), channel_id=1, source_target_pairs={{0,6},{2,0},{4,2},{6,4},{1,7},{3,1},{5,3},{7,5},{8,14},{10,8},{12,... | collective-permute-start | bytes 1572872 | tf_op jit(solution)/shard_map/ppermute | solution.py:266
  61.5 12.3 %all_to_all.20 = bf16[8,2,64,128]{3,2,1,0:T(8,128)(2,1)S(1)} all-to-all(bf16[8,2,64,128]{3,2,1,0:T(8,128)(2,1)S(1)} %broadcast_in_dim.27), channel_id=1, replica_groups=mesh['y'=8,'zl'=4,'core'=2,'x'=4,'zh'=2] {'y'}, dimensions={0} | all-to-all | bytes 524288 | tf_op jit(solution)/shard_map/all_to_all | solution.py:261
  73.8 1.2 %broadcast_in_dim.28 = bf16[4,8,2,64,128]{4,3,2,1,0:T(8,128)(2,1)} broadcast(bf16[8,2,64,128]{3,2,1,0:T(8,128)(2,1)S(1)} %all_to_all.20), dimensions={1,2,3,4} | broadcast | bytes 1310720 | tf_op jit(solution)/shard_map/broadcast_in_dim | solution.py:253
  75.0 3.5 %all-to-all-start.3 = ((bf16[4,8,2,64,128]{4,3,2,1,0:T(8,128)(2,1)}), bf16[4,8,2,64,128]{4,3,2,1,0:T(8,128)(2,1)S(1)}, u32[]{:S(2)}, u32[]{:S(2)}) async-start(bf16[4,8,2,64,128]{4,3,2,1,0:T(8,128)(2,1)} %broadcast_in_dim.28), calls=%async_computation.3 | async-start | bytes 2097152 | tf_op jit(solution)/shard_map/all_to_all | solution.py:261
  78.5 0.0 collective-permute-done.1.refs_1_
  78.5 0.0 copy-start.2
  78.5 1.8 %collective-permute-done.2.refs_2_ = bf16[2,64,2048]{2,1,0:T(8,128)(2,1)S(1)} collective-permute-done((bf16[2,64,2048]{2,1,0:T(8,128)(2,1)}, bf16[2,64,2048]{2,1,0:T(8,128)(2,1)S(1)}, u32[]{:S(2)}, u32[]{:S(2)}) %collective-permute-start.2) | collective-permute-done | bytes 524320 | tf_op jit(solution)/shard_map/ppermute | solution.py:266
  80.3 0.0 copy-start.3
  80.3 1.3 %collective-permute-done.3.refs_3_ = bf16[2,64,2048]{2,1,0:T(8,128)(2,1)S(1)} collective-permute-done((bf16[2,64,2048]{2,1,0:T(8,128)(2,1)}, bf16[2,64,2048]{2,1,0:T(8,128)(2,1)S(1)}, u32[]{:S(2)}, u32[]{:S(2)}) %collective-permute-start.3) | collective-permute-done | bytes 524320 | tf_op jit(solution)/shard_map/ppermute | solution.py:266
  81.6 0.0 copy-done.2
  81.6 0.0 copy-done.3
  81.6 0.0 copy-start.4
  81.6 0.8 copy-done.4
  82.4 10.3 %shard_map.66 = (f32[8,512,128]{2,1,0:T(8,128)}, f32[8,512,128]{2,1,0:T(8,128)}) custom-call(s32[1]{0:T(128)} %bitcast.me, s32[64]{0:T(128)} %assignment.3, s32[64]{0:T(128)} %lengths.3, bf16[64,8192]{1,0:T(8,128)(2,1)} %q_hbm.3, bf16[2,64,2048]{2,1,0:T(8,128)(2,1)} %shard_map.65.refs_0_, bf16[2,64,2048]{2,1,0:T(8,128)(2,1)} %copy-done.2, ...), custom_call_target="tpu_custom_call" | custom-call | flops 68719476736 | bytes 6291456 | tf_op jit(solution)/shard_map/pallas_call | solution.py:156
  92.7 0.0 all-to-all-done.3.mine_hbm
  92.7 0.0 copy-start
  92.7 6.3 %collective-permute-start.4 = (bf16[4,8,2,64,128]{4,3,2,1,0:T(8,128)(2,1)S(1)}, bf16[4,8,2,64,128]{4,3,2,1,0:T(8,128)(2,1)S(1)}, u32[]{:S(2)}, u32[]{:S(2)}) collective-permute-start(bf16[4,8,2,64,128]{4,3,2,1,0:T(8,128)(2,1)S(1)} %all-to-all-done.3.mine_hbm), channel_id=1, source_target_pairs={{0,8},{8,0},{1,9},{9,1},{2,10},{10,2},{3,11},{11,3},{4,12},{12,4},... | collective-permute-start | bytes 3145736 | tf_op jit(solution)/shard_map/ppermute | solution.py:257
  99.0 2.3 %collective-permute-done.4.theirs_hbm = bf16[4,8,2,64,128]{4,3,2,1,0:T(8,128)(2,1)S(1)} collective-permute-done((bf16[4,8,2,64,128]{4,3,2,1,0:T(8,128)(2,1)S(1)}, bf16[4,8,2,64,128]{4,3,2,1,0:T(8,128)(2,1)S(1)}, u32[]{:S(2)}, u32[]{:S(2)}) %collective-permute-start.4) | collective-permute-done | bytes 1048608 | tf_op jit(solution)/shard_map/ppermute | solution.py:257
  101.3 0.0 copy-done
  101.3 0.0 copy-start.1
  101.3 1.0 copy-done.1
  102.3 10.7 %shard_map.67 = bf16[64,8192]{1,0:T(8,128)(2,1)} custom-call(s32[1]{0:T(128)} %bitcast.me, s32[64]{0:T(128)} %assignment.3, s32[1]{0:T(128)} %copy.7.anchor, s32[64]{0:T(128)} %lengths.3, bf16[64,8192]{1,0:T(8,128)(2,1)} %q_hbm.3, bf16[4,8,2,64,128]{4,3,2,1,0:T(8,128)(2,1)} %copy-done, bf16[4,8,2,64,128]{4,3,2,1,0:T(8,128)(2,1)} %copy-done.1, ...), custom_call_target="tpu_custom_call" | custom-call | flops 2147483648 | bytes 6291456 | tf_op jit(solution)/shard_map/pallas_call | solution.py:181
  (3 shorter events, 0.1 us)
Async XLA Ops:
  1.8 22.9 %all-to-all-start = ((bf16[16,64,128]{2,1,0:T(8,128)(2,1)}), bf16[16,64,128]{2,1,0:T(8,128)(2,1)S(1)}, u32[]{:S(2)}, u32[]{:S(2)}) async-start(bf16[16,64,128]{2,1,0:T(8,128)(2,1)} %bitcast.9), calls=%async_computation | async-start | bytes 524288 | tf_op jit(solution)/shard_map/all_to_all | solution.py:261
  12.0 21.1 %collective-permute-start = (bf16[64,2048]{1,0:T(8,128)(2,1)}, bf16[64,2048]{1,0:T(8,128)(2,1)S(1)}, u32[]{:S(2)}, u32[]{:S(2)}) collective-permute-start(bf16[64,2048]{1,0:T(8,128)(2,1)} %get-tuple-element.15.kv_hbm), channel_id=1, source_target_pairs={{0,1},{1,0},{2,3},{3,2},{4,5},{5,4},{6,7},{7,6},{8,9},{9,8},{10,11... | collective-permute-start | bytes 786440 | tf_op jit(solution)/shard_map/ppermute | solution.py:257
  25.4 25.4 %all-to-all-start.1 = ((bf16[8,64,128]{2,1,0:T(8,128)(2,1)}), bf16[8,64,128]{2,1,0:T(8,128)(2,1)S(1)}, u32[]{:S(2)}, u32[]{:S(2)}) async-start(bf16[8,64,128]{2,1,0:T(8,128)(2,1)} %broadcast_in_dim.26), calls=%async_computation.1 | async-start | bytes 262144 | tf_op jit(solution)/shard_map/all_to_all | solution.py:261
  33.1 0.7 copy-start.5
  50.9 27.6 %collective-permute-start.1 = (bf16[2,64,2048]{2,1,0:T(8,128)(2,1)}, bf16[2,64,2048]{2,1,0:T(8,128)(2,1)S(1)}, u32[]{:S(2)}, u32[]{:S(2)}) collective-permute-start(bf16[2,64,2048]{2,1,0:T(8,128)(2,1)} %shard_map.65.refs_0_), channel_id=1, source_target_pairs={{0,2},{2,4},{4,6},{6,0},{1,3},{3,5},{5,7},{7,1},{8,10},{10,12},{12... | collective-permute-start | bytes 1572872 | tf_op jit(solution)/shard_map/ppermute | solution.py:266
  54.0 26.3 %collective-permute-start.2 = (bf16[2,64,2048]{2,1,0:T(8,128)(2,1)}, bf16[2,64,2048]{2,1,0:T(8,128)(2,1)S(1)}, u32[]{:S(2)}, u32[]{:S(2)}) collective-permute-start(bf16[2,64,2048]{2,1,0:T(8,128)(2,1)} %shard_map.65.refs_0_), channel_id=1, source_target_pairs={{0,4},{2,6},{4,0},{6,2},{1,5},{3,7},{5,1},{7,3},{8,12},{10,14},{12... | collective-permute-start | bytes 1572872 | tf_op jit(solution)/shard_map/ppermute | solution.py:266
  58.4 23.2 %collective-permute-start.3 = (bf16[2,64,2048]{2,1,0:T(8,128)(2,1)}, bf16[2,64,2048]{2,1,0:T(8,128)(2,1)S(1)}, u32[]{:S(2)}, u32[]{:S(2)}) collective-permute-start(bf16[2,64,2048]{2,1,0:T(8,128)(2,1)} %shard_map.65.refs_0_), channel_id=1, source_target_pairs={{0,6},{2,0},{4,2},{6,4},{1,7},{3,1},{5,3},{7,5},{8,14},{10,8},{12,... | collective-permute-start | bytes 1572872 | tf_op jit(solution)/shard_map/ppermute | solution.py:266
  75.0 17.7 %all-to-all-start.3 = ((bf16[4,8,2,64,128]{4,3,2,1,0:T(8,128)(2,1)}), bf16[4,8,2,64,128]{4,3,2,1,0:T(8,128)(2,1)S(1)}, u32[]{:S(2)}, u32[]{:S(2)}) async-start(bf16[4,8,2,64,128]{4,3,2,1,0:T(8,128)(2,1)} %broadcast_in_dim.28), calls=%async_computation.3 | async-start | bytes 2097152 | tf_op jit(solution)/shard_map/all_to_all | solution.py:261
  78.5 3.1 %copy-start.2 = (bf16[2,64,2048]{2,1,0:T(8,128)(2,1)}, bf16[2,64,2048]{2,1,0:T(8,128)(2,1)S(1)}, u32[]{:S(2)}) copy-start(bf16[2,64,2048]{2,1,0:T(8,128)(2,1)S(1)} %collective-permute-done.1.refs_1_) | copy-start | bytes 1572868
  80.3 1.3 %copy-start.3 = (bf16[2,64,2048]{2,1,0:T(8,128)(2,1)}, bf16[2,64,2048]{2,1,0:T(8,128)(2,1)S(1)}, u32[]{:S(2)}) copy-start(bf16[2,64,2048]{2,1,0:T(8,128)(2,1)S(1)} %collective-permute-done.2.refs_2_) | copy-start | bytes 1572868
  81.6 0.8 copy-start.4
  92.7 8.5 %copy-start = (bf16[4,8,2,64,128]{4,3,2,1,0:T(8,128)(2,1)}, bf16[4,8,2,64,128]{4,3,2,1,0:T(8,128)(2,1)S(1)}, u32[]{:S(2)}) copy-start(bf16[4,8,2,64,128]{4,3,2,1,0:T(8,128)(2,1)S(1)} %all-to-all-done.3.mine_hbm) | copy-start | bytes 3145732
  92.7 8.5 %collective-permute-start.4 = (bf16[4,8,2,64,128]{4,3,2,1,0:T(8,128)(2,1)S(1)}, bf16[4,8,2,64,128]{4,3,2,1,0:T(8,128)(2,1)S(1)}, u32[]{:S(2)}, u32[]{:S(2)}) collective-permute-start(bf16[4,8,2,64,128]{4,3,2,1,0:T(8,128)(2,1)S(1)} %all-to-all-done.3.mine_hbm), channel_id=1, source_target_pairs={{0,8},{8,0},{1,9},{9,1},{2,10},{10,2},{3,11},{11,3},{4,12},{12,4},... | collective-permute-start | bytes 3145736 | tf_op jit(solution)/shard_map/ppermute | solution.py:257
  101.3 1.0 copy-start.1

commit v4 on v3

v4 whole, which is shorter than its diff:
```python
import functools
import math

import jax
import jax.numpy as jnp
from jax import lax
from jax.experimental import pallas as pl
from jax.experimental.pallas import tpu as pltpu
from jax.sharding import Mesh, PartitionSpec as P

HEAD_DIM = 128
GROUP = 8
KV_HEADS = 8
HALF = 4
WIDTH = GROUP * HEAD_DIM
AXES = ("y", "zl", "core", "x", "zh")
SIZES = (8, 4, 2, 4, 2)
CHUNK = 4
SCALE = math.log2(math.e) / math.sqrt(HEAD_DIM)
NEG = -math.inf


def group_columns(g):
    return pl.ds(pl.multiple_of(g * WIDTH, WIDTH), WIDTH)


def attend_set(q_ref, c, k, v, bias):
    rows = q_ref.shape[0]
    first = c * CHUNK * HEAD_DIM
    q = jnp.concatenate(
        [q_ref[:, first + i * HEAD_DIM : first + (i + 1) * HEAD_DIM] for i in range(CHUNK)], axis=0
    )
    s = lax.dot_general(q, k, (((1,), (1,)), ((), ())), preferred_element_type=jnp.float32)
    free = s.shape[1] - bias.shape[1]
    tail = (s[:, free:].reshape(CHUNK, rows, -1) + bias[None]).reshape(CHUNK * rows, -1)
    s = jnp.concatenate([s[:, :free], tail], axis=1) if free else tail
    m = jnp.max(s, axis=1, keepdims=True)
    e = jnp.exp2((s - m) * SCALE)
    l = jnp.sum(e, axis=1, keepdims=True)
    o = jnp.dot(e.astype(jnp.bfloat16), v, preferred_element_type=jnp.float32)
    return m, l, o


def query_copy(q_hbm, q_buf, sem, g):
    return pltpu.make_async_copy(q_hbm.at[:, group_columns(g)], q_buf.at[g], sem.at[g])


def start_ahead(copies, g, count=KV_HEADS):
    def start():
        for copy in copies(g):
            copy.start()

    if isinstance(g, int):
        start()
    else:
        pl.when(g < count)(start)


def two_at_a_time(body, count):
    def step(i, carry):
        body(2 * i)
        body(2 * i + 1)
        return carry

    lax.fori_loop(0, count // 2, step, 0)


def own_kernel(me, assignment, lengths, q_hbm, *refs):
    pairs_hbm, (o_hbm, lse_hbm) = refs[:4], refs[4:6]
    bias_ref, q_buf, kv_buf, o_buf, lse_buf, q_sem, kv_sem, o_sem, lse_sem = refs[6:]
    rows = q_buf.shape[1]

    def group_copies(g):
        return [query_copy(q_hbm, q_buf, q_sem, g)] + [
            pltpu.make_async_copy(ref.at[:, g & 3, :, g >> 2], kv_buf.at[g, i], kv_sem.at[i, g])
            for i, ref in enumerate(pairs_hbm)
        ]

    start_ahead(group_copies, 0)
    start_ahead(group_copies, 1)
    head_me = me[0] & 7
    my_len = lengths[assignment[me[0] >> 3]]
    col = lax.broadcasted_iota(jnp.int32, bias_ref.shape, 1)
    row = lax.broadcasted_iota(jnp.int32, bias_ref.shape, 0) + head_me * rows
    pos = (((head_me >> 1) - (col >> 7)) & 3) * 2 * rows + (col & 127)
    bias_ref[...] = jnp.where((pos <= row) & (pos < my_len), 0.0, NEG)
    def result_copies(g):
        return (
            pltpu.make_async_copy(o_buf.at[g], o_hbm.at[g], o_sem.at[g]),
            pltpu.make_async_copy(lse_buf.at[g], lse_hbm.at[g], lse_sem.at[g]),
        )

    def one_group(g):
        start_ahead(group_copies, g + 2)
        for copy in group_copies(g):
            copy.wait()
        k = kv_buf[g, :, :, 0].reshape(8 * rows, HEAD_DIM)
        v = kv_buf[g, :, :, 1].reshape(8 * rows, HEAD_DIM)
        for c in range(GROUP // CHUNK):
            m, l, o = attend_set(q_buf.at[g], c, k, v, bias_ref[...])
            at = pl.ds(c * CHUNK * rows, CHUNK * rows)
            o_buf[g, at] = o * (1.0 / l)
            lse_buf[g, at] = jnp.broadcast_to(m * SCALE + jnp.log2(l), o.shape)
        for copy in result_copies(g):
            copy.start()

    two_at_a_time(one_group, KV_HEADS)
    for g in range(KV_HEADS):
        for copy in result_copies(g):
            copy.wait()


def anchor_kernel(which, me, assignment, anchor, lengths, q_hbm, kv_hbm, o_hbm, lse_hbm, *refs):
    out_hbm, bias_ref, q_buf, kv_buf, o_buf, lse_buf, out_buf, in_sem, out_sem = refs[-9:]
    rows = q_buf.shape[1]
    core = (me[0] >> 3) & 1
    first = (core ^ which) * HALF

    def group_copies(i):
        g = first + i
        return (
            pltpu.make_async_copy(q_hbm.at[:, group_columns(g)], q_buf.at[i], in_sem.at[0, i]),
            pltpu.make_async_copy(kv_hbm.at[:, pl.ds(2 * i, 2)], kv_buf.at[i], in_sem.at[1, i]),
            pltpu.make_async_copy(o_hbm.at[g], o_buf.at[i], in_sem.at[2, i]),
            pltpu.make_async_copy(lse_hbm.at[g], lse_buf.at[i], in_sem.at[3, i]),
        )

    def out_copy(i):
        to = out_hbm.at[:, group_columns(first + i)]
        return pltpu.make_async_copy(out_buf.at[i], to, out_sem.at[i])

    start_ahead(group_copies, 0)
    start_ahead(group_copies, 1)
    anc_len = lengths[anchor[0]]
    is_anchor = assignment[me[0] >> 3] == anchor[0]
    col = lax.broadcasted_iota(jnp.int32, bias_ref.shape, 1) + 256
    bias_ref[...] = jnp.where(col < anc_len, 0.0, NEG)

    def one_group(i):
        start_ahead(group_copies, i + 2, HALF)
        for copy in group_copies(i):
            copy.wait()
        k = kv_buf[i, :, 0].reshape(8 * rows, HEAD_DIM)
        v = kv_buf[i, :, 1].reshape(8 * rows, HEAD_DIM)
        for c in range(GROUP // CHUNK):
            m1, l1, o1 = attend_set(q_buf.at[i], c, k, v, bias_ref[0:1, :])
            at = pl.ds(c * CHUNK * rows, CHUNK * rows)
            lse1 = jnp.where(is_anchor, NEG, m1 * SCALE + jnp.log2(l1))
            share = 1.0 / (1.0 + jnp.exp2(lse_buf[i, at] - lse1))
            o = (1.0 - share) * o_buf[i, at] + (share * (1.0 / l1)) * o1
            o = o.astype(out_buf.dtype)
            for j in range(CHUNK):
                to = (c * CHUNK + j) * HEAD_DIM
                out_buf[i, :, to : to + HEAD_DIM] = o[j * rows : (j + 1) * rows]
        out_copy(i).start()

    two_at_a_time(one_group, HALF)
    for i in range(HALF):
        out_copy(i).wait()


VMEM = pl.BlockSpec(memory_space=pltpu.VMEM)
SMEM = pl.BlockSpec(memory_space=pltpu.SMEM)
ANY = pl.BlockSpec(memory_space=pl.ANY)
COST = pl.CostEstimate(flops=2**31, bytes_accessed=6 * 2**20, transcendentals=2**21)
LONG = pl.CostEstimate(flops=2**36, bytes_accessed=6 * 2**20, transcendentals=2**21)
PARAMS = pltpu.CompilerParams(vmem_limit_bytes=60 * 1024 * 1024)


def attend_own(me, assignment, lengths, queries, own, interpret=False):
    rows = queries.shape[0]
    part = jax.ShapeDtypeStruct((KV_HEADS, GROUP * rows, HEAD_DIM), jnp.float32)
    return pl.pallas_call(
        own_kernel,
        out_shape=(part, part),
        in_specs=[SMEM, SMEM, SMEM] + [ANY] * 5,
        out_specs=(ANY, ANY),
        scratch_shapes=[
            pltpu.VMEM((rows, 8 * rows), jnp.float32),
            pltpu.VMEM((KV_HEADS, rows, WIDTH), jnp.bfloat16),
            pltpu.VMEM((KV_HEADS, 4, 2, 2, rows, HEAD_DIM), jnp.bfloat16),
            pltpu.VMEM(part.shape, jnp.float32),
            pltpu.VMEM(part.shape, jnp.float32),
            pltpu.SemaphoreType.DMA((KV_HEADS,)),
            pltpu.SemaphoreType.DMA((4, KV_HEADS)),
            pltpu.SemaphoreType.DMA((KV_HEADS,)),
            pltpu.SemaphoreType.DMA((KV_HEADS,)),
        ],
        compiler_params=PARAMS,
        cost_estimate=LONG,
        interpret=interpret,
    )(me, assignment, lengths, queries, *own)


def attend_anchor(
    which, me, assignment, anchor, lengths, queries, kv, o, lse, out=None, interpret=False
):
    rows = queries.shape[0]
    extra = () if out is None else (out,)
    return pl.pallas_call(
        functools.partial(anchor_kernel, which),
        out_shape=jax.ShapeDtypeStruct(queries.shape, jnp.bfloat16),
        in_specs=[SMEM] * 4 + [ANY] * (4 + len(extra)),
        out_specs=ANY,
        input_output_aliases={8: 0} if extra else {},
        scratch_shapes=[
            pltpu.VMEM((8, 8 * rows - 256), jnp.float32),
            pltpu.VMEM((HALF, rows, WIDTH), jnp.bfloat16),
            pltpu.VMEM((HALF, 4, 2, 2, rows, HEAD_DIM), jnp.bfloat16),
            pltpu.VMEM((HALF,) + o.shape[1:], jnp.float32),
            pltpu.VMEM((HALF,) + o.shape[1:], jnp.float32),
            pltpu.VMEM((HALF, rows, WIDTH), jnp.bfloat16),
            pltpu.SemaphoreType.DMA((4, HALF)),
            pltpu.SemaphoreType.DMA((HALF,)),
        ],
        compiler_params=PARAMS,
        cost_estimate=COST,
        interpret=interpret,
    )(me, assignment, anchor, lengths, queries, kv, o, lse, *extra)


def pair_kernel(me, mine_ref, other_ref, pair_ref):
    zh = me[0] & 1
    pair_ref[zh] = mine_ref[...]
    pair_ref[1 - zh] = other_ref[...]


def make_pair(me, mine, other, interpret=False):
    return pl.pallas_call(
        pair_kernel,
        out_shape=jax.ShapeDtypeStruct((2,) + mine.shape, mine.dtype),
        in_specs=[SMEM, VMEM, VMEM],
        out_specs=VMEM,
        cost_estimate=LONG,
        interpret=interpret,
    )(me, mine, other)


def cut_kernel(k_ref, v_ref, piece_ref):
    for kind, ref in enumerate((k_ref, v_ref)):
        for g in range(KV_HEADS):
            piece_ref[g % HALF, kind, g // HALF] = ref[:, g * HEAD_DIM : (g + 1) * HEAD_DIM]


def cut(keys, values, interpret=False):
    return pl.pallas_call(
        cut_kernel,
        out_shape=jax.ShapeDtypeStruct((HALF, 2, 2, keys.shape[0], HEAD_DIM), keys.dtype),
        in_specs=[VMEM, VMEM],
        out_specs=VMEM,
        interpret=interpret,
    )(keys, values)


def to_all(a, axes, n):
    return exchange(jnp.broadcast_to(a[None], (n,) + a.shape), axes)


def swap(a, axis):
    return lax.ppermute(a, axis, [(0, 1), (1, 0)])


def exchange(a, axes):
    return lax.all_to_all(a, axes, split_axis=0, concat_axis=0, tiled=True)


def shift(a, axis, by):
    n = lax.axis_size(axis)
    return lax.ppermute(a, axis, [(i, (i + by) % n) for i in range(n)])


def run(me, queries, keys, values, assignment, anchor, lengths, interpret=False):
    ids = jnp.arange(assignment.shape[0], dtype=jnp.int32)
    anchor_shard = jnp.sum(jnp.where(assignment == anchor[0], ids, 0))
    pieces = cut(keys, values, interpret)
    got = exchange(pieces.reshape((16,) + pieces.shape[3:]), ("y", "core"))
    other = swap(pieces, "zh")
    source = (anchor_shard >> 3) * 2 + (anchor_shard & 1)
    part = lax.dynamic_index_in_dim(got, source, 0, keepdims=False)
    part = to_all(part, ("zl", "zh"), 8)
    part = part.reshape((4, 2) + part.shape[1:])
    part = lax.dynamic_index_in_dim(part, (anchor_shard >> 1) & 3, 0, keepdims=False)
    pair = make_pair(me, pieces, other, interpret)
    part, pair = lax.optimization_barrier((part, pair))
    own = [pair] + [shift(pair, "x", s) for s in range(1, 4)]
    part = to_all(part, "y", 8)
    mine = to_all(part, "x", 4)
    o, lse = attend_own(me, assignment, lengths, queries, own, interpret)
    mine, o, lse = lax.optimization_barrier((mine, o, lse))
    theirs = swap(mine, "core")
    out = attend_anchor(
        0, me, assignment, anchor, lengths, queries, mine, o, lse, None, interpret
    )
    return attend_anchor(
        1, me, assignment, anchor, lengths, queries, theirs, o, lse, out, interpret
    )


def shards(queries, keys, values, assignment, anchor, lengths):
    me = lax.axis_index(AXES).astype(jnp.int32).reshape(1)
    return run(me, queries, keys, values, assignment, anchor, lengths)


def solution(mesh):
    fine = Mesh(mesh.devices.reshape(SIZES), AXES)
    spec = P(AXES, None)
    return jax.shard_map(
        shards,
        mesh=fine,
        in_specs=(spec, spec, spec, P(), P(), P()),
        out_specs=spec,
        check_vma=False,
    )
```

time: 114 us -> 103 us (0.904)
  Pallas kernels: 39.8 us -> 24.7 us
  blocking collectives: 12.3 us -> 15.5 us
    pallas_call x3 -> x4, Pallas kernels: 29.5 us -> 15.5 us  [the longest x2 11.9 us: attend_anchor(): pl.pallas_call(functools.partial(anchor_kernel, which), out_shape=jax.Sha...]
    all_to_all x3, waiting for transfers between devices: 0.01 us -> 5.25 us  [exchange(): return lax.all_to_all(a, axes, split_axis=0, concat_axis=0, tiled=True)]
    all_to_all x1, blocking collectives: 12.3 us -> 15.5 us  [exchange(): return lax.all_to_all(a, axes, split_axis=0, concat_axis=0, tiled=True)]
    ppermute x3, waiting for transfers between devices: 3.08 us -> 0.01 us  [shift(): return lax.ppermute(a, axis, [(i, (i + by) % n) for i in range(n)])]
    ppermute x2, waiting for transfers between devices: 2.27 us -> 0.01 us  [swap(): return lax.ppermute(a, axis, [(0, 1), (1, 0)])]
  transfers between devices with their start and end apart: 8 -> 8, of which waited for: 3 -> 2; matrix products, arithmetic and copies ran while one was open for 3% -> 3% of each run, Pallas kernels for 24% -> 17%
where the time goes in v4:
time: 103 us; the launch traced here: 102 us
  starting transfers between devices  47.3 us (46%)
  Pallas kernels  24.7 us (24%)
  blocking collectives  15.5 us (15%)
  local copies, waits for them, and re-layouts  5.38 us (5%)
  waiting for transfers between devices  5.26 us (5%)
  between operations  2.71 us (3%)
  other arithmetic  1.35 us (1%)
    all_to_all x3, starting transfers between devices, exchange(): return lax.all_to_all(a, axes, split_axis=0, concat_axis=0, tiled=True)  21.2 us
    ppermute x2, starting transfers between devices, swap(): return lax.ppermute(a, axis, [(0, 1), (1, 0)])  15.5 us
    all_to_all x1, blocking collectives, exchange(): return lax.all_to_all(a, axes, split_axis=0, concat_axis=0, tiled=True)  15.5 us
    pallas_call x2, Pallas kernels, attend_anchor(): pl.pallas_call(functools.partial(anchor_kernel, which), out_shape=jax.Sha...  11.9 us
    ppermute x3, starting transfers between devices, shift(): return lax.ppermute(a, axis, [(i, (i + by) % n) for i in range(n)])  10.5 us
    pallas_call x1, Pallas kernels, attend_own(): pl.pallas_call(own_kernel, out_shape=(part, part), in_specs=[SMEM, SMEM,...  9.21 us
    all_to_all x3, waiting for transfers between devices, exchange(): return lax.all_to_all(a, axes, split_axis=0, concat_axis=0, tiled=True)  5.25 us
    unnamed x12, local copies, waits for them, and re-layouts  3.42 us
  transfers between devices with their start and end apart: 8, of which 2 were waited for; matrix products, arithmetic and copies ran while one was open for 3% of the time, Pallas kernels for 17%

profile of v4, /device:TPU:1, one launch (start us, length us, event | category | flops | bytes accessed | tf_op | source)
XLA Modules:
  0.0 102.2 jit_solution(14649317234349354739)
XLA Ops:
  0.0 1.7 %shard_map.64.mine_ref = bf16[4,2,2,64,128]{4,3,2,1,0:T(8,128)(2,1)} custom-call(bf16[64,1024]{1,0:T(8,128)(2,1)} %k_ref.1, bf16[64,1024]{1,0:T(8,128)(2,1)} %v_ref.1), custom_call_target="tpu_custom_call" | custom-call | tf_op jit(solution)/shard_map/pallas_call | solution.py:246
  1.7 10.2 %all-to-all-start = ((bf16[16,64,128]{2,1,0:T(8,128)(2,1)}), bf16[16,64,128]{2,1,0:T(8,128)(2,1)S(1)}, u32[]{:S(2)}, u32[]{:S(2)}) async-start(bf16[16,64,128]{2,1,0:T(8,128)(2,1)} %bitcast.9), calls=%async_computation | async-start | bytes 524288 | tf_op jit(solution)/shard_map/all_to_all | solution.py:264
  11.9 9.1 %collective-permute-start = (bf16[4,2,2,64,128]{4,3,2,1,0:T(8,128)(2,1)}, bf16[4,2,2,64,128]{4,3,2,1,0:T(8,128)(2,1)S(1)}, u32[]{:S(2)}, u32[]{:S(2)}) collective-permute-start(bf16[4,2,2,64,128]{4,3,2,1,0:T(8,128)(2,1)} %shard_map.64.mine_ref), channel_id=1, source_target_pairs={{0,1},{1,0},{2,3},{3,2},{4,5},{5,4},{6,7},{7,6},{8,9},{9,8},{10,11... | collective-permute-start | bytes 786440 | tf_op jit(solution)/shard_map/ppermute | solution.py:260
  21.6 1.4 %fusion = s32[]{:T(128)} fusion(s32[64]{0:T(128)} %assignment.5, s32[]{:T(128)} %bitcast.8), kind=kLoop, calls=%fused_computation.3 | loop fusion | flops 191 | bytes 264 | tf_op jit(solution)/shard_map/reduce_sum | solution.py:274
  24.9 0.0 all-to-all-done
  24.9 0.7 broadcast_in_dim.26
  25.6 7.5 %all-to-all-start.1 = ((bf16[8,64,128]{2,1,0:T(8,128)(2,1)}), bf16[8,64,128]{2,1,0:T(8,128)(2,1)S(1)}, u32[]{:S(2)}, u32[]{:S(2)}) async-start(bf16[8,64,128]{2,1,0:T(8,128)(2,1)} %broadcast_in_dim.26), calls=%async_computation.1 | async-start | bytes 262144 | tf_op jit(solution)/shard_map/all_to_all | solution.py:264
  33.0 0.0 collective-permute-done.other_ref
  33.1 0.0 copy-start.5
  33.1 0.7 copy-done.5
  33.8 1.9 %shard_map.65.refs_0_ = bf16[2,4,2,2,64,128]{5,4,3,2,1,0:T(8,128)(2,1)} custom-call(s32[1]{0:T(128)} %bitcast.me, bf16[4,2,2,64,128]{4,3,2,1,0:T(8,128)(2,1)} %shard_map.64.mine_ref, bf16[4,2,2,64,128]{4,3,2,1,0:T(8,128)(2,1)} %copy-done.5), custom_call_target="tpu_custom_call" | custom-call | flops 68719476736 | bytes 6291456 | tf_op jit(solution)/shard_map/pallas_call | solution.py:229
  35.6 4.8 %all-to-all-done.1 = bf16[8,64,128]{2,1,0:T(8,128)(2,1)S(1)} async-done(((bf16[8,64,128]{2,1,0:T(8,128)(2,1)}), bf16[8,64,128]{2,1,0:T(8,128)(2,1)S(1)}, u32[]{:S(2)}, u32[]{:S(2)}) %all-to-all-start.1) | async-done | bytes 131104 | tf_op jit(solution)/shard_map/all_to_all | solution.py:264
  40.5 3.1 %collective-permute-start.1 = (bf16[2,4,2,2,64,128]{5,4,3,2,1,0:T(8,128)(2,1)}, bf16[2,4,2,2,64,128]{5,4,3,2,1,0:T(8,128)(2,1)S(1)}, u32[]{:S(2)}, u32[]{:S(2)}) collective-permute-start(bf16[2,4,2,2,64,128]{5,4,3,2,1,0:T(8,128)(2,1)} %shard_map.65.refs_0_), channel_id=1, source_target_pairs={{0,2},{2,4},{4,6},{6,0},{1,3},{3,5},{5,7},{7,1},{8,10},{10,12},{12... | collective-permute-start | bytes 1572872 | tf_op jit(solution)/shard_map/ppermute | solution.py:269
  43.6 4.4 %collective-permute-start.2 = (bf16[2,4,2,2,64,128]{5,4,3,2,1,0:T(8,128)(2,1)}, bf16[2,4,2,2,64,128]{5,4,3,2,1,0:T(8,128)(2,1)S(1)}, u32[]{:S(2)}, u32[]{:S(2)}) collective-permute-start(bf16[2,4,2,2,64,128]{5,4,3,2,1,0:T(8,128)(2,1)} %shard_map.65.refs_0_), channel_id=1, source_target_pairs={{0,4},{2,6},{4,0},{6,2},{1,5},{3,7},{5,1},{7,3},{8,12},{10,14},{12... | collective-permute-start | bytes 1572872 | tf_op jit(solution)/shard_map/ppermute | solution.py:269
  47.9 3.1 %collective-permute-start.3 = (bf16[2,4,2,2,64,128]{5,4,3,2,1,0:T(8,128)(2,1)}, bf16[2,4,2,2,64,128]{5,4,3,2,1,0:T(8,128)(2,1)S(1)}, u32[]{:S(2)}, u32[]{:S(2)}) collective-permute-start(bf16[2,4,2,2,64,128]{5,4,3,2,1,0:T(8,128)(2,1)} %shard_map.65.refs_0_), channel_id=1, source_target_pairs={{0,6},{2,0},{4,2},{6,4},{1,7},{3,1},{5,3},{7,5},{8,14},{10,8},{12,... | collective-permute-start | bytes 1572872 | tf_op jit(solution)/shard_map/ppermute | solution.py:269
  51.1 15.5 %all_to_all.20 = bf16[8,2,64,128]{3,2,1,0:T(8,128)(2,1)S(1)} all-to-all(bf16[8,2,64,128]{3,2,1,0:T(8,128)(2,1)S(1)} %broadcast_in_dim.27), channel_id=1, replica_groups=mesh['y'=8,'zl'=4,'core'=2,'x'=4,'zh'=2] {'y'}, dimensions={0} | all-to-all | bytes 524288 | tf_op jit(solution)/shard_map/all_to_all | solution.py:264
  66.6 1.2 %broadcast_in_dim.28 = bf16[4,8,2,64,128]{4,3,2,1,0:T(8,128)(2,1)} broadcast(bf16[8,2,64,128]{3,2,1,0:T(8,128)(2,1)S(1)} %all_to_all.20), dimensions={1,2,3,4} | broadcast | bytes 1310720 | tf_op jit(solution)/shard_map/broadcast_in_dim | solution.py:256
  67.8 3.5 %all-to-all-start.3 = ((bf16[4,8,2,64,128]{4,3,2,1,0:T(8,128)(2,1)}), bf16[4,8,2,64,128]{4,3,2,1,0:T(8,128)(2,1)S(1)}, u32[]{:S(2)}, u32[]{:S(2)}) async-start(bf16[4,8,2,64,128]{4,3,2,1,0:T(8,128)(2,1)} %broadcast_in_dim.28), calls=%async_computation.3 | async-start | bytes 2097152 | tf_op jit(solution)/shard_map/all_to_all | solution.py:264
  71.3 0.0 collective-permute-done.1.refs_1_
  71.3 0.0 copy-start.2
  71.4 0.0 collective-permute-done.2.refs_2_
  71.4 0.0 copy-start.3
  71.4 0.0 collective-permute-done.3.refs_3_
  71.4 0.8 copy-done.2
  72.1 0.2 copy-done.3
  72.3 0.0 copy-start.4
  72.3 0.8 copy-done.4
  73.1 9.2 %shard_map.66 = (f32[8,512,128]{2,1,0:T(8,128)}, f32[8,512,128]{2,1,0:T(8,128)}) custom-call(s32[1]{0:T(128)} %bitcast.me, s32[64]{0:T(128)} %assignment.5, s32[64]{0:T(128)} %lengths.5, bf16[64,8192]{1,0:T(8,128)(2,1)} %q_hbm.5, bf16[2,4,2,2,64,128]{5,4,3,2,1,0:T(8,128)(2,1)} %shard_map.65.refs_0_, bf16[2,4,2,2,64,128]{5,4,3,2,1,0:T(8,128)(2,1)} %copy-done.2, ...), custom_call_target="tpu_custom_call" | custom-call | flops 68719476736 | bytes 6291456 | tf_op jit(solution)/shard_map/pallas_call | solution.py:173
  82.4 0.4 all-to-all-done.3.kv_hbm
  82.8 0.0 copy-start.1
  82.8 6.5 %collective-permute-start.4 = (bf16[4,8,2,64,128]{4,3,2,1,0:T(8,128)(2,1)S(1)}, bf16[4,8,2,64,128]{4,3,2,1,0:T(8,128)(2,1)S(1)}, u32[]{:S(2)}, u32[]{:S(2)}) collective-permute-start(bf16[4,8,2,64,128]{4,3,2,1,0:T(8,128)(2,1)S(1)} %all-to-all-done.3.kv_hbm), channel_id=1, source_target_pairs={{0,8},{8,0},{1,9},{9,1},{2,10},{10,2},{3,11},{11,3},{4,12},{12,4},... | collective-permute-start | bytes 3145736 | tf_op jit(solution)/shard_map/ppermute | solution.py:260
  89.3 0.0 copy-done.1
  89.3 6.0 %shard_map.67.refs_0_ = bf16[64,8192]{1,0:T(8,128)(2,1)} custom-call(s32[1]{0:T(128)} %bitcast.me, s32[64]{0:T(128)} %assignment.5, s32[1]{0:T(128)} %copy.9.anchor, s32[64]{0:T(128)} %lengths.5, bf16[64,8192]{1,0:T(8,128)(2,1)} %q_hbm.5, bf16[4,8,2,64,128]{4,3,2,1,0:T(8,128)(2,1)} %copy-done.1, f32[8,512,128]{2,1,0:T(8,128)} %get-tuple-element.17.o_hbm, ...), custom_call_target="tpu_custom_call" | custom-call | flops 2147483648 | bytes 6291456 | tf_op jit(solution)/shard_map/pallas_call | solution.py:200
  95.2 0.0 collective-permute-done.4.kv_hbm
  95.3 0.0 copy-start
  95.3 1.0 copy-done
  96.2 6.0 %shard_map.68 = bf16[64,8192]{1,0:T(8,128)(2,1)} custom-call(s32[1]{0:T(128)} %bitcast.me, s32[64]{0:T(128)} %assignment.5, s32[1]{0:T(128)} %copy.9.anchor, s32[64]{0:T(128)} %lengths.5, bf16[64,8192]{1,0:T(8,128)(2,1)} %q_hbm.5, bf16[4,8,2,64,128]{4,3,2,1,0:T(8,128)(2,1)} %copy-done, ...), custom_call_target="tpu_custom_call", output_to_operand_aliasing={{}: (8, {})} | custom-call | flops 2147483648 | bytes 6291456 | tf_op jit(solution)/shard_map/pallas_call | solution.py:200
  (3 shorter events, 0.1 us)
Async XLA Ops:
  1.7 23.2 %all-to-all-start = ((bf16[16,64,128]{2,1,0:T(8,128)(2,1)}), bf16[16,64,128]{2,1,0:T(8,128)(2,1)S(1)}, u32[]{:S(2)}, u32[]{:S(2)}) async-start(bf16[16,64,128]{2,1,0:T(8,128)(2,1)} %bitcast.9), calls=%async_computation | async-start | bytes 524288 | tf_op jit(solution)/shard_map/all_to_all | solution.py:264
  11.9 21.1 %collective-permute-start = (bf16[4,2,2,64,128]{4,3,2,1,0:T(8,128)(2,1)}, bf16[4,2,2,64,128]{4,3,2,1,0:T(8,128)(2,1)S(1)}, u32[]{:S(2)}, u32[]{:S(2)}) collective-permute-start(bf16[4,2,2,64,128]{4,3,2,1,0:T(8,128)(2,1)} %shard_map.64.mine_ref), channel_id=1, source_target_pairs={{0,1},{1,0},{2,3},{3,2},{4,5},{5,4},{6,7},{7,6},{8,9},{9,8},{10,11... | collective-permute-start | bytes 786440 | tf_op jit(solution)/shard_map/ppermute | solution.py:260
  25.6 14.9 %all-to-all-start.1 = ((bf16[8,64,128]{2,1,0:T(8,128)(2,1)}), bf16[8,64,128]{2,1,0:T(8,128)(2,1)S(1)}, u32[]{:S(2)}, u32[]{:S(2)}) async-start(bf16[8,64,128]{2,1,0:T(8,128)(2,1)} %broadcast_in_dim.26), calls=%async_computation.1 | async-start | bytes 262144 | tf_op jit(solution)/shard_map/all_to_all | solution.py:264
  33.1 0.7 copy-start.5
  40.5 30.9 %collective-permute-start.1 = (bf16[2,4,2,2,64,128]{5,4,3,2,1,0:T(8,128)(2,1)}, bf16[2,4,2,2,64,128]{5,4,3,2,1,0:T(8,128)(2,1)S(1)}, u32[]{:S(2)}, u32[]{:S(2)}) collective-permute-start(bf16[2,4,2,2,64,128]{5,4,3,2,1,0:T(8,128)(2,1)} %shard_map.65.refs_0_), channel_id=1, source_target_pairs={{0,2},{2,4},{4,6},{6,0},{1,3},{3,5},{5,7},{7,1},{8,10},{10,12},{12... | collective-permute-start | bytes 1572872 | tf_op jit(solution)/shard_map/ppermute | solution.py:269
  43.6 27.8 %collective-permute-start.2 = (bf16[2,4,2,2,64,128]{5,4,3,2,1,0:T(8,128)(2,1)}, bf16[2,4,2,2,64,128]{5,4,3,2,1,0:T(8,128)(2,1)S(1)}, u32[]{:S(2)}, u32[]{:S(2)}) collective-permute-start(bf16[2,4,2,2,64,128]{5,4,3,2,1,0:T(8,128)(2,1)} %shard_map.65.refs_0_), channel_id=1, source_target_pairs={{0,4},{2,6},{4,0},{6,2},{1,5},{3,7},{5,1},{7,3},{8,12},{10,14},{12... | collective-permute-start | bytes 1572872 | tf_op jit(solution)/shard_map/ppermute | solution.py:269
  47.9 23.4 %collective-permute-start.3 = (bf16[2,4,2,2,64,128]{5,4,3,2,1,0:T(8,128)(2,1)}, bf16[2,4,2,2,64,128]{5,4,3,2,1,0:T(8,128)(2,1)S(1)}, u32[]{:S(2)}, u32[]{:S(2)}) collective-permute-start(bf16[2,4,2,2,64,128]{5,4,3,2,1,0:T(8,128)(2,1)} %shard_map.65.refs_0_), channel_id=1, source_target_pairs={{0,6},{2,0},{4,2},{6,4},{1,7},{3,1},{5,3},{7,5},{8,14},{10,8},{12,... | collective-permute-start | bytes 1572872 | tf_op jit(solution)/shard_map/ppermute | solution.py:269
  67.8 15.0 %all-to-all-start.3 = ((bf16[4,8,2,64,128]{4,3,2,1,0:T(8,128)(2,1)}), bf16[4,8,2,64,128]{4,3,2,1,0:T(8,128)(2,1)S(1)}, u32[]{:S(2)}, u32[]{:S(2)}) async-start(bf16[4,8,2,64,128]{4,3,2,1,0:T(8,128)(2,1)} %broadcast_in_dim.28), calls=%async_computation.3 | async-start | bytes 2097152 | tf_op jit(solution)/shard_map/all_to_all | solution.py:264
  71.3 0.8 copy-start.2
  71.4 1.0 copy-start.3
  72.3 0.8 copy-start.4
  82.8 6.5 %copy-start.1 = (bf16[4,8,2,64,128]{4,3,2,1,0:T(8,128)(2,1)}, bf16[4,8,2,64,128]{4,3,2,1,0:T(8,128)(2,1)S(1)}, u32[]{:S(2)}) copy-start(bf16[4,8,2,64,128]{4,3,2,1,0:T(8,128)(2,1)S(1)} %all-to-all-done.3.kv_hbm) | copy-start | bytes 3145732
  82.8 12.5 %collective-permute-start.4 = (bf16[4,8,2,64,128]{4,3,2,1,0:T(8,128)(2,1)S(1)}, bf16[4,8,2,64,128]{4,3,2,1,0:T(8,128)(2,1)S(1)}, u32[]{:S(2)}, u32[]{:S(2)}) collective-permute-start(bf16[4,8,2,64,128]{4,3,2,1,0:T(8,128)(2,1)S(1)} %all-to-all-done.3.kv_hbm), channel_id=1, source_target_pairs={{0,8},{8,0},{1,9},{9,1},{2,10},{10,2},{3,11},{11,3},{4,12},{12,4},... | collective-permute-start | bytes 3145736 | tf_op jit(solution)/shard_map/ppermute | solution.py:260
  95.3 1.0 copy-start

commit v5 on v4

--- a/solution.py
+++ b/solution.py
@@ -24,21 +24,40 @@
     return pl.ds(pl.multiple_of(g * WIDTH, WIDTH), WIDTH)
 
 
-def attend_set(q_ref, c, k, v, bias):
-    rows = q_ref.shape[0]
+def scores(q_ref, c, k):
     first = c * CHUNK * HEAD_DIM
     q = jnp.concatenate(
         [q_ref[:, first + i * HEAD_DIM : first + (i + 1) * HEAD_DIM] for i in range(CHUNK)], axis=0
     )
-    s = lax.dot_general(q, k, (((1,), (1,)), ((), ())), preferred_element_type=jnp.float32)
+    return lax.dot_general(q, k, (((1,), (1,)), ((), ())), preferred_element_type=jnp.float32)
+
+
+def softmax(s, bias):
     free = s.shape[1] - bias.shape[1]
+    rows = s.shape[0] // CHUNK
     tail = (s[:, free:].reshape(CHUNK, rows, -1) + bias[None]).reshape(CHUNK * rows, -1)
     s = jnp.concatenate([s[:, :free], tail], axis=1) if free else tail
     m = jnp.max(s, axis=1, keepdims=True)
     e = jnp.exp2((s - m) * SCALE)
-    l = jnp.sum(e, axis=1, keepdims=True)
-    o = jnp.dot(e.astype(jnp.bfloat16), v, preferred_element_type=jnp.float32)
-    return m, l, o
+    return m, jnp.sum(e, axis=1, keepdims=True), e.astype(jnp.bfloat16)
+
+
+def attend_heads(q_buf, heads, load, bias, finish):
+    work = [(g, c) for g in heads for c in range(GROUP // CHUNK)]
+    found, weighed, values = {}, {}, {}
+    for t in range(len(work) + 2):
+        if t < len(work):
+            g, c = work[t]
+            if c == 0:
+                k, v = load(g)
+            values[t] = v
+            found[t] = scores(q_buf.at[g], c, k)
+        if t >= 2:
+            m, l, e = weighed.pop(t - 2)
+            o = jnp.dot(e, values.pop(t - 2), preferred_element_type=jnp.float32)
+            finish(*work[t - 2], m, l, o)
+        if 1 <= t <= len(work):
+            weighed[t - 1] = softmax(found.pop(t - 1), bias)
 
 
 def query_copy(q_hbm, q_buf, sem, g):
@@ -51,18 +70,10 @@
             copy.start()
 
     if isinstance(g, int):
-        start()
+        if g < count:
+            start()
     else:
         pl.when(g < count)(start)
-
-
-def two_at_a_time(body, count):
-    def step(i, carry):
-        body(2 * i)
-        body(2 * i + 1)
-        return carry
-
-    lax.fori_loop(0, count // 2, step, 0)
 
 
 def own_kernel(me, assignment, lengths, q_hbm, *refs):
@@ -90,21 +101,25 @@
             pltpu.make_async_copy(lse_buf.at[g], lse_hbm.at[g], lse_sem.at[g]),
         )
 
-    def one_group(g):
+    def load(g):
         start_ahead(group_copies, g + 2)
         for copy in group_copies(g):
             copy.wait()
-        k = kv_buf[g, :, :, 0].reshape(8 * rows, HEAD_DIM)
-        v = kv_buf[g, :, :, 1].reshape(8 * rows, HEAD_DIM)
-        for c in range(GROUP // CHUNK):
-            m, l, o = attend_set(q_buf.at[g], c, k, v, bias_ref[...])
-            at = pl.ds(c * CHUNK * rows, CHUNK * rows)
-            o_buf[g, at] = o * (1.0 / l)
-            lse_buf[g, at] = jnp.broadcast_to(m * SCALE + jnp.log2(l), o.shape)
-        for copy in result_copies(g):
-            copy.start()
-
-    two_at_a_time(one_group, KV_HEADS)
+        return [kv_buf[g, :, :, kind].reshape(8 * rows, HEAD_DIM) for kind in range(2)]
+
+    def finish(g, c, m, l, o):
+        at = pl.ds(c * CHUNK * rows, CHUNK * rows)
+        o_buf[g, at] = o * (1.0 / l)
+        lse_buf[g, at] = jnp.broadcast_to(m * SCALE + jnp.log2(l), o.shape)
+        if c == GROUP // CHUNK - 1:
+            for copy in result_copies(g):
+                copy.start()
+
+    def step(i, carry):
+        attend_heads(q_buf, [4 * i + j for j in range(4)], load, bias_ref[...], finish)
+        return carry
+
+    lax.fori_loop(0, KV_HEADS // 4, step, 0)
     for g in range(KV_HEADS):
         for copy in result_copies(g):
             copy.wait()
@@ -136,25 +151,25 @@
     col = lax.broadcasted_iota(jnp.int32, bias_ref.shape, 1) + 256
     bias_ref[...] = jnp.where(col < anc_len, 0.0, NEG)
 
-    def one_group(i):
+    def load(i):
         start_ahead(group_copies, i + 2, HALF)
         for copy in group_copies(i):
             copy.wait()
-        k = kv_buf[i, :, 0].reshape(8 * rows, HEAD_DIM)
-        v = kv_buf[i, :, 1].reshape(8 * rows, HEAD_DIM)
-        for c in range(GROUP // CHUNK):
-            m1, l1, o1 = attend_set(q_buf.at[i], c, k, v, bias_ref[0:1, :])
-            at = pl.ds(c * CHUNK * rows, CHUNK * rows)
-            lse1 = jnp.where(is_anchor, NEG, m1 * SCALE + jnp.log2(l1))
-            share = 1.0 / (1.0 + jnp.exp2(lse_buf[i, at] - lse1))
-            o = (1.0 - share) * o_buf[i, at] + (share * (1.0 / l1)) * o1
-            o = o.astype(out_buf.dtype)
-            for j in range(CHUNK):
-                to = (c * CHUNK + j) * HEAD_DIM
-                out_buf[i, :, to : to + HEAD_DIM] = o[j * rows : (j + 1) * rows]
-        out_copy(i).start()
-
-    two_at_a_time(one_group, HALF)
+        return [kv_buf[i, :, kind].reshape(8 * rows, HEAD_DIM) for kind in range(2)]
+
+    def finish(i, c, m1, l1, o1):
+        at = pl.ds(c * CHUNK * rows, CHUNK * rows)
+        lse1 = jnp.where(is_anchor, NEG, m1 * SCALE + jnp.log2(l1))
+        share = 1.0 / (1.0 + jnp.exp2(lse_buf[i, at] - lse1))
+        o = (1.0 - share) * o_buf[i, at] + (share * (1.0 / l1)) * o1
+        o = o.astype(out_buf.dtype)
+        for j in range(CHUNK):
+            to = (c * CHUNK + j) * HEAD_DIM
+            out_buf[i, :, to : to + HEAD_DIM] = o[j * rows : (j + 1) * rows]
+        if c == GROUP // CHUNK - 1:
+            out_copy(i).start()
+
+    attend_heads(q_buf, list(range(HALF)), load, bias_ref[0:1, :], finish)
     for i in range(HALF):
         out_copy(i).wait()
 

time: 103 us -> 101 us (0.981)
  Pallas kernels: 24.7 us -> 21.5 us
  waiting for transfers between devices: 5.26 us -> 6.65 us
    pallas_call x2, Pallas kernels: 11.9 us -> 10.1 us  [attend_anchor(): pl.pallas_call(functools.partial(anchor_kernel, which), out_shape=jax.Sha...]
    all_to_all x3, waiting for transfers between devices: 5.25 us -> 6.63 us  [exchange(): return lax.all_to_all(a, axes, split_axis=0, concat_axis=0, tiled=True)]
    pallas_call x1, Pallas kernels: 9.21 us -> 7.83 us  [attend_own(): pl.pallas_call(own_kernel, out_shape=(part, part), in_specs=[SMEM, SMEM,...]
  transfers between devices with their start and end apart: 8 -> 8, of which waited for: 2 -> 2; matrix products, arithmetic and copies ran while one was open for 3% -> 3% of each run, Pallas kernels for 17% -> 15%
where the time goes in v5:
time: 101 us; the launch traced here: 100 us
  starting transfers between devices  47.3 us (47%)
  Pallas kernels  21.5 us (21%)
  blocking collectives  15.5 us (15%)
  waiting for transfers between devices  6.65 us (7%)
  local copies, waits for them, and re-layouts  5.38 us (5%)
  between operations  2.71 us (3%)
  other arithmetic  1.35 us (1%)
    all_to_all x3, starting transfers between devices, exchange(): return lax.all_to_all(a, axes, split_axis=0, concat_axis=0, tiled=True)  21.2 us
    ppermute x2, starting transfers between devices, swap(): return lax.ppermute(a, axis, [(0, 1), (1, 0)])  15.5 us
    all_to_all x1, blocking collectives, exchange(): return lax.all_to_all(a, axes, split_axis=0, concat_axis=0, tiled=True)  15.5 us
    ppermute x3, starting transfers between devices, shift(): return lax.ppermute(a, axis, [(i, (i + by) % n) for i in range(n)])  10.5 us
    pallas_call x2, Pallas kernels, attend_anchor(): pl.pallas_call(functools.partial(anchor_kernel, which), out_shape=jax.Sha...  10.1 us
    pallas_call x1, Pallas kernels, attend_own(): pl.pallas_call(own_kernel, out_shape=(part, part), in_specs=[SMEM, SMEM,...  7.83 us
    all_to_all x3, waiting for transfers between devices, exchange(): return lax.all_to_all(a, axes, split_axis=0, concat_axis=0, tiled=True)  6.63 us
    unnamed x12, local copies, waits for them, and re-layouts  3.42 us
  transfers between devices with their start and end apart: 8, of which 2 were waited for; matrix products, arithmetic and copies ran while one was open for 3% of the time, Pallas kernels for 15%

profile of v5, /device:TPU:1, one launch (start us, length us, event | category | flops | bytes accessed | tf_op | source)
XLA Modules:
  0.0 100.4 jit_solution(468308093663081125)
XLA Ops:
  0.0 1.7 %shard_map.64.mine_ref = bf16[4,2,2,64,128]{4,3,2,1,0:T(8,128)(2,1)} custom-call(bf16[64,1024]{1,0:T(8,128)(2,1)} %k_ref.1, bf16[64,1024]{1,0:T(8,128)(2,1)} %v_ref.1), custom_call_target="tpu_custom_call" | custom-call | tf_op jit(solution)/shard_map/pallas_call | solution.py:261
  1.7 10.2 %all-to-all-start = ((bf16[16,64,128]{2,1,0:T(8,128)(2,1)}), bf16[16,64,128]{2,1,0:T(8,128)(2,1)S(1)}, u32[]{:S(2)}, u32[]{:S(2)}) async-start(bf16[16,64,128]{2,1,0:T(8,128)(2,1)} %bitcast.9), calls=%async_computation | async-start | bytes 524288 | tf_op jit(solution)/shard_map/all_to_all | solution.py:279
  11.9 9.1 %collective-permute-start = (bf16[4,2,2,64,128]{4,3,2,1,0:T(8,128)(2,1)}, bf16[4,2,2,64,128]{4,3,2,1,0:T(8,128)(2,1)S(1)}, u32[]{:S(2)}, u32[]{:S(2)}) collective-permute-start(bf16[4,2,2,64,128]{4,3,2,1,0:T(8,128)(2,1)} %shard_map.64.mine_ref), channel_id=1, source_target_pairs={{0,1},{1,0},{2,3},{3,2},{4,5},{5,4},{6,7},{7,6},{8,9},{9,8},{10,11... | collective-permute-start | bytes 786440 | tf_op jit(solution)/shard_map/ppermute | solution.py:275
  21.6 1.4 %fusion = s32[]{:T(128)} fusion(s32[64]{0:T(128)} %assignment.5, s32[]{:T(128)} %bitcast.8), kind=kLoop, calls=%fused_computation.3 | loop fusion | flops 191 | bytes 264 | tf_op jit(solution)/shard_map/reduce_sum | solution.py:289
  24.9 0.0 all-to-all-done
  24.9 0.7 broadcast_in_dim.26
  25.6 7.5 %all-to-all-start.1 = ((bf16[8,64,128]{2,1,0:T(8,128)(2,1)}), bf16[8,64,128]{2,1,0:T(8,128)(2,1)S(1)}, u32[]{:S(2)}, u32[]{:S(2)}) async-start(bf16[8,64,128]{2,1,0:T(8,128)(2,1)} %broadcast_in_dim.26), calls=%async_computation.1 | async-start | bytes 262144 | tf_op jit(solution)/shard_map/all_to_all | solution.py:279
  33.0 0.0 collective-permute-done.other_ref
  33.1 0.0 copy-start.5
  33.1 0.7 copy-done.5
  33.8 1.9 %shard_map.65.refs_0_ = bf16[2,4,2,2,64,128]{5,4,3,2,1,0:T(8,128)(2,1)} custom-call(s32[1]{0:T(128)} %bitcast.me, bf16[4,2,2,64,128]{4,3,2,1,0:T(8,128)(2,1)} %shard_map.64.mine_ref, bf16[4,2,2,64,128]{4,3,2,1,0:T(8,128)(2,1)} %copy-done.5), custom_call_target="tpu_custom_call" | custom-call | flops 68719476736 | bytes 6291456 | tf_op jit(solution)/shard_map/pallas_call | solution.py:244
  35.6 4.8 %all-to-all-done.1 = bf16[8,64,128]{2,1,0:T(8,128)(2,1)S(1)} async-done(((bf16[8,64,128]{2,1,0:T(8,128)(2,1)}), bf16[8,64,128]{2,1,0:T(8,128)(2,1)S(1)}, u32[]{:S(2)}, u32[]{:S(2)}) %all-to-all-start.1) | async-done | bytes 131104 | tf_op jit(solution)/shard_map/all_to_all | solution.py:279
  40.5 3.1 %collective-permute-start.1 = (bf16[2,4,2,2,64,128]{5,4,3,2,1,0:T(8,128)(2,1)}, bf16[2,4,2,2,64,128]{5,4,3,2,1,0:T(8,128)(2,1)S(1)}, u32[]{:S(2)}, u32[]{:S(2)}) collective-permute-start(bf16[2,4,2,2,64,128]{5,4,3,2,1,0:T(8,128)(2,1)} %shard_map.65.refs_0_), channel_id=1, source_target_pairs={{0,2},{2,4},{4,6},{6,0},{1,3},{3,5},{5,7},{7,1},{8,10},{10,12},{12... | collective-permute-start | bytes 1572872 | tf_op jit(solution)/shard_map/ppermute | solution.py:284
  43.6 4.4 %collective-permute-start.2 = (bf16[2,4,2,2,64,128]{5,4,3,2,1,0:T(8,128)(2,1)}, bf16[2,4,2,2,64,128]{5,4,3,2,1,0:T(8,128)(2,1)S(1)}, u32[]{:S(2)}, u32[]{:S(2)}) collective-permute-start(bf16[2,4,2,2,64,128]{5,4,3,2,1,0:T(8,128)(2,1)} %shard_map.65.refs_0_), channel_id=1, source_target_pairs={{0,4},{2,6},{4,0},{6,2},{1,5},{3,7},{5,1},{7,3},{8,12},{10,14},{12... | collective-permute-start | bytes 1572872 | tf_op jit(solution)/shard_map/ppermute | solution.py:284
  47.9 3.1 %collective-permute-start.3 = (bf16[2,4,2,2,64,128]{5,4,3,2,1,0:T(8,128)(2,1)}, bf16[2,4,2,2,64,128]{5,4,3,2,1,0:T(8,128)(2,1)S(1)}, u32[]{:S(2)}, u32[]{:S(2)}) collective-permute-start(bf16[2,4,2,2,64,128]{5,4,3,2,1,0:T(8,128)(2,1)} %shard_map.65.refs_0_), channel_id=1, source_target_pairs={{0,6},{2,0},{4,2},{6,4},{1,7},{3,1},{5,3},{7,5},{8,14},{10,8},{12,... | collective-permute-start | bytes 1572872 | tf_op jit(solution)/shard_map/ppermute | solution.py:284
  51.1 15.5 %all_to_all.20 = bf16[8,2,64,128]{3,2,1,0:T(8,128)(2,1)S(1)} all-to-all(bf16[8,2,64,128]{3,2,1,0:T(8,128)(2,1)S(1)} %broadcast_in_dim.27), channel_id=1, replica_groups=mesh['y'=8,'zl'=4,'core'=2,'x'=4,'zh'=2] {'y'}, dimensions={0} | all-to-all | bytes 524288 | tf_op jit(solution)/shard_map/all_to_all | solution.py:279
  66.6 1.2 %broadcast_in_dim.28 = bf16[4,8,2,64,128]{4,3,2,1,0:T(8,128)(2,1)} broadcast(bf16[8,2,64,128]{3,2,1,0:T(8,128)(2,1)S(1)} %all_to_all.20), dimensions={1,2,3,4} | broadcast | bytes 1310720 | tf_op jit(solution)/shard_map/broadcast_in_dim | solution.py:271
  67.8 3.5 %all-to-all-start.3 = ((bf16[4,8,2,64,128]{4,3,2,1,0:T(8,128)(2,1)}), bf16[4,8,2,64,128]{4,3,2,1,0:T(8,128)(2,1)S(1)}, u32[]{:S(2)}, u32[]{:S(2)}) async-start(bf16[4,8,2,64,128]{4,3,2,1,0:T(8,128)(2,1)} %broadcast_in_dim.28), calls=%async_computation.3 | async-start | bytes 2097152 | tf_op jit(solution)/shard_map/all_to_all | solution.py:279
  71.3 0.0 collective-permute-done.1.refs_1_
  71.3 0.0 copy-start.2
  71.4 0.0 collective-permute-done.2.refs_2_
  71.4 0.0 copy-start.3
  71.4 0.0 collective-permute-done.3.refs_3_
  71.4 0.8 copy-done.2
  72.1 0.2 copy-done.3
  72.3 0.0 copy-start.4
  72.3 0.8 copy-done.4
  73.1 7.8 %shard_map.66 = (f32[8,512,128]{2,1,0:T(8,128)}, f32[8,512,128]{2,1,0:T(8,128)}) custom-call(s32[1]{0:T(128)} %bitcast.me, s32[64]{0:T(128)} %assignment.5, s32[64]{0:T(128)} %lengths.5, bf16[64,8192]{1,0:T(8,128)(2,1)} %q_hbm.5, bf16[2,4,2,2,64,128]{5,4,3,2,1,0:T(8,128)(2,1)} %shard_map.65.refs_0_, bf16[2,4,2,2,64,128]{5,4,3,2,1,0:T(8,128)(2,1)} %copy-done.2, ...), custom_call_target="tpu_custom_call" | custom-call | flops 68719476736 | bytes 6291456 | tf_op jit(solution)/shard_map/pallas_call | solution.py:188
  81.0 1.8 %all-to-all-done.3.kv_hbm = bf16[4,8,2,64,128]{4,3,2,1,0:T(8,128)(2,1)S(1)} async-done(((bf16[4,8,2,64,128]{4,3,2,1,0:T(8,128)(2,1)}), bf16[4,8,2,64,128]{4,3,2,1,0:T(8,128)(2,1)S(1)}, u32[]{:S(2)}, u32[]{:S(2)}) %all-to-all-start.3) | async-done | bytes 1048608 | tf_op jit(solution)/shard_map/all_to_all | solution.py:279
  82.8 0.0 copy-start.1
  82.8 6.5 %collective-permute-start.4 = (bf16[4,8,2,64,128]{4,3,2,1,0:T(8,128)(2,1)S(1)}, bf16[4,8,2,64,128]{4,3,2,1,0:T(8,128)(2,1)S(1)}, u32[]{:S(2)}, u32[]{:S(2)}) collective-permute-start(bf16[4,8,2,64,128]{4,3,2,1,0:T(8,128)(2,1)S(1)} %all-to-all-done.3.kv_hbm), channel_id=1, source_target_pairs={{0,8},{8,0},{1,9},{9,1},{2,10},{10,2},{3,11},{11,3},{4,12},{12,4},... | collective-permute-start | bytes 3145736 | tf_op jit(solution)/shard_map/ppermute | solution.py:275
  89.3 0.0 copy-done.1
  89.3 5.1 %shard_map.67.refs_0_ = bf16[64,8192]{1,0:T(8,128)(2,1)} custom-call(s32[1]{0:T(128)} %bitcast.me, s32[64]{0:T(128)} %assignment.5, s32[1]{0:T(128)} %copy.9.anchor, s32[64]{0:T(128)} %lengths.5, bf16[64,8192]{1,0:T(8,128)(2,1)} %q_hbm.5, bf16[4,8,2,64,128]{4,3,2,1,0:T(8,128)(2,1)} %copy-done.1, f32[8,512,128]{2,1,0:T(8,128)} %get-tuple-element.17.o_hbm, ...), custom_call_target="tpu_custom_call" | custom-call | flops 2147483648 | bytes 6291456 | tf_op jit(solution)/shard_map/pallas_call | solution.py:215
  94.3 0.0 collective-permute-done.4.kv_hbm
  94.3 0.0 copy-start
  94.4 1.0 copy-done
  95.3 5.1 %shard_map.68 = bf16[64,8192]{1,0:T(8,128)(2,1)} custom-call(s32[1]{0:T(128)} %bitcast.me, s32[64]{0:T(128)} %assignment.5, s32[1]{0:T(128)} %copy.9.anchor, s32[64]{0:T(128)} %lengths.5, bf16[64,8192]{1,0:T(8,128)(2,1)} %q_hbm.5, bf16[4,8,2,64,128]{4,3,2,1,0:T(8,128)(2,1)} %copy-done, ...), custom_call_target="tpu_custom_call", output_to_operand_aliasing={{}: (8, {})} | custom-call | flops 2147483648 | bytes 6291456 | tf_op jit(solution)/shard_map/pallas_call | solution.py:215
  (3 shorter events, 0.1 us)
Async XLA Ops:
  1.7 23.2 %all-to-all-start = ((bf16[16,64,128]{2,1,0:T(8,128)(2,1)}), bf16[16,64,128]{2,1,0:T(8,128)(2,1)S(1)}, u32[]{:S(2)}, u32[]{:S(2)}) async-start(bf16[16,64,128]{2,1,0:T(8,128)(2,1)} %bitcast.9), calls=%async_computation | async-start | bytes 524288 | tf_op jit(solution)/shard_map/all_to_all | solution.py:279
  11.9 21.1 %collective-permute-start = (bf16[4,2,2,64,128]{4,3,2,1,0:T(8,128)(2,1)}, bf16[4,2,2,64,128]{4,3,2,1,0:T(8,128)(2,1)S(1)}, u32[]{:S(2)}, u32[]{:S(2)}) collective-permute-start(bf16[4,2,2,64,128]{4,3,2,1,0:T(8,128)(2,1)} %shard_map.64.mine_ref), channel_id=1, source_target_pairs={{0,1},{1,0},{2,3},{3,2},{4,5},{5,4},{6,7},{7,6},{8,9},{9,8},{10,11... | collective-permute-start | bytes 786440 | tf_op jit(solution)/shard_map/ppermute | solution.py:275
  25.6 14.9 %all-to-all-start.1 = ((bf16[8,64,128]{2,1,0:T(8,128)(2,1)}), bf16[8,64,128]{2,1,0:T(8,128)(2,1)S(1)}, u32[]{:S(2)}, u32[]{:S(2)}) async-start(bf16[8,64,128]{2,1,0:T(8,128)(2,1)} %broadcast_in_dim.26), calls=%async_computation.1 | async-start | bytes 262144 | tf_op jit(solution)/shard_map/all_to_all | solution.py:279
  33.1 0.7 copy-start.5
  40.5 30.9 %collective-permute-start.1 = (bf16[2,4,2,2,64,128]{5,4,3,2,1,0:T(8,128)(2,1)}, bf16[2,4,2,2,64,128]{5,4,3,2,1,0:T(8,128)(2,1)S(1)}, u32[]{:S(2)}, u32[]{:S(2)}) collective-permute-start(bf16[2,4,2,2,64,128]{5,4,3,2,1,0:T(8,128)(2,1)} %shard_map.65.refs_0_), channel_id=1, source_target_pairs={{0,2},{2,4},{4,6},{6,0},{1,3},{3,5},{5,7},{7,1},{8,10},{10,12},{12... | collective-permute-start | bytes 1572872 | tf_op jit(solution)/shard_map/ppermute | solution.py:284
  43.6 27.8 %collective-permute-start.2 = (bf16[2,4,2,2,64,128]{5,4,3,2,1,0:T(8,128)(2,1)}, bf16[2,4,2,2,64,128]{5,4,3,2,1,0:T(8,128)(2,1)S(1)}, u32[]{:S(2)}, u32[]{:S(2)}) collective-permute-start(bf16[2,4,2,2,64,128]{5,4,3,2,1,0:T(8,128)(2,1)} %shard_map.65.refs_0_), channel_id=1, source_target_pairs={{0,4},{2,6},{4,0},{6,2},{1,5},{3,7},{5,1},{7,3},{8,12},{10,14},{12... | collective-permute-start | bytes 1572872 | tf_op jit(solution)/shard_map/ppermute | solution.py:284
  47.9 23.4 %collective-permute-start.3 = (bf16[2,4,2,2,64,128]{5,4,3,2,1,0:T(8,128)(2,1)}, bf16[2,4,2,2,64,128]{5,4,3,2,1,0:T(8,128)(2,1)S(1)}, u32[]{:S(2)}, u32[]{:S(2)}) collective-permute-start(bf16[2,4,2,2,64,128]{5,4,3,2,1,0:T(8,128)(2,1)} %shard_map.65.refs_0_), channel_id=1, source_target_pairs={{0,6},{2,0},{4,2},{6,4},{1,7},{3,1},{5,3},{7,5},{8,14},{10,8},{12,... | collective-permute-start | bytes 1572872 | tf_op jit(solution)/shard_map/ppermute | solution.py:284
  67.8 15.0 %all-to-all-start.3 = ((bf16[4,8,2,64,128]{4,3,2,1,0:T(8,128)(2,1)}), bf16[4,8,2,64,128]{4,3,2,1,0:T(8,128)(2,1)S(1)}, u32[]{:S(2)}, u32[]{:S(2)}) async-start(bf16[4,8,2,64,128]{4,3,2,1,0:T(8,128)(2,1)} %broadcast_in_dim.28), calls=%async_computation.3 | async-start | bytes 2097152 | tf_op jit(solution)/shard_map/all_to_all | solution.py:279
  71.3 0.8 copy-start.2
  71.4 1.0 copy-start.3
  72.3 0.8 copy-start.4
  82.8 6.5 %copy-start.1 = (bf16[4,8,2,64,128]{4,3,2,1,0:T(8,128)(2,1)}, bf16[4,8,2,64,128]{4,3,2,1,0:T(8,128)(2,1)S(1)}, u32[]{:S(2)}) copy-start(bf16[4,8,2,64,128]{4,3,2,1,0:T(8,128)(2,1)S(1)} %all-to-all-done.3.kv_hbm) | copy-start | bytes 3145732
  82.8 11.6 %collective-permute-start.4 = (bf16[4,8,2,64,128]{4,3,2,1,0:T(8,128)(2,1)S(1)}, bf16[4,8,2,64,128]{4,3,2,1,0:T(8,128)(2,1)S(1)}, u32[]{:S(2)}, u32[]{:S(2)}) collective-permute-start(bf16[4,8,2,64,128]{4,3,2,1,0:T(8,128)(2,1)S(1)} %all-to-all-done.3.kv_hbm), channel_id=1, source_target_pairs={{0,8},{8,0},{1,9},{9,1},{2,10},{10,2},{3,11},{11,3},{4,12},{12,4},... | collective-permute-start | bytes 3145736 | tf_op jit(solution)/shard_map/ppermute | solution.py:275
  94.3 1.0 copy-start

commit v6 on v5

--- a/solution.py
+++ b/solution.py
@@ -15,7 +15,7 @@
 WIDTH = GROUP * HEAD_DIM
 AXES = ("y", "zl", "core", "x", "zh")
 SIZES = (8, 4, 2, 4, 2)
-CHUNK = 4
+CHUNK = 8
 SCALE = math.log2(math.e) / math.sqrt(HEAD_DIM)
 NEG = -math.inf
 
@@ -153,11 +153,14 @@
 
     def load(i):
         start_ahead(group_copies, i + 2, HALF)
-        for copy in group_copies(i):
+        for copy in group_copies(i)[:2]:
             copy.wait()
         return [kv_buf[i, :, kind].reshape(8 * rows, HEAD_DIM) for kind in range(2)]
 
     def finish(i, c, m1, l1, o1):
+        if c == 0:
+            for copy in group_copies(i)[2:]:
+                copy.wait()
         at = pl.ds(c * CHUNK * rows, CHUNK * rows)
         lse1 = jnp.where(is_anchor, NEG, m1 * SCALE + jnp.log2(l1))
         share = 1.0 / (1.0 + jnp.exp2(lse_buf[i, at] - lse1))
@@ -267,6 +270,22 @@
     )(keys, values)
 
 
+def copies_kernel(a_ref, out_ref):
+    for i in range(out_ref.shape[0]):
+        out_ref[i] = a_ref[...]
+
+
+def copies(a, n, interpret=False):
+    return pl.pallas_call(
+        copies_kernel,
+        out_shape=jax.ShapeDtypeStruct((n,) + a.shape, a.dtype),
+        in_specs=[VMEM],
+        out_specs=VMEM,
+        cost_estimate=LONG,
+        interpret=interpret,
+    )(a)
+
+
 def to_all(a, axes, n):
     return exchange(jnp.broadcast_to(a[None], (n,) + a.shape), axes)
 
@@ -297,9 +316,10 @@
     part = lax.dynamic_index_in_dim(part, (anchor_shard >> 1) & 3, 0, keepdims=False)
     pair = make_pair(me, pieces, other, interpret)
     part, pair = lax.optimization_barrier((part, pair))
-    own = [pair] + [shift(pair, "x", s) for s in range(1, 4)]
+    ahead = shift(pair, "x", 3)
+    own = [pair, shift(pair, "x", 1), shift(ahead, "x", 3), ahead]
     part = to_all(part, "y", 8)
-    mine = to_all(part, "x", 4)
+    mine = exchange(copies(part, 4, interpret), "x")
     o, lse = attend_own(me, assignment, lengths, queries, own, interpret)
     mine, o, lse = lax.optimization_barrier((mine, o, lse))
     theirs = swap(mine, "core")

time: 101 us -> 101 us (level)
  blocking collectives: 15.5 us -> 0 us
  starting transfers between devices: 47.3 us -> 54 us
  Pallas kernels: 21.5 us -> 26.3 us
  waiting for transfers between devices: 6.65 us -> 10.7 us
    all_to_all x1 -> x0, blocking collectives: 15.5 us -> none  [exchange(): return lax.all_to_all(a, axes, split_axis=0, concat_axis=0, tiled=True)]
    all_to_all x3 -> x4, starting transfers between devices: 21.2 us -> 27.2 us  [exchange(): return lax.all_to_all(a, axes, split_axis=0, concat_axis=0, tiled=True)]
    ppermute x3, waiting for transfers between devices: 0.01 us -> 5.15 us  [shift(): return lax.ppermute(a, axis, [(i, (i + by) % n) for i in range(n)])]
    pallas_call x2, Pallas kernels: 10.1 us -> 12.3 us  [attend_anchor(): pl.pallas_call(functools.partial(anchor_kernel, which), out_shape=jax.Sha...]
    pallas_call x0 -> x1, Pallas kernels: none -> 2.04 us  [copies(): pl.pallas_call(copies_kernel, out_shape=jax.ShapeDtypeStruct((n,) + a.sha...]
    all_to_all x3 -> x4, waiting for transfers between devices: 6.63 us -> 5.55 us  [exchange(): return lax.all_to_all(a, axes, split_axis=0, concat_axis=0, tiled=True)]
    unnamed x12 -> x14, local copies, waits for them, and re-layouts: 3.42 us -> 3.2 us
  transfers between devices with their start and end apart: 8 -> 9, of which waited for: 2 -> 4; matrix products, arithmetic and copies ran while one was open for 3% -> 3% of each run, Pallas kernels for 15% -> 18%
where the time goes in v6:
time: 101 us; the launch traced here: 99.9 us
  starting transfers between devices  54 us (53%)
  Pallas kernels  26.3 us (26%)
  waiting for transfers between devices  10.7 us (11%)
  local copies, waits for them, and re-layouts  4.63 us (5%)
  between operations  2.89 us (3%)
  other arithmetic  1.37 us (1%)
    all_to_all x4, starting transfers between devices, exchange(): return lax.all_to_all(a, axes, split_axis=0, concat_axis=0, tiled=True)  27.2 us
    ppermute x2, starting transfers between devices, swap(): return lax.ppermute(a, axis, [(0, 1), (1, 0)])  15.3 us
    pallas_call x2, Pallas kernels, attend_anchor(): pl.pallas_call(functools.partial(anchor_kernel, which), out_shape=jax.Sha...  12.3 us
    ppermute x3, starting transfers between devices, shift(): return lax.ppermute(a, axis, [(i, (i + by) % n) for i in range(n)])  11.5 us
    pallas_call x1, Pallas kernels, attend_own(): pl.pallas_call(own_kernel, out_shape=(part, part), in_specs=[SMEM, SMEM,...  8.38 us
    all_to_all x4, waiting for transfers between devices, exchange(): return lax.all_to_all(a, axes, split_axis=0, concat_axis=0, tiled=True)  5.55 us
    ppermute x3, waiting for transfers between devices, shift(): return lax.ppermute(a, axis, [(i, (i + by) % n) for i in range(n)])  5.15 us
    unnamed x14, local copies, waits for them, and re-layouts  3.2 us
  transfers between devices with their start and end apart: 9, of which 4 were waited for; matrix products, arithmetic and copies ran while one was open for 3% of the time, Pallas kernels for 18%

profile of v6, /device:TPU:1, one launch (start us, length us, event | category | flops | bytes accessed | tf_op | source)
XLA Modules:
  0.0 99.9 jit_solution(7963002221588189586)
XLA Ops:
  0.0 1.7 %shard_map.64.mine_ref = bf16[4,2,2,64,128]{4,3,2,1,0:T(8,128)(2,1)} custom-call(bf16[64,1024]{1,0:T(8,128)(2,1)} %k_ref.1, bf16[64,1024]{1,0:T(8,128)(2,1)} %v_ref.1), custom_call_target="tpu_custom_call" | custom-call | tf_op jit(solution)/shard_map/pallas_call | solution.py:264
  1.7 10.2 %all-to-all-start = ((bf16[16,64,128]{2,1,0:T(8,128)(2,1)}), bf16[16,64,128]{2,1,0:T(8,128)(2,1)S(1)}, u32[]{:S(2)}, u32[]{:S(2)}) async-start(bf16[16,64,128]{2,1,0:T(8,128)(2,1)} %bitcast.9), calls=%async_computation | async-start | bytes 524288 | tf_op jit(solution)/shard_map/all_to_all | solution.py:298
  11.9 9.1 %collective-permute-start = (bf16[4,2,2,64,128]{4,3,2,1,0:T(8,128)(2,1)}, bf16[4,2,2,64,128]{4,3,2,1,0:T(8,128)(2,1)S(1)}, u32[]{:S(2)}, u32[]{:S(2)}) collective-permute-start(bf16[4,2,2,64,128]{4,3,2,1,0:T(8,128)(2,1)} %shard_map.64.mine_ref), channel_id=1, source_target_pairs={{0,1},{1,0},{2,3},{3,2},{4,5},{5,4},{6,7},{7,6},{8,9},{9,8},{10,11... | collective-permute-start | bytes 786440 | tf_op jit(solution)/shard_map/ppermute | solution.py:294
  21.6 1.4 %fusion = s32[]{:T(128)} fusion(s32[64]{0:T(128)} %assignment.5, s32[]{:T(128)} %bitcast.8), kind=kLoop, calls=%fused_computation.3 | loop fusion | flops 191 | bytes 264 | tf_op jit(solution)/shard_map/reduce_sum | solution.py:308
  25.1 0.0 all-to-all-done
  25.1 0.7 broadcast_in_dim.20
  25.8 7.2 %all-to-all-start.1 = ((bf16[8,64,128]{2,1,0:T(8,128)(2,1)}), bf16[8,64,128]{2,1,0:T(8,128)(2,1)S(1)}, u32[]{:S(2)}, u32[]{:S(2)}) async-start(bf16[8,64,128]{2,1,0:T(8,128)(2,1)} %broadcast_in_dim.20), calls=%async_computation.1 | async-start | bytes 262144 | tf_op jit(solution)/shard_map/all_to_all | solution.py:298
  33.0 0.0 collective-permute-done.other_ref
  33.0 0.0 copy-start.6
  33.1 0.7 copy-done.6
  33.8 1.9 %shard_map.65.refs_0_ = bf16[2,4,2,2,64,128]{5,4,3,2,1,0:T(8,128)(2,1)} custom-call(s32[1]{0:T(128)} %bitcast.me, bf16[4,2,2,64,128]{4,3,2,1,0:T(8,128)(2,1)} %shard_map.64.mine_ref, bf16[4,2,2,64,128]{4,3,2,1,0:T(8,128)(2,1)} %copy-done.6), custom_call_target="tpu_custom_call" | custom-call | flops 68719476736 | bytes 6291456 | tf_op jit(solution)/shard_map/pallas_call | solution.py:247
  35.6 4.8 %all-to-all-done.1 = bf16[8,64,128]{2,1,0:T(8,128)(2,1)S(1)} async-done(((bf16[8,64,128]{2,1,0:T(8,128)(2,1)}), bf16[8,64,128]{2,1,0:T(8,128)(2,1)S(1)}, u32[]{:S(2)}, u32[]{:S(2)}) %all-to-all-start.1) | async-done | bytes 131104 | tf_op jit(solution)/shard_map/all_to_all | solution.py:298
  40.5 4.4 %collective-permute-start.2 = (bf16[2,4,2,2,64,128]{5,4,3,2,1,0:T(8,128)(2,1)}, bf16[2,4,2,2,64,128]{5,4,3,2,1,0:T(8,128)(2,1)S(1)}, u32[]{:S(2)}, u32[]{:S(2)}) collective-permute-start(bf16[2,4,2,2,64,128]{5,4,3,2,1,0:T(8,128)(2,1)} %shard_map.65.refs_0_), channel_id=1, source_target_pairs={{0,6},{2,0},{4,2},{6,4},{1,7},{3,1},{5,3},{7,5},{8,14},{10,8},{12,... | collective-permute-start | bytes 1572872 | tf_op jit(solution)/shard_map/ppermute | solution.py:303
  44.8 0.8 broadcast_in_dim.21
  45.6 6.3 %all-to-all-start.2 = ((bf16[8,2,64,128]{3,2,1,0:T(8,128)(2,1)}), bf16[8,2,64,128]{3,2,1,0:T(8,128)(2,1)S(1)}, u32[]{:S(2)}, u32[]{:S(2)}) async-start(bf16[8,2,64,128]{3,2,1,0:T(8,128)(2,1)} %broadcast_in_dim.21), calls=%async_computation.2 | async-start | bytes 524288 | tf_op jit(solution)/shard_map/all_to_all | solution.py:298
  51.8 1.9 %collective-permute-start.1 = (bf16[2,4,2,2,64,128]{5,4,3,2,1,0:T(8,128)(2,1)}, bf16[2,4,2,2,64,128]{5,4,3,2,1,0:T(8,128)(2,1)S(1)}, u32[]{:S(2)}, u32[]{:S(2)}) collective-permute-start(bf16[2,4,2,2,64,128]{5,4,3,2,1,0:T(8,128)(2,1)} %shard_map.65.refs_0_), channel_id=1, source_target_pairs={{0,2},{2,4},{4,6},{6,0},{1,3},{3,5},{5,7},{7,1},{8,10},{10,12},{12... | collective-permute-start | bytes 1572872 | tf_op jit(solution)/shard_map/ppermute | solution.py:303
  53.8 2.2 %collective-permute-done.2.refs_3_ = bf16[2,4,2,2,64,128]{5,4,3,2,1,0:T(8,128)(2,1)S(1)} collective-permute-done((bf16[2,4,2,2,64,128]{5,4,3,2,1,0:T(8,128)(2,1)}, bf16[2,4,2,2,64,128]{5,4,3,2,1,0:T(8,128)(2,1)S(1)}, u32[]{:S(2)}, u32[]{:S(2)}) %collective-permute-start.2) | collective-permute-done | bytes 524320 | tf_op jit(solution)/shard_map/ppermute | solution.py:303
  56.0 0.0 copy-start.3
  56.0 5.2 %collective-permute-start.3 = (bf16[2,4,2,2,64,128]{5,4,3,2,1,0:T(8,128)(2,1)S(1)}, bf16[2,4,2,2,64,128]{5,4,3,2,1,0:T(8,128)(2,1)S(1)}, u32[]{:S(2)}, u32[]{:S(2)}) collective-permute-start(bf16[2,4,2,2,64,128]{5,4,3,2,1,0:T(8,128)(2,1)S(1)} %collective-permute-done.2.refs_3_), channel_id=1, source_target_pairs={{0,6},{2,0},{4,2},{6,4},{1,7},{3,1},{5,3},{7,5},{8,14},{10,8},{12,... | collective-permute-start | bytes 1572872 | tf_op jit(solution)/shard_map/ppermute | solution.py:303
  61.2 0.7 all-to-all-done.2.a_ref
  61.9 0.0 copy-start.2
  61.9 0.7 copy-done.2
  62.6 2.0 %shard_map.66 = bf16[4,8,2,64,128]{4,3,2,1,0:T(8,128)(2,1)} custom-call(bf16[8,2,64,128]{3,2,1,0:T(8,128)(2,1)} %copy-done.2), custom_call_target="tpu_custom_call" | custom-call | flops 68719476736 | bytes 6291456 | tf_op jit(solution)/shard_map/pallas_call | solution.py:279
  64.7 0.0 copy-done.3
  64.7 3.5 %all-to-all-start.3 = ((bf16[4,8,2,64,128]{4,3,2,1,0:T(8,128)(2,1)}), bf16[4,8,2,64,128]{4,3,2,1,0:T(8,128)(2,1)S(1)}, u32[]{:S(2)}, u32[]{:S(2)}) async-start(bf16[4,8,2,64,128]{4,3,2,1,0:T(8,128)(2,1)} %shard_map.66), calls=%async_computation.3 | async-start | bytes 2097152 | tf_op jit(solution)/shard_map/all_to_all | solution.py:298
  68.2 0.0 collective-permute-done.1.refs_1_
  68.2 0.0 copy-start.4
  68.2 2.9 %collective-permute-done.3.refs_2_ = bf16[2,4,2,2,64,128]{5,4,3,2,1,0:T(8,128)(2,1)S(1)} collective-permute-done((bf16[2,4,2,2,64,128]{5,4,3,2,1,0:T(8,128)(2,1)S(1)}, bf16[2,4,2,2,64,128]{5,4,3,2,1,0:T(8,128)(2,1)S(1)}, u32[]{:S(2)}, u32[]{:S(2)}) %collective-permute-start.3) | collective-permute-done | bytes 524320 | tf_op jit(solution)/shard_map/ppermute | solution.py:303
  71.1 0.0 copy-done.4
  71.1 0.0 copy-start.5
  71.1 0.8 copy-done.5
  71.9 8.4 %shard_map.67 = (f32[8,512,128]{2,1,0:T(8,128)}, f32[8,512,128]{2,1,0:T(8,128)}) custom-call(s32[1]{0:T(128)} %bitcast.me, s32[64]{0:T(128)} %assignment.5, s32[64]{0:T(128)} %lengths.5, bf16[64,8192]{1,0:T(8,128)(2,1)} %q_hbm.5, bf16[2,4,2,2,64,128]{5,4,3,2,1,0:T(8,128)(2,1)} %shard_map.65.refs_0_, bf16[2,4,2,2,64,128]{5,4,3,2,1,0:T(8,128)(2,1)} %copy-done.4, ...), custom_call_target="tpu_custom_call" | custom-call | flops 68719476736 | bytes 6291456 | tf_op jit(solution)/shard_map/pallas_call | solution.py:191
  80.3 0.0 all-to-all-done.3.kv_hbm
  80.3 0.0 copy-start.1
  80.4 6.2 %collective-permute-start.4 = (bf16[4,8,2,64,128]{4,3,2,1,0:T(8,128)(2,1)S(1)}, bf16[4,8,2,64,128]{4,3,2,1,0:T(8,128)(2,1)S(1)}, u32[]{:S(2)}, u32[]{:S(2)}) collective-permute-start(bf16[4,8,2,64,128]{4,3,2,1,0:T(8,128)(2,1)S(1)} %all-to-all-done.3.kv_hbm), channel_id=1, source_target_pairs={{0,8},{8,0},{1,9},{9,1},{2,10},{10,2},{3,11},{11,3},{4,12},{12,4},... | collective-permute-start | bytes 3145736 | tf_op jit(solution)/shard_map/ppermute | solution.py:294
  86.6 0.0 copy-done.1
  86.6 6.2 %shard_map.68.refs_0_ = bf16[64,8192]{1,0:T(8,128)(2,1)} custom-call(s32[1]{0:T(128)} %bitcast.me, s32[64]{0:T(128)} %assignment.5, s32[1]{0:T(128)} %copy.9.anchor, s32[64]{0:T(128)} %lengths.5, bf16[64,8192]{1,0:T(8,128)(2,1)} %q_hbm.5, bf16[4,8,2,64,128]{4,3,2,1,0:T(8,128)(2,1)} %copy-done.1, f32[8,512,128]{2,1,0:T(8,128)} %get-tuple-element.17.o_hbm, ...), custom_call_target="tpu_custom_call" | custom-call | flops 2147483648 | bytes 6291456 | tf_op jit(solution)/shard_map/pallas_call | solution.py:218
  92.8 0.0 collective-permute-done.4.kv_hbm
  92.8 0.0 copy-start
  92.8 1.0 copy-done
  93.8 6.2 %shard_map.69 = bf16[64,8192]{1,0:T(8,128)(2,1)} custom-call(s32[1]{0:T(128)} %bitcast.me, s32[64]{0:T(128)} %assignment.5, s32[1]{0:T(128)} %copy.9.anchor, s32[64]{0:T(128)} %lengths.5, bf16[64,8192]{1,0:T(8,128)(2,1)} %q_hbm.5, bf16[4,8,2,64,128]{4,3,2,1,0:T(8,128)(2,1)} %copy-done, ...), custom_call_target="tpu_custom_call", output_to_operand_aliasing={{}: (8, {})} | custom-call | flops 2147483648 | bytes 6291456 | tf_op jit(solution)/shard_map/pallas_call | solution.py:218
  (2 shorter events, 0.0 us)
Async XLA Ops:
  1.7 23.4 %all-to-all-start = ((bf16[16,64,128]{2,1,0:T(8,128)(2,1)}), bf16[16,64,128]{2,1,0:T(8,128)(2,1)S(1)}, u32[]{:S(2)}, u32[]{:S(2)}) async-start(bf16[16,64,128]{2,1,0:T(8,128)(2,1)} %bitcast.9), calls=%async_computation | async-start | bytes 524288 | tf_op jit(solution)/shard_map/all_to_all | solution.py:298
  11.9 21.1 %collective-permute-start = (bf16[4,2,2,64,128]{4,3,2,1,0:T(8,128)(2,1)}, bf16[4,2,2,64,128]{4,3,2,1,0:T(8,128)(2,1)S(1)}, u32[]{:S(2)}, u32[]{:S(2)}) collective-permute-start(bf16[4,2,2,64,128]{4,3,2,1,0:T(8,128)(2,1)} %shard_map.64.mine_ref), channel_id=1, source_target_pairs={{0,1},{1,0},{2,3},{3,2},{4,5},{5,4},{6,7},{7,6},{8,9},{9,8},{10,11... | collective-permute-start | bytes 786440 | tf_op jit(solution)/shard_map/ppermute | solution.py:294
  25.8 14.7 %all-to-all-start.1 = ((bf16[8,64,128]{2,1,0:T(8,128)(2,1)}), bf16[8,64,128]{2,1,0:T(8,128)(2,1)S(1)}, u32[]{:S(2)}, u32[]{:S(2)}) async-start(bf16[8,64,128]{2,1,0:T(8,128)(2,1)} %broadcast_in_dim.20), calls=%async_computation.1 | async-start | bytes 262144 | tf_op jit(solution)/shard_map/all_to_all | solution.py:298
  33.0 0.7 copy-start.6
  40.5 15.5 %collective-permute-start.2 = (bf16[2,4,2,2,64,128]{5,4,3,2,1,0:T(8,128)(2,1)}, bf16[2,4,2,2,64,128]{5,4,3,2,1,0:T(8,128)(2,1)S(1)}, u32[]{:S(2)}, u32[]{:S(2)}) collective-permute-start(bf16[2,4,2,2,64,128]{5,4,3,2,1,0:T(8,128)(2,1)} %shard_map.65.refs_0_), channel_id=1, source_target_pairs={{0,6},{2,0},{4,2},{6,4},{1,7},{3,1},{5,3},{7,5},{8,14},{10,8},{12,... | collective-permute-start | bytes 1572872 | tf_op jit(solution)/shard_map/ppermute | solution.py:303
  45.6 16.3 %all-to-all-start.2 = ((bf16[8,2,64,128]{3,2,1,0:T(8,128)(2,1)}), bf16[8,2,64,128]{3,2,1,0:T(8,128)(2,1)S(1)}, u32[]{:S(2)}, u32[]{:S(2)}) async-start(bf16[8,2,64,128]{3,2,1,0:T(8,128)(2,1)} %broadcast_in_dim.21), calls=%async_computation.2 | async-start | bytes 524288 | tf_op jit(solution)/shard_map/all_to_all | solution.py:298
  51.8 16.4 %collective-permute-start.1 = (bf16[2,4,2,2,64,128]{5,4,3,2,1,0:T(8,128)(2,1)}, bf16[2,4,2,2,64,128]{5,4,3,2,1,0:T(8,128)(2,1)S(1)}, u32[]{:S(2)}, u32[]{:S(2)}) collective-permute-start(bf16[2,4,2,2,64,128]{5,4,3,2,1,0:T(8,128)(2,1)} %shard_map.65.refs_0_), channel_id=1, source_target_pairs={{0,2},{2,4},{4,6},{6,0},{1,3},{3,5},{5,7},{7,1},{8,10},{10,12},{12... | collective-permute-start | bytes 1572872 | tf_op jit(solution)/shard_map/ppermute | solution.py:303
  56.0 8.7 %copy-start.3 = (bf16[2,4,2,2,64,128]{5,4,3,2,1,0:T(8,128)(2,1)}, bf16[2,4,2,2,64,128]{5,4,3,2,1,0:T(8,128)(2,1)S(1)}, u32[]{:S(2)}) copy-start(bf16[2,4,2,2,64,128]{5,4,3,2,1,0:T(8,128)(2,1)S(1)} %collective-permute-done.2.refs_3_) | copy-start | bytes 1572868
  56.0 15.1 %collective-permute-start.3 = (bf16[2,4,2,2,64,128]{5,4,3,2,1,0:T(8,128)(2,1)S(1)}, bf16[2,4,2,2,64,128]{5,4,3,2,1,0:T(8,128)(2,1)S(1)}, u32[]{:S(2)}, u32[]{:S(2)}) collective-permute-start(bf16[2,4,2,2,64,128]{5,4,3,2,1,0:T(8,128)(2,1)S(1)} %collective-permute-done.2.refs_3_), channel_id=1, source_target_pairs={{0,6},{2,0},{4,2},{6,4},{1,7},{3,1},{5,3},{7,5},{8,14},{10,8},{12,... | collective-permute-start | bytes 1572872 | tf_op jit(solution)/shard_map/ppermute | solution.py:303
  61.9 0.7 copy-start.2
  64.7 15.7 %all-to-all-start.3 = ((bf16[4,8,2,64,128]{4,3,2,1,0:T(8,128)(2,1)}), bf16[4,8,2,64,128]{4,3,2,1,0:T(8,128)(2,1)S(1)}, u32[]{:S(2)}, u32[]{:S(2)}) async-start(bf16[4,8,2,64,128]{4,3,2,1,0:T(8,128)(2,1)} %shard_map.66), calls=%async_computation.3 | async-start | bytes 2097152 | tf_op jit(solution)/shard_map/all_to_all | solution.py:298
  68.2 2.9 %copy-start.4 = (bf16[2,4,2,2,64,128]{5,4,3,2,1,0:T(8,128)(2,1)}, bf16[2,4,2,2,64,128]{5,4,3,2,1,0:T(8,128)(2,1)S(1)}, u32[]{:S(2)}) copy-start(bf16[2,4,2,2,64,128]{5,4,3,2,1,0:T(8,128)(2,1)S(1)} %collective-permute-done.1.refs_1_) | copy-start | bytes 1572868
  71.1 0.8 copy-start.5
  80.3 6.2 %copy-start.1 = (bf16[4,8,2,64,128]{4,3,2,1,0:T(8,128)(2,1)}, bf16[4,8,2,64,128]{4,3,2,1,0:T(8,128)(2,1)S(1)}, u32[]{:S(2)}) copy-start(bf16[4,8,2,64,128]{4,3,2,1,0:T(8,128)(2,1)S(1)} %all-to-all-done.3.kv_hbm) | copy-start | bytes 3145732
  80.4 12.4 %collective-permute-start.4 = (bf16[4,8,2,64,128]{4,3,2,1,0:T(8,128)(2,1)S(1)}, bf16[4,8,2,64,128]{4,3,2,1,0:T(8,128)(2,1)S(1)}, u32[]{:S(2)}, u32[]{:S(2)}) collective-permute-start(bf16[4,8,2,64,128]{4,3,2,1,0:T(8,128)(2,1)S(1)} %all-to-all-done.3.kv_hbm), channel_id=1, source_target_pairs={{0,8},{8,0},{1,9},{9,1},{2,10},{10,2},{3,11},{11,3},{4,12},{12,4},... | collective-permute-start | bytes 3145736 | tf_op jit(solution)/shard_map/ppermute | solution.py:294
  92.8 1.0 copy-start

commit v7 on v5

--- a/solution.py
+++ b/solution.py
@@ -15,7 +15,8 @@
 WIDTH = GROUP * HEAD_DIM
 AXES = ("y", "zl", "core", "x", "zh")
 SIZES = (8, 4, 2, 4, 2)
-CHUNK = 4
+OWN_CHUNK = 4
+ANCHOR_CHUNK = 2
 SCALE = math.log2(math.e) / math.sqrt(HEAD_DIM)
 NEG = -math.inf
 
@@ -24,26 +25,26 @@
     return pl.ds(pl.multiple_of(g * WIDTH, WIDTH), WIDTH)
 
 
-def scores(q_ref, c, k):
-    first = c * CHUNK * HEAD_DIM
+def scores(q_ref, c, chunk, k):
+    first = c * chunk * HEAD_DIM
     q = jnp.concatenate(
-        [q_ref[:, first + i * HEAD_DIM : first + (i + 1) * HEAD_DIM] for i in range(CHUNK)], axis=0
+        [q_ref[:, first + i * HEAD_DIM : first + (i + 1) * HEAD_DIM] for i in range(chunk)], axis=0
     )
     return lax.dot_general(q, k, (((1,), (1,)), ((), ())), preferred_element_type=jnp.float32)
 
 
-def softmax(s, bias):
+def softmax(s, chunk, bias):
     free = s.shape[1] - bias.shape[1]
-    rows = s.shape[0] // CHUNK
-    tail = (s[:, free:].reshape(CHUNK, rows, -1) + bias[None]).reshape(CHUNK * rows, -1)
+    rows = s.shape[0] // chunk
+    tail = (s[:, free:].reshape(chunk, rows, -1) + bias[None]).reshape(chunk * rows, -1)
     s = jnp.concatenate([s[:, :free], tail], axis=1) if free else tail
     m = jnp.max(s, axis=1, keepdims=True)
     e = jnp.exp2((s - m) * SCALE)
     return m, jnp.sum(e, axis=1, keepdims=True), e.astype(jnp.bfloat16)
 
 
-def attend_heads(q_buf, heads, load, bias, finish):
-    work = [(g, c) for g in heads for c in range(GROUP // CHUNK)]
+def attend_heads(q_buf, heads, chunk, load, bias, finish):
+    work = [(g, c) for g in heads for c in range(GROUP // chunk)]
     found, weighed, values = {}, {}, {}
     for t in range(len(work) + 2):
         if t < len(work):
@@ -51,13 +52,13 @@
             if c == 0:
                 k, v = load(g)
             values[t] = v
-            found[t] = scores(q_buf.at[g], c, k)
+            found[t] = scores(q_buf.at[g], c, chunk, k)
         if t >= 2:
             m, l, e = weighed.pop(t - 2)
             o = jnp.dot(e, values.pop(t - 2), preferred_element_type=jnp.float32)
             finish(*work[t - 2], m, l, o)
         if 1 <= t <= len(work):
-            weighed[t - 1] = softmax(found.pop(t - 1), bias)
+            weighed[t - 1] = softmax(found.pop(t - 1), chunk, bias)
 
 
 def query_copy(q_hbm, q_buf, sem, g):
@@ -108,15 +109,15 @@
         return [kv_buf[g, :, :, kind].reshape(8 * rows, HEAD_DIM) for kind in range(2)]
 
     def finish(g, c, m, l, o):
-        at = pl.ds(c * CHUNK * rows, CHUNK * rows)
+        at = pl.ds(c * OWN_CHUNK * rows, OWN_CHUNK * rows)
         o_buf[g, at] = o * (1.0 / l)
         lse_buf[g, at] = jnp.broadcast_to(m * SCALE + jnp.log2(l), o.shape)
-        if c == GROUP // CHUNK - 1:
+        if c == GROUP // OWN_CHUNK - 1:
             for copy in result_copies(g):
                 copy.start()
 
     def step(i, carry):
-        attend_heads(q_buf, [4 * i + j for j in range(4)], load, bias_ref[...], finish)
+        attend_heads(q_buf, [4 * i + j for j in range(4)], OWN_CHUNK, load, bias_ref[...], finish)
         return carry
 
     lax.fori_loop(0, KV_HEADS // 4, step, 0)
@@ -158,18 +159,18 @@
         return [kv_buf[i, :, kind].reshape(8 * rows, HEAD_DIM) for kind in range(2)]
 
     def finish(i, c, m1, l1, o1):
-        at = pl.ds(c * CHUNK * rows, CHUNK * rows)
+        at = pl.ds(c * ANCHOR_CHUNK * rows, ANCHOR_CHUNK * rows)
         lse1 = jnp.where(is_anchor, NEG, m1 * SCALE + jnp.log2(l1))
         share = 1.0 / (1.0 + jnp.exp2(lse_buf[i, at] - lse1))
         o = (1.0 - share) * o_buf[i, at] + (share * (1.0 / l1)) * o1
         o = o.astype(out_buf.dtype)
-        for j in range(CHUNK):
-            to = (c * CHUNK + j) * HEAD_DIM
+        for j in range(ANCHOR_CHUNK):
+            to = (c * ANCHOR_CHUNK + j) * HEAD_DIM
             out_buf[i, :, to : to + HEAD_DIM] = o[j * rows : (j + 1) * rows]
-        if c == GROUP // CHUNK - 1:
+        if c == GROUP // ANCHOR_CHUNK - 1:
             out_copy(i).start()
 
-    attend_heads(q_buf, list(range(HALF)), load, bias_ref[0:1, :], finish)
+    attend_heads(q_buf, list(range(HALF)), ANCHOR_CHUNK, load, bias_ref[0:1, :], finish)
     for i in range(HALF):
         out_copy(i).wait()
 
@@ -267,6 +268,18 @@
     )(keys, values)
 
 
+def hold(a, interpret=False):
+    return pl.pallas_call(
+        lambda a_ref, out_ref: None,
+        out_shape=jax.ShapeDtypeStruct(a.shape, a.dtype),
+        in_specs=[ANY],
+        out_specs=ANY,
+        input_output_aliases={0: 0},
+        cost_estimate=LONG,
+        interpret=interpret,
+    )(a)
+
+
 def to_all(a, axes, n):
     return exchange(jnp.broadcast_to(a[None], (n,) + a.shape), axes)
 
@@ -297,9 +310,10 @@
     part = lax.dynamic_index_in_dim(part, (anchor_shard >> 1) & 3, 0, keepdims=False)
     pair = make_pair(me, pieces, other, interpret)
     part, pair = lax.optimization_barrier((part, pair))
-    own = [pair] + [shift(pair, "x", s) for s in range(1, 4)]
+    ahead = shift(pair, "x", 3)
+    own = [pair, shift(pair, "x", 1), shift(ahead, "x", 3), ahead]
     part = to_all(part, "y", 8)
-    mine = to_all(part, "x", 4)
+    mine = to_all(hold(part, interpret), "x", 4)
     o, lse = attend_own(me, assignment, lengths, queries, own, interpret)
     mine, o, lse = lax.optimization_barrier((mine, o, lse))
     theirs = swap(mine, "core")

time: 101 us -> 99 us (0.980)
  blocking collectives: 15.5 us -> 0 us
  starting transfers between devices: 47.3 us -> 54 us
  waiting for transfers between devices: 6.65 us -> 11.2 us
  local copies, waits for them, and re-layouts: 5.38 us -> 6.8 us
    all_to_all x1 -> x0, blocking collectives: 15.5 us -> none  [exchange(): return lax.all_to_all(a, axes, split_axis=0, concat_axis=0, tiled=True)]
    all_to_all x3 -> x4, starting transfers between devices: 21.2 us -> 27.2 us  [exchange(): return lax.all_to_all(a, axes, split_axis=0, concat_axis=0, tiled=True)]
    ppermute x3, waiting for transfers between devices: 0.01 us -> 5.01 us  [shift(): return lax.ppermute(a, axis, [(i, (i + by) % n) for i in range(n)])]
    broadcast_in_dim x4, local copies, waits for them, and re-layouts: 1.95 us -> 3.6 us  [to_all(): return exchange(jnp.broadcast_to(a[None], (n,) + a.shape), axes)]
    all_to_all x3 -> x4, waiting for transfers between devices: 6.63 us -> 6.14 us  [exchange(): return lax.all_to_all(a, axes, split_axis=0, concat_axis=0, tiled=True)]
    unnamed x12 -> x14, local copies, waits for them, and re-layouts: 3.42 us -> 3.19 us
  transfers between devices with their start and end apart: 8 -> 9, of which waited for: 2 -> 5; matrix products, arithmetic and copies ran while one was open for 3% -> 5% of each run, Pallas kernels for 15% -> 15%
where the time goes in v7:
time: 99 us; the launch traced here: 98 us
  starting transfers between devices  54 us (55%)
  Pallas kernels  21.8 us (22%)
  waiting for transfers between devices  11.2 us (11%)
  local copies, waits for them, and re-layouts  6.8 us (7%)
  between operations  2.88 us (3%)
  other arithmetic  1.37 us (1%)
    all_to_all x4, starting transfers between devices, exchange(): return lax.all_to_all(a, axes, split_axis=0, concat_axis=0, tiled=True)  27.2 us
    ppermute x2, starting transfers between devices, swap(): return lax.ppermute(a, axis, [(0, 1), (1, 0)])  15.3 us
    ppermute x3, starting transfers between devices, shift(): return lax.ppermute(a, axis, [(i, (i + by) % n) for i in range(n)])  11.5 us
    pallas_call x2, Pallas kernels, attend_anchor(): pl.pallas_call(functools.partial(anchor_kernel, which), out_shape=jax.Sha...  10.4 us
    pallas_call x1, Pallas kernels, attend_own(): pl.pallas_call(own_kernel, out_shape=(part, part), in_specs=[SMEM, SMEM,...  7.83 us
    all_to_all x4, waiting for transfers between devices, exchange(): return lax.all_to_all(a, axes, split_axis=0, concat_axis=0, tiled=True)  6.14 us
    ppermute x3, waiting for transfers between devices, shift(): return lax.ppermute(a, axis, [(i, (i + by) % n) for i in range(n)])  5.01 us
    broadcast_in_dim x4, local copies, waits for them, and re-layouts, to_all(): return exchange(jnp.broadcast_to(a[None], (n,) + a.shape), axes)  3.6 us
  transfers between devices with their start and end apart: 9, of which 5 were waited for; matrix products, arithmetic and copies ran while one was open for 5% of the time, Pallas kernels for 15%

profile of v7, /device:TPU:1, one launch (start us, length us, event | category | flops | bytes accessed | tf_op | source)
XLA Modules:
  0.0 98.0 jit_solution(16594134702282186180)
XLA Ops:
  0.0 1.7 %shard_map.64.mine_ref = bf16[4,2,2,64,128]{4,3,2,1,0:T(8,128)(2,1)} custom-call(bf16[64,1024]{1,0:T(8,128)(2,1)} %k_ref.1, bf16[64,1024]{1,0:T(8,128)(2,1)} %v_ref.1), custom_call_target="tpu_custom_call" | custom-call | tf_op jit(solution)/shard_map/pallas_call | solution.py:262
  1.7 10.2 %all-to-all-start = ((bf16[16,64,128]{2,1,0:T(8,128)(2,1)}), bf16[16,64,128]{2,1,0:T(8,128)(2,1)S(1)}, u32[]{:S(2)}, u32[]{:S(2)}) async-start(bf16[16,64,128]{2,1,0:T(8,128)(2,1)} %bitcast.9), calls=%async_computation | async-start | bytes 524288 | tf_op jit(solution)/shard_map/all_to_all | solution.py:292
  11.9 9.1 %collective-permute-start = (bf16[4,2,2,64,128]{4,3,2,1,0:T(8,128)(2,1)}, bf16[4,2,2,64,128]{4,3,2,1,0:T(8,128)(2,1)S(1)}, u32[]{:S(2)}, u32[]{:S(2)}) collective-permute-start(bf16[4,2,2,64,128]{4,3,2,1,0:T(8,128)(2,1)} %shard_map.64.mine_ref), channel_id=1, source_target_pairs={{0,1},{1,0},{2,3},{3,2},{4,5},{5,4},{6,7},{7,6},{8,9},{9,8},{10,11... | collective-permute-start | bytes 786440 | tf_op jit(solution)/shard_map/ppermute | solution.py:288
  21.6 1.4 %fusion = s32[]{:T(128)} fusion(s32[64]{0:T(128)} %assignment.5, s32[]{:T(128)} %bitcast.8), kind=kLoop, calls=%fused_computation.3 | loop fusion | flops 191 | bytes 264 | tf_op jit(solution)/shard_map/reduce_sum | solution.py:302
  25.1 0.0 all-to-all-done
  25.1 0.7 broadcast_in_dim.26
  25.8 7.2 %all-to-all-start.1 = ((bf16[8,64,128]{2,1,0:T(8,128)(2,1)}), bf16[8,64,128]{2,1,0:T(8,128)(2,1)S(1)}, u32[]{:S(2)}, u32[]{:S(2)}) async-start(bf16[8,64,128]{2,1,0:T(8,128)(2,1)} %broadcast_in_dim.26), calls=%async_computation.1 | async-start | bytes 262144 | tf_op jit(solution)/shard_map/all_to_all | solution.py:292
  33.0 0.0 collective-permute-done.other_ref
  33.0 0.0 copy-start.6
  33.1 0.7 copy-done.6
  33.8 1.9 %shard_map.65.refs_0_ = bf16[2,4,2,2,64,128]{5,4,3,2,1,0:T(8,128)(2,1)} custom-call(s32[1]{0:T(128)} %bitcast.me, bf16[4,2,2,64,128]{4,3,2,1,0:T(8,128)(2,1)} %shard_map.64.mine_ref, bf16[4,2,2,64,128]{4,3,2,1,0:T(8,128)(2,1)} %copy-done.6), custom_call_target="tpu_custom_call" | custom-call | flops 68719476736 | bytes 6291456 | tf_op jit(solution)/shard_map/pallas_call | solution.py:245
  35.6 4.8 %all-to-all-done.1 = bf16[8,64,128]{2,1,0:T(8,128)(2,1)S(1)} async-done(((bf16[8,64,128]{2,1,0:T(8,128)(2,1)}), bf16[8,64,128]{2,1,0:T(8,128)(2,1)S(1)}, u32[]{:S(2)}, u32[]{:S(2)}) %all-to-all-start.1) | async-done | bytes 131104 | tf_op jit(solution)/shard_map/all_to_all | solution.py:292
  40.5 4.4 %collective-permute-start.2 = (bf16[2,4,2,2,64,128]{5,4,3,2,1,0:T(8,128)(2,1)}, bf16[2,4,2,2,64,128]{5,4,3,2,1,0:T(8,128)(2,1)S(1)}, u32[]{:S(2)}, u32[]{:S(2)}) collective-permute-start(bf16[2,4,2,2,64,128]{5,4,3,2,1,0:T(8,128)(2,1)} %shard_map.65.refs_0_), channel_id=1, source_target_pairs={{0,6},{2,0},{4,2},{6,4},{1,7},{3,1},{5,3},{7,5},{8,14},{10,8},{12,... | collective-permute-start | bytes 1572872 | tf_op jit(solution)/shard_map/ppermute | solution.py:297
  44.8 0.8 broadcast_in_dim.27
  45.6 6.3 %all-to-all-start.2 = ((bf16[8,2,64,128]{3,2,1,0:T(8,128)(2,1)}), bf16[8,2,64,128]{3,2,1,0:T(8,128)(2,1)S(1)}, u32[]{:S(2)}, u32[]{:S(2)}) async-start(bf16[8,2,64,128]{3,2,1,0:T(8,128)(2,1)} %broadcast_in_dim.27), calls=%async_computation.2 | async-start | bytes 524288 | tf_op jit(solution)/shard_map/all_to_all | solution.py:292
  51.8 1.9 %collective-permute-start.1 = (bf16[2,4,2,2,64,128]{5,4,3,2,1,0:T(8,128)(2,1)}, bf16[2,4,2,2,64,128]{5,4,3,2,1,0:T(8,128)(2,1)S(1)}, u32[]{:S(2)}, u32[]{:S(2)}) collective-permute-start(bf16[2,4,2,2,64,128]{5,4,3,2,1,0:T(8,128)(2,1)} %shard_map.65.refs_0_), channel_id=1, source_target_pairs={{0,2},{2,4},{4,6},{6,0},{1,3},{3,5},{5,7},{7,1},{8,10},{10,12},{12... | collective-permute-start | bytes 1572872 | tf_op jit(solution)/shard_map/ppermute | solution.py:297
  53.8 2.2 %collective-permute-done.2.refs_3_ = bf16[2,4,2,2,64,128]{5,4,3,2,1,0:T(8,128)(2,1)S(1)} collective-permute-done((bf16[2,4,2,2,64,128]{5,4,3,2,1,0:T(8,128)(2,1)}, bf16[2,4,2,2,64,128]{5,4,3,2,1,0:T(8,128)(2,1)S(1)}, u32[]{:S(2)}, u32[]{:S(2)}) %collective-permute-start.2) | collective-permute-done | bytes 524320 | tf_op jit(solution)/shard_map/ppermute | solution.py:297
  56.0 0.0 copy-start.3
  56.0 5.2 %collective-permute-start.3 = (bf16[2,4,2,2,64,128]{5,4,3,2,1,0:T(8,128)(2,1)S(1)}, bf16[2,4,2,2,64,128]{5,4,3,2,1,0:T(8,128)(2,1)S(1)}, u32[]{:S(2)}, u32[]{:S(2)}) collective-permute-start(bf16[2,4,2,2,64,128]{5,4,3,2,1,0:T(8,128)(2,1)S(1)} %collective-permute-done.2.refs_3_), channel_id=1, source_target_pairs={{0,6},{2,0},{4,2},{6,4},{1,7},{3,1},{5,3},{7,5},{8,14},{10,8},{12,... | collective-permute-start | bytes 1572872 | tf_op jit(solution)/shard_map/ppermute | solution.py:297
  61.2 0.7 all-to-all-done.2.a_ref
  61.9 0.0 copy-start.1
  61.9 0.7 copy-done.1
  62.6 0.0 copy-done.3
  62.6 2.2 %broadcast_in_dim.28 = bf16[4,8,2,64,128]{4,3,2,1,0:T(8,128)(2,1)} broadcast(bf16[8,2,64,128]{3,2,1,0:T(8,128)(2,1)} %shard_map.66), dimensions={1,2,3,4} | broadcast | bytes 1310720 | tf_op jit(solution)/shard_map/broadcast_in_dim | solution.py:284
  64.8 3.5 %all-to-all-start.3 = ((bf16[4,8,2,64,128]{4,3,2,1,0:T(8,128)(2,1)}), bf16[4,8,2,64,128]{4,3,2,1,0:T(8,128)(2,1)S(1)}, u32[]{:S(2)}, u32[]{:S(2)}) async-start(bf16[4,8,2,64,128]{4,3,2,1,0:T(8,128)(2,1)} %broadcast_in_dim.28), calls=%async_computation.3 | async-start | bytes 2097152 | tf_op jit(solution)/shard_map/all_to_all | solution.py:292
  68.3 0.0 collective-permute-done.1.refs_1_
  68.4 0.0 copy-start.4
  68.4 2.8 %collective-permute-done.3.refs_2_ = bf16[2,4,2,2,64,128]{5,4,3,2,1,0:T(8,128)(2,1)S(1)} collective-permute-done((bf16[2,4,2,2,64,128]{5,4,3,2,1,0:T(8,128)(2,1)S(1)}, bf16[2,4,2,2,64,128]{5,4,3,2,1,0:T(8,128)(2,1)S(1)}, u32[]{:S(2)}, u32[]{:S(2)}) %collective-permute-start.3) | collective-permute-done | bytes 524320 | tf_op jit(solution)/shard_map/ppermute | solution.py:297
  71.1 0.0 copy-done.4
  71.1 0.0 copy-start.5
  71.1 0.8 copy-done.5
  71.9 7.8 %shard_map.67 = (f32[8,512,128]{2,1,0:T(8,128)}, f32[8,512,128]{2,1,0:T(8,128)}) custom-call(s32[1]{0:T(128)} %bitcast.me, s32[64]{0:T(128)} %assignment.5, s32[64]{0:T(128)} %lengths.5, bf16[64,8192]{1,0:T(8,128)(2,1)} %q_hbm.5, bf16[2,4,2,2,64,128]{5,4,3,2,1,0:T(8,128)(2,1)} %shard_map.65.refs_0_, bf16[2,4,2,2,64,128]{5,4,3,2,1,0:T(8,128)(2,1)} %copy-done.4, ...), custom_call_target="tpu_custom_call" | custom-call | flops 68719476736 | bytes 6291456 | tf_op jit(solution)/shard_map/pallas_call | solution.py:189
  79.8 0.6 all-to-all-done.3.kv_hbm
  80.4 0.0 copy-start.2
  80.4 6.2 %collective-permute-start.4 = (bf16[4,8,2,64,128]{4,3,2,1,0:T(8,128)(2,1)S(1)}, bf16[4,8,2,64,128]{4,3,2,1,0:T(8,128)(2,1)S(1)}, u32[]{:S(2)}, u32[]{:S(2)}) collective-permute-start(bf16[4,8,2,64,128]{4,3,2,1,0:T(8,128)(2,1)S(1)} %all-to-all-done.3.kv_hbm), channel_id=1, source_target_pairs={{0,8},{8,0},{1,9},{9,1},{2,10},{10,2},{3,11},{11,3},{4,12},{12,4},... | collective-permute-start | bytes 3145736 | tf_op jit(solution)/shard_map/ppermute | solution.py:288
  86.6 0.0 copy-done.2
  86.6 5.2 %shard_map.68.refs_0_ = bf16[64,8192]{1,0:T(8,128)(2,1)} custom-call(s32[1]{0:T(128)} %bitcast.me, s32[64]{0:T(128)} %assignment.5, s32[1]{0:T(128)} %copy.11.anchor, s32[64]{0:T(128)} %lengths.5, bf16[64,8192]{1,0:T(8,128)(2,1)} %q_hbm.5, bf16[4,8,2,64,128]{4,3,2,1,0:T(8,128)(2,1)} %copy-done.2, f32[8,512,128]{2,1,0:T(8,128)} %get-tuple-element.17.o_hbm, ...), custom_call_target="tpu_custom_call" | custom-call | flops 2147483648 | bytes 6291456 | tf_op jit(solution)/shard_map/pallas_call | solution.py:216
  91.8 0.0 collective-permute-done.4.kv_hbm
  91.8 0.0 copy-start
  91.8 1.0 copy-done
  92.8 5.2 %shard_map.69 = bf16[64,8192]{1,0:T(8,128)(2,1)} custom-call(s32[1]{0:T(128)} %bitcast.me, s32[64]{0:T(128)} %assignment.5, s32[1]{0:T(128)} %copy.11.anchor, s32[64]{0:T(128)} %lengths.5, bf16[64,8192]{1,0:T(8,128)(2,1)} %q_hbm.5, bf16[4,8,2,64,128]{4,3,2,1,0:T(8,128)(2,1)} %copy-done, ...), custom_call_target="tpu_custom_call", output_to_operand_aliasing={{}: (8, {})} | custom-call | flops 2147483648 | bytes 6291456 | tf_op jit(solution)/shard_map/pallas_call | solution.py:216
  (3 shorter events, 0.0 us)
Async XLA Ops:
  1.7 23.4 %all-to-all-start = ((bf16[16,64,128]{2,1,0:T(8,128)(2,1)}), bf16[16,64,128]{2,1,0:T(8,128)(2,1)S(1)}, u32[]{:S(2)}, u32[]{:S(2)}) async-start(bf16[16,64,128]{2,1,0:T(8,128)(2,1)} %bitcast.9), calls=%async_computation | async-start | bytes 524288 | tf_op jit(solution)/shard_map/all_to_all | solution.py:292
  11.9 21.1 %collective-permute-start = (bf16[4,2,2,64,128]{4,3,2,1,0:T(8,128)(2,1)}, bf16[4,2,2,64,128]{4,3,2,1,0:T(8,128)(2,1)S(1)}, u32[]{:S(2)}, u32[]{:S(2)}) collective-permute-start(bf16[4,2,2,64,128]{4,3,2,1,0:T(8,128)(2,1)} %shard_map.64.mine_ref), channel_id=1, source_target_pairs={{0,1},{1,0},{2,3},{3,2},{4,5},{5,4},{6,7},{7,6},{8,9},{9,8},{10,11... | collective-permute-start | bytes 786440 | tf_op jit(solution)/shard_map/ppermute | solution.py:288
  25.8 14.7 %all-to-all-start.1 = ((bf16[8,64,128]{2,1,0:T(8,128)(2,1)}), bf16[8,64,128]{2,1,0:T(8,128)(2,1)S(1)}, u32[]{:S(2)}, u32[]{:S(2)}) async-start(bf16[8,64,128]{2,1,0:T(8,128)(2,1)} %broadcast_in_dim.26), calls=%async_computation.1 | async-start | bytes 262144 | tf_op jit(solution)/shard_map/all_to_all | solution.py:292
  33.0 0.7 copy-start.6
  40.5 15.5 %collective-permute-start.2 = (bf16[2,4,2,2,64,128]{5,4,3,2,1,0:T(8,128)(2,1)}, bf16[2,4,2,2,64,128]{5,4,3,2,1,0:T(8,128)(2,1)S(1)}, u32[]{:S(2)}, u32[]{:S(2)}) collective-permute-start(bf16[2,4,2,2,64,128]{5,4,3,2,1,0:T(8,128)(2,1)} %shard_map.65.refs_0_), channel_id=1, source_target_pairs={{0,6},{2,0},{4,2},{6,4},{1,7},{3,1},{5,3},{7,5},{8,14},{10,8},{12,... | collective-permute-start | bytes 1572872 | tf_op jit(solution)/shard_map/ppermute | solution.py:297
  45.6 16.3 %all-to-all-start.2 = ((bf16[8,2,64,128]{3,2,1,0:T(8,128)(2,1)}), bf16[8,2,64,128]{3,2,1,0:T(8,128)(2,1)S(1)}, u32[]{:S(2)}, u32[]{:S(2)}) async-start(bf16[8,2,64,128]{3,2,1,0:T(8,128)(2,1)} %broadcast_in_dim.27), calls=%async_computation.2 | async-start | bytes 524288 | tf_op jit(solution)/shard_map/all_to_all | solution.py:292
  51.8 16.5 %collective-permute-start.1 = (bf16[2,4,2,2,64,128]{5,4,3,2,1,0:T(8,128)(2,1)}, bf16[2,4,2,2,64,128]{5,4,3,2,1,0:T(8,128)(2,1)S(1)}, u32[]{:S(2)}, u32[]{:S(2)}) collective-permute-start(bf16[2,4,2,2,64,128]{5,4,3,2,1,0:T(8,128)(2,1)} %shard_map.65.refs_0_), channel_id=1, source_target_pairs={{0,2},{2,4},{4,6},{6,0},{1,3},{3,5},{5,7},{7,1},{8,10},{10,12},{12... | collective-permute-start | bytes 1572872 | tf_op jit(solution)/shard_map/ppermute | solution.py:297
  56.0 6.6 %copy-start.3 = (bf16[2,4,2,2,64,128]{5,4,3,2,1,0:T(8,128)(2,1)}, bf16[2,4,2,2,64,128]{5,4,3,2,1,0:T(8,128)(2,1)S(1)}, u32[]{:S(2)}) copy-start(bf16[2,4,2,2,64,128]{5,4,3,2,1,0:T(8,128)(2,1)S(1)} %collective-permute-done.2.refs_3_) | copy-start | bytes 1572868
  56.0 15.1 %collective-permute-start.3 = (bf16[2,4,2,2,64,128]{5,4,3,2,1,0:T(8,128)(2,1)S(1)}, bf16[2,4,2,2,64,128]{5,4,3,2,1,0:T(8,128)(2,1)S(1)}, u32[]{:S(2)}, u32[]{:S(2)}) collective-permute-start(bf16[2,4,2,2,64,128]{5,4,3,2,1,0:T(8,128)(2,1)S(1)} %collective-permute-done.2.refs_3_), channel_id=1, source_target_pairs={{0,6},{2,0},{4,2},{6,4},{1,7},{3,1},{5,3},{7,5},{8,14},{10,8},{12,... | collective-permute-start | bytes 1572872 | tf_op jit(solution)/shard_map/ppermute | solution.py:297
  61.9 0.7 copy-start.1
  64.8 15.6 %all-to-all-start.3 = ((bf16[4,8,2,64,128]{4,3,2,1,0:T(8,128)(2,1)}), bf16[4,8,2,64,128]{4,3,2,1,0:T(8,128)(2,1)S(1)}, u32[]{:S(2)}, u32[]{:S(2)}) async-start(bf16[4,8,2,64,128]{4,3,2,1,0:T(8,128)(2,1)} %broadcast_in_dim.28), calls=%async_computation.3 | async-start | bytes 2097152 | tf_op jit(solution)/shard_map/all_to_all | solution.py:292
  68.4 2.8 %copy-start.4 = (bf16[2,4,2,2,64,128]{5,4,3,2,1,0:T(8,128)(2,1)}, bf16[2,4,2,2,64,128]{5,4,3,2,1,0:T(8,128)(2,1)S(1)}, u32[]{:S(2)}) copy-start(bf16[2,4,2,2,64,128]{5,4,3,2,1,0:T(8,128)(2,1)S(1)} %collective-permute-done.1.refs_1_) | copy-start | bytes 1572868
  71.1 0.8 copy-start.5
  80.4 6.2 %copy-start.2 = (bf16[4,8,2,64,128]{4,3,2,1,0:T(8,128)(2,1)}, bf16[4,8,2,64,128]{4,3,2,1,0:T(8,128)(2,1)S(1)}, u32[]{:S(2)}) copy-start(bf16[4,8,2,64,128]{4,3,2,1,0:T(8,128)(2,1)S(1)} %all-to-all-done.3.kv_hbm) | copy-start | bytes 3145732
  80.4 11.4 %collective-permute-start.4 = (bf16[4,8,2,64,128]{4,3,2,1,0:T(8,128)(2,1)S(1)}, bf16[4,8,2,64,128]{4,3,2,1,0:T(8,128)(2,1)S(1)}, u32[]{:S(2)}, u32[]{:S(2)}) collective-permute-start(bf16[4,8,2,64,128]{4,3,2,1,0:T(8,128)(2,1)S(1)} %all-to-all-done.3.kv_hbm), channel_id=1, source_target_pairs={{0,8},{8,0},{1,9},{9,1},{2,10},{10,2},{3,11},{11,3},{4,12},{12,4},... | collective-permute-start | bytes 3145736 | tf_op jit(solution)/shard_map/ppermute | solution.py:288
  91.8 1.0 copy-start

commit v8 on v7

--- a/solution.py
+++ b/solution.py
@@ -16,7 +16,7 @@
 AXES = ("y", "zl", "core", "x", "zh")
 SIZES = (8, 4, 2, 4, 2)
 OWN_CHUNK = 4
-ANCHOR_CHUNK = 2
+ANCHOR_CHUNK = 4
 SCALE = math.log2(math.e) / math.sqrt(HEAD_DIM)
 NEG = -math.inf
 
@@ -268,13 +268,16 @@
     )(keys, values)
 
 
+def hold_kernel(a_ref, out_ref):
+    out_ref[...] = a_ref[...]
+
+
 def hold(a, interpret=False):
     return pl.pallas_call(
-        lambda a_ref, out_ref: None,
+        hold_kernel,
         out_shape=jax.ShapeDtypeStruct(a.shape, a.dtype),
-        in_specs=[ANY],
-        out_specs=ANY,
-        input_output_aliases={0: 0},
+        in_specs=[VMEM],
+        out_specs=VMEM,
         cost_estimate=LONG,
         interpret=interpret,
     )(a)

time: 99 us -> 99.9 us (level)
  Pallas kernels: 21.8 us -> 23.2 us
    pallas_call x1, Pallas kernels: 0.01 us -> 1.67 us  [hold(): pl.pallas_call(hold_kernel, out_shape=jax.ShapeDtypeStruct(a.shape, a.dty...]
    all_to_all x4, waiting for transfers between devices: 6.14 us -> 7.81 us  [exchange(): return lax.all_to_all(a, axes, split_axis=0, concat_axis=0, tiled=True)]
    ppermute x3, waiting for transfers between devices: 5.01 us -> 3.35 us  [shift(): return lax.ppermute(a, axis, [(i, (i + by) % n) for i in range(n)])]
  transfers between devices with their start and end apart: 9 -> 9, of which waited for: 5 -> 5; matrix products, arithmetic and copies ran while one was open for 5% -> 5% of each run, Pallas kernels for 15% -> 17%
where the time goes in v8:
time: 99.9 us; the launch traced here: 99.1 us
  starting transfers between devices  53.6 us (54%)
  Pallas kernels  23.2 us (23%)
  waiting for transfers between devices  11.2 us (11%)
  local copies, waits for them, and re-layouts  6.8 us (7%)
  between operations  2.88 us (3%)
  other arithmetic  1.37 us (1%)
    all_to_all x4, starting transfers between devices, exchange(): return lax.all_to_all(a, axes, split_axis=0, concat_axis=0, tiled=True)  27.2 us
    ppermute x2, starting transfers between devices, swap(): return lax.ppermute(a, axis, [(0, 1), (1, 0)])  14.9 us
    ppermute x3, starting transfers between devices, shift(): return lax.ppermute(a, axis, [(i, (i + by) % n) for i in range(n)])  11.5 us
    pallas_call x2, Pallas kernels, attend_anchor(): pl.pallas_call(functools.partial(anchor_kernel, which), out_shape=jax.Sha...  10.1 us
    pallas_call x1, Pallas kernels, attend_own(): pl.pallas_call(own_kernel, out_shape=(part, part), in_specs=[SMEM, SMEM,...  7.83 us
    all_to_all x4, waiting for transfers between devices, exchange(): return lax.all_to_all(a, axes, split_axis=0, concat_axis=0, tiled=True)  7.81 us
    broadcast_in_dim x4, local copies, waits for them, and re-layouts, to_all(): return exchange(jnp.broadcast_to(a[None], (n,) + a.shape), axes)  3.6 us
    ppermute x3, waiting for transfers between devices, shift(): return lax.ppermute(a, axis, [(i, (i + by) % n) for i in range(n)])  3.35 us
  transfers between devices with their start and end apart: 9, of which 5 were waited for; matrix products, arithmetic and copies ran while one was open for 5% of the time, Pallas kernels for 17%

profile of v8, /device:TPU:1, one launch (start us, length us, event | category | flops | bytes accessed | tf_op | source)
XLA Modules:
  0.0 99.1 jit_solution(5422940125104280359)
XLA Ops:
  0.0 1.7 %shard_map.64.mine_ref = bf16[4,2,2,64,128]{4,3,2,1,0:T(8,128)(2,1)} custom-call(bf16[64,1024]{1,0:T(8,128)(2,1)} %k_ref.1, bf16[64,1024]{1,0:T(8,128)(2,1)} %v_ref.1), custom_call_target="tpu_custom_call" | custom-call | tf_op jit(solution)/shard_map/pallas_call | solution.py:262
  1.7 10.2 %all-to-all-start = ((bf16[16,64,128]{2,1,0:T(8,128)(2,1)}), bf16[16,64,128]{2,1,0:T(8,128)(2,1)S(1)}, u32[]{:S(2)}, u32[]{:S(2)}) async-start(bf16[16,64,128]{2,1,0:T(8,128)(2,1)} %bitcast.9), calls=%async_computation | async-start | bytes 524288 | tf_op jit(solution)/shard_map/all_to_all | solution.py:295
  11.9 9.1 %collective-permute-start = (bf16[4,2,2,64,128]{4,3,2,1,0:T(8,128)(2,1)}, bf16[4,2,2,64,128]{4,3,2,1,0:T(8,128)(2,1)S(1)}, u32[]{:S(2)}, u32[]{:S(2)}) collective-permute-start(bf16[4,2,2,64,128]{4,3,2,1,0:T(8,128)(2,1)} %shard_map.64.mine_ref), channel_id=1, source_target_pairs={{0,1},{1,0},{2,3},{3,2},{4,5},{5,4},{6,7},{7,6},{8,9},{9,8},{10,11... | collective-permute-start | bytes 786440 | tf_op jit(solution)/shard_map/ppermute | solution.py:291
  21.6 1.4 %fusion = s32[]{:T(128)} fusion(s32[64]{0:T(128)} %assignment.5, s32[]{:T(128)} %bitcast.8), kind=kLoop, calls=%fused_computation.3 | loop fusion | flops 191 | bytes 264 | tf_op jit(solution)/shard_map/reduce_sum | solution.py:305
  25.1 0.0 all-to-all-done
  25.1 0.7 broadcast_in_dim.26
  25.8 7.2 %all-to-all-start.1 = ((bf16[8,64,128]{2,1,0:T(8,128)(2,1)}), bf16[8,64,128]{2,1,0:T(8,128)(2,1)S(1)}, u32[]{:S(2)}, u32[]{:S(2)}) async-start(bf16[8,64,128]{2,1,0:T(8,128)(2,1)} %broadcast_in_dim.26), calls=%async_computation.1 | async-start | bytes 262144 | tf_op jit(solution)/shard_map/all_to_all | solution.py:295
  33.0 0.0 collective-permute-done.other_ref
  33.0 0.0 copy-start.6
  33.1 0.7 copy-done.6
  33.8 1.9 %shard_map.65.refs_0_ = bf16[2,4,2,2,64,128]{5,4,3,2,1,0:T(8,128)(2,1)} custom-call(s32[1]{0:T(128)} %bitcast.me, bf16[4,2,2,64,128]{4,3,2,1,0:T(8,128)(2,1)} %shard_map.64.mine_ref, bf16[4,2,2,64,128]{4,3,2,1,0:T(8,128)(2,1)} %copy-done.6), custom_call_target="tpu_custom_call" | custom-call | flops 68719476736 | bytes 6291456 | tf_op jit(solution)/shard_map/pallas_call | solution.py:245
  35.6 4.8 %all-to-all-done.1 = bf16[8,64,128]{2,1,0:T(8,128)(2,1)S(1)} async-done(((bf16[8,64,128]{2,1,0:T(8,128)(2,1)}), bf16[8,64,128]{2,1,0:T(8,128)(2,1)S(1)}, u32[]{:S(2)}, u32[]{:S(2)}) %all-to-all-start.1) | async-done | bytes 131104 | tf_op jit(solution)/shard_map/all_to_all | solution.py:295
  40.5 4.4 %collective-permute-start.2 = (bf16[2,4,2,2,64,128]{5,4,3,2,1,0:T(8,128)(2,1)}, bf16[2,4,2,2,64,128]{5,4,3,2,1,0:T(8,128)(2,1)S(1)}, u32[]{:S(2)}, u32[]{:S(2)}) collective-permute-start(bf16[2,4,2,2,64,128]{5,4,3,2,1,0:T(8,128)(2,1)} %shard_map.65.refs_0_), channel_id=1, source_target_pairs={{0,6},{2,0},{4,2},{6,4},{1,7},{3,1},{5,3},{7,5},{8,14},{10,8},{12,... | collective-permute-start | bytes 1572872 | tf_op jit(solution)/shard_map/ppermute | solution.py:300
  44.8 0.8 broadcast_in_dim.27
  45.6 6.3 %all-to-all-start.2 = ((bf16[8,2,64,128]{3,2,1,0:T(8,128)(2,1)}), bf16[8,2,64,128]{3,2,1,0:T(8,128)(2,1)S(1)}, u32[]{:S(2)}, u32[]{:S(2)}) async-start(bf16[8,2,64,128]{3,2,1,0:T(8,128)(2,1)} %broadcast_in_dim.27), calls=%async_computation.2 | async-start | bytes 524288 | tf_op jit(solution)/shard_map/all_to_all | solution.py:295
  51.8 1.9 %collective-permute-start.1 = (bf16[2,4,2,2,64,128]{5,4,3,2,1,0:T(8,128)(2,1)}, bf16[2,4,2,2,64,128]{5,4,3,2,1,0:T(8,128)(2,1)S(1)}, u32[]{:S(2)}, u32[]{:S(2)}) collective-permute-start(bf16[2,4,2,2,64,128]{5,4,3,2,1,0:T(8,128)(2,1)} %shard_map.65.refs_0_), channel_id=1, source_target_pairs={{0,2},{2,4},{4,6},{6,0},{1,3},{3,5},{5,7},{7,1},{8,10},{10,12},{12... | collective-permute-start | bytes 1572872 | tf_op jit(solution)/shard_map/ppermute | solution.py:300
  53.8 2.2 %collective-permute-done.2.refs_3_ = bf16[2,4,2,2,64,128]{5,4,3,2,1,0:T(8,128)(2,1)S(1)} collective-permute-done((bf16[2,4,2,2,64,128]{5,4,3,2,1,0:T(8,128)(2,1)}, bf16[2,4,2,2,64,128]{5,4,3,2,1,0:T(8,128)(2,1)S(1)}, u32[]{:S(2)}, u32[]{:S(2)}) %collective-permute-start.2) | collective-permute-done | bytes 524320 | tf_op jit(solution)/shard_map/ppermute | solution.py:300
  56.0 0.0 copy-start.3
  56.0 5.2 %collective-permute-start.3 = (bf16[2,4,2,2,64,128]{5,4,3,2,1,0:T(8,128)(2,1)S(1)}, bf16[2,4,2,2,64,128]{5,4,3,2,1,0:T(8,128)(2,1)S(1)}, u32[]{:S(2)}, u32[]{:S(2)}) collective-permute-start(bf16[2,4,2,2,64,128]{5,4,3,2,1,0:T(8,128)(2,1)S(1)} %collective-permute-done.2.refs_3_), channel_id=1, source_target_pairs={{0,6},{2,0},{4,2},{6,4},{1,7},{3,1},{5,3},{7,5},{8,14},{10,8},{12,... | collective-permute-start | bytes 1572872 | tf_op jit(solution)/shard_map/ppermute | solution.py:300
  61.2 0.7 all-to-all-done.2.a_ref
  61.9 0.0 copy-start.2
  61.9 0.7 copy-done.2
  62.6 1.7 %shard_map.66 = bf16[8,2,64,128]{3,2,1,0:T(8,128)(2,1)} custom-call(bf16[8,2,64,128]{3,2,1,0:T(8,128)(2,1)} %copy-done.2), custom_call_target="tpu_custom_call" | custom-call | flops 68719476736 | bytes 6291456 | tf_op jit(solution)/shard_map/pallas_call | solution.py:276
  64.3 0.0 copy-done.3
  64.3 2.2 %broadcast_in_dim.28 = bf16[4,8,2,64,128]{4,3,2,1,0:T(8,128)(2,1)} broadcast(bf16[8,2,64,128]{3,2,1,0:T(8,128)(2,1)} %shard_map.66), dimensions={1,2,3,4} | broadcast | bytes 1310720 | tf_op jit(solution)/shard_map/broadcast_in_dim | solution.py:287
  66.5 3.5 %all-to-all-start.3 = ((bf16[4,8,2,64,128]{4,3,2,1,0:T(8,128)(2,1)}), bf16[4,8,2,64,128]{4,3,2,1,0:T(8,128)(2,1)S(1)}, u32[]{:S(2)}, u32[]{:S(2)}) async-start(bf16[4,8,2,64,128]{4,3,2,1,0:T(8,128)(2,1)} %broadcast_in_dim.28), calls=%async_computation.3 | async-start | bytes 2097152 | tf_op jit(solution)/shard_map/all_to_all | solution.py:295
  70.0 0.0 collective-permute-done.1.refs_1_
  70.0 0.0 copy-start.4
  70.0 1.1 %collective-permute-done.3.refs_2_ = bf16[2,4,2,2,64,128]{5,4,3,2,1,0:T(8,128)(2,1)S(1)} collective-permute-done((bf16[2,4,2,2,64,128]{5,4,3,2,1,0:T(8,128)(2,1)S(1)}, bf16[2,4,2,2,64,128]{5,4,3,2,1,0:T(8,128)(2,1)S(1)}, u32[]{:S(2)}, u32[]{:S(2)}) %collective-permute-start.3) | collective-permute-done | bytes 524320 | tf_op jit(solution)/shard_map/ppermute | solution.py:300
  71.1 0.0 copy-done.4
  71.1 0.0 copy-start.5
  71.1 0.8 copy-done.5
  71.9 7.8 %shard_map.67 = (f32[8,512,128]{2,1,0:T(8,128)}, f32[8,512,128]{2,1,0:T(8,128)}) custom-call(s32[1]{0:T(128)} %bitcast.me, s32[64]{0:T(128)} %assignment.5, s32[64]{0:T(128)} %lengths.5, bf16[64,8192]{1,0:T(8,128)(2,1)} %q_hbm.5, bf16[2,4,2,2,64,128]{5,4,3,2,1,0:T(8,128)(2,1)} %shard_map.65.refs_0_, bf16[2,4,2,2,64,128]{5,4,3,2,1,0:T(8,128)(2,1)} %copy-done.4, ...), custom_call_target="tpu_custom_call" | custom-call | flops 68719476736 | bytes 6291456 | tf_op jit(solution)/shard_map/pallas_call | solution.py:189
  79.8 2.3 %all-to-all-done.3.kv_hbm = bf16[4,8,2,64,128]{4,3,2,1,0:T(8,128)(2,1)S(1)} async-done(((bf16[4,8,2,64,128]{4,3,2,1,0:T(8,128)(2,1)}), bf16[4,8,2,64,128]{4,3,2,1,0:T(8,128)(2,1)S(1)}, u32[]{:S(2)}, u32[]{:S(2)}) %all-to-all-start.3) | async-done | bytes 1048608 | tf_op jit(solution)/shard_map/all_to_all | solution.py:295
  82.1 0.0 copy-start.1
  82.1 5.9 %collective-permute-start.4 = (bf16[4,8,2,64,128]{4,3,2,1,0:T(8,128)(2,1)S(1)}, bf16[4,8,2,64,128]{4,3,2,1,0:T(8,128)(2,1)S(1)}, u32[]{:S(2)}, u32[]{:S(2)}) collective-permute-start(bf16[4,8,2,64,128]{4,3,2,1,0:T(8,128)(2,1)S(1)} %all-to-all-done.3.kv_hbm), channel_id=1, source_target_pairs={{0,8},{8,0},{1,9},{9,1},{2,10},{10,2},{3,11},{11,3},{4,12},{12,4},... | collective-permute-start | bytes 3145736 | tf_op jit(solution)/shard_map/ppermute | solution.py:291
  87.9 0.0 copy-done.1
  87.9 5.1 %shard_map.68.refs_0_ = bf16[64,8192]{1,0:T(8,128)(2,1)} custom-call(s32[1]{0:T(128)} %bitcast.me, s32[64]{0:T(128)} %assignment.5, s32[1]{0:T(128)} %copy.9.anchor, s32[64]{0:T(128)} %lengths.5, bf16[64,8192]{1,0:T(8,128)(2,1)} %q_hbm.5, bf16[4,8,2,64,128]{4,3,2,1,0:T(8,128)(2,1)} %copy-done.1, f32[8,512,128]{2,1,0:T(8,128)} %get-tuple-element.17.o_hbm, ...), custom_call_target="tpu_custom_call" | custom-call | flops 2147483648 | bytes 6291456 | tf_op jit(solution)/shard_map/pallas_call | solution.py:216
  93.0 0.0 collective-permute-done.4.kv_hbm
  93.0 0.0 copy-start
  93.0 1.0 copy-done
  94.0 5.1 %shard_map.69 = bf16[64,8192]{1,0:T(8,128)(2,1)} custom-call(s32[1]{0:T(128)} %bitcast.me, s32[64]{0:T(128)} %assignment.5, s32[1]{0:T(128)} %copy.9.anchor, s32[64]{0:T(128)} %lengths.5, bf16[64,8192]{1,0:T(8,128)(2,1)} %q_hbm.5, bf16[4,8,2,64,128]{4,3,2,1,0:T(8,128)(2,1)} %copy-done, ...), custom_call_target="tpu_custom_call", output_to_operand_aliasing={{}: (8, {})} | custom-call | flops 2147483648 | bytes 6291456 | tf_op jit(solution)/shard_map/pallas_call | solution.py:216
  (2 shorter events, 0.0 us)
Async XLA Ops:
  1.7 23.4 %all-to-all-start = ((bf16[16,64,128]{2,1,0:T(8,128)(2,1)}), bf16[16,64,128]{2,1,0:T(8,128)(2,1)S(1)}, u32[]{:S(2)}, u32[]{:S(2)}) async-start(bf16[16,64,128]{2,1,0:T(8,128)(2,1)} %bitcast.9), calls=%async_computation | async-start | bytes 524288 | tf_op jit(solution)/shard_map/all_to_all | solution.py:295
  11.9 21.1 %collective-permute-start = (bf16[4,2,2,64,128]{4,3,2,1,0:T(8,128)(2,1)}, bf16[4,2,2,64,128]{4,3,2,1,0:T(8,128)(2,1)S(1)}, u32[]{:S(2)}, u32[]{:S(2)}) collective-permute-start(bf16[4,2,2,64,128]{4,3,2,1,0:T(8,128)(2,1)} %shard_map.64.mine_ref), channel_id=1, source_target_pairs={{0,1},{1,0},{2,3},{3,2},{4,5},{5,4},{6,7},{7,6},{8,9},{9,8},{10,11... | collective-permute-start | bytes 786440 | tf_op jit(solution)/shard_map/ppermute | solution.py:291
  25.8 14.7 %all-to-all-start.1 = ((bf16[8,64,128]{2,1,0:T(8,128)(2,1)}), bf16[8,64,128]{2,1,0:T(8,128)(2,1)S(1)}, u32[]{:S(2)}, u32[]{:S(2)}) async-start(bf16[8,64,128]{2,1,0:T(8,128)(2,1)} %broadcast_in_dim.26), calls=%async_computation.1 | async-start | bytes 262144 | tf_op jit(solution)/shard_map/all_to_all | solution.py:295
  33.0 0.7 copy-start.6
  40.5 15.5 %collective-permute-start.2 = (bf16[2,4,2,2,64,128]{5,4,3,2,1,0:T(8,128)(2,1)}, bf16[2,4,2,2,64,128]{5,4,3,2,1,0:T(8,128)(2,1)S(1)}, u32[]{:S(2)}, u32[]{:S(2)}) collective-permute-start(bf16[2,4,2,2,64,128]{5,4,3,2,1,0:T(8,128)(2,1)} %shard_map.65.refs_0_), channel_id=1, source_target_pairs={{0,6},{2,0},{4,2},{6,4},{1,7},{3,1},{5,3},{7,5},{8,14},{10,8},{12,... | collective-permute-start | bytes 1572872 | tf_op jit(solution)/shard_map/ppermute | solution.py:300
  45.6 16.3 %all-to-all-start.2 = ((bf16[8,2,64,128]{3,2,1,0:T(8,128)(2,1)}), bf16[8,2,64,128]{3,2,1,0:T(8,128)(2,1)S(1)}, u32[]{:S(2)}, u32[]{:S(2)}) async-start(bf16[8,2,64,128]{3,2,1,0:T(8,128)(2,1)} %broadcast_in_dim.27), calls=%async_computation.2 | async-start | bytes 524288 | tf_op jit(solution)/shard_map/all_to_all | solution.py:295
  51.8 18.2 %collective-permute-start.1 = (bf16[2,4,2,2,64,128]{5,4,3,2,1,0:T(8,128)(2,1)}, bf16[2,4,2,2,64,128]{5,4,3,2,1,0:T(8,128)(2,1)S(1)}, u32[]{:S(2)}, u32[]{:S(2)}) collective-permute-start(bf16[2,4,2,2,64,128]{5,4,3,2,1,0:T(8,128)(2,1)} %shard_map.65.refs_0_), channel_id=1, source_target_pairs={{0,2},{2,4},{4,6},{6,0},{1,3},{3,5},{5,7},{7,1},{8,10},{10,12},{12... | collective-permute-start | bytes 1572872 | tf_op jit(solution)/shard_map/ppermute | solution.py:300
  56.0 8.3 %copy-start.3 = (bf16[2,4,2,2,64,128]{5,4,3,2,1,0:T(8,128)(2,1)}, bf16[2,4,2,2,64,128]{5,4,3,2,1,0:T(8,128)(2,1)S(1)}, u32[]{:S(2)}) copy-start(bf16[2,4,2,2,64,128]{5,4,3,2,1,0:T(8,128)(2,1)S(1)} %collective-permute-done.2.refs_3_) | copy-start | bytes 1572868
  56.0 15.1 %collective-permute-start.3 = (bf16[2,4,2,2,64,128]{5,4,3,2,1,0:T(8,128)(2,1)S(1)}, bf16[2,4,2,2,64,128]{5,4,3,2,1,0:T(8,128)(2,1)S(1)}, u32[]{:S(2)}, u32[]{:S(2)}) collective-permute-start(bf16[2,4,2,2,64,128]{5,4,3,2,1,0:T(8,128)(2,1)S(1)} %collective-permute-done.2.refs_3_), channel_id=1, source_target_pairs={{0,6},{2,0},{4,2},{6,4},{1,7},{3,1},{5,3},{7,5},{8,14},{10,8},{12,... | collective-permute-start | bytes 1572872 | tf_op jit(solution)/shard_map/ppermute | solution.py:300
  61.9 0.7 copy-start.2
  66.5 15.6 %all-to-all-start.3 = ((bf16[4,8,2,64,128]{4,3,2,1,0:T(8,128)(2,1)}), bf16[4,8,2,64,128]{4,3,2,1,0:T(8,128)(2,1)S(1)}, u32[]{:S(2)}, u32[]{:S(2)}) async-start(bf16[4,8,2,64,128]{4,3,2,1,0:T(8,128)(2,1)} %broadcast_in_dim.28), calls=%async_computation.3 | async-start | bytes 2097152 | tf_op jit(solution)/shard_map/all_to_all | solution.py:295
  70.0 1.1 %copy-start.4 = (bf16[2,4,2,2,64,128]{5,4,3,2,1,0:T(8,128)(2,1)}, bf16[2,4,2,2,64,128]{5,4,3,2,1,0:T(8,128)(2,1)S(1)}, u32[]{:S(2)}) copy-start(bf16[2,4,2,2,64,128]{5,4,3,2,1,0:T(8,128)(2,1)S(1)} %collective-permute-done.1.refs_1_) | copy-start | bytes 1572868
  71.1 0.8 copy-start.5
  82.1 5.9 %copy-start.1 = (bf16[4,8,2,64,128]{4,3,2,1,0:T(8,128)(2,1)}, bf16[4,8,2,64,128]{4,3,2,1,0:T(8,128)(2,1)S(1)}, u32[]{:S(2)}) copy-start(bf16[4,8,2,64,128]{4,3,2,1,0:T(8,128)(2,1)S(1)} %all-to-all-done.3.kv_hbm) | copy-start | bytes 3145732
  82.1 11.0 %collective-permute-start.4 = (bf16[4,8,2,64,128]{4,3,2,1,0:T(8,128)(2,1)S(1)}, bf16[4,8,2,64,128]{4,3,2,1,0:T(8,128)(2,1)S(1)}, u32[]{:S(2)}, u32[]{:S(2)}) collective-permute-start(bf16[4,8,2,64,128]{4,3,2,1,0:T(8,128)(2,1)S(1)} %all-to-all-done.3.kv_hbm), channel_id=1, source_target_pairs={{0,8},{8,0},{1,9},{9,1},{2,10},{10,2},{3,11},{11,3},{4,12},{12,4},... | collective-permute-start | bytes 3145736 | tf_op jit(solution)/shard_map/ppermute | solution.py:291
  93.0 1.0 copy-start
